TPU v7x, 32 devices: a whole 2x2x4 slice. The times are simulated.
32 devices in a mesh: grp: 4 (over y, x), rows: 8 (over z, core).
Axes of the slice: x: 2, y: 2, z: 4, core: 2. Of those that a mesh axis runs over, the one named last changes fastest.
Arguments:
- single_rep: bfloat16 [4, 128, 512], P('grp', 'rows'), may hold values from -6 to 6
- pair_rep: bfloat16 [4, 128, 128, 128], P('grp', 'rows'), may hold values from -6 to 6
- residue_mask: int32 [4, 128], P('grp'), may hold values 0 or 1
- single_gains: bfloat16 [3, 512], replicated, may hold values from 0.25 to 1.75
- pair_gains: bfloat16 [6, 128], replicated, may hold values from 0.25 to 1.75
- mult_gains: bfloat16 [2, 128], replicated, may hold values from 0.25 to 1.75
- single_proj: bfloat16 [5, 512, 512], replicated, may hold values from -0.25 to 0.25
- single_bias: bfloat16 [128, 8], replicated, may hold values from -0.5 to 0.5
- single_up: bfloat16 [512, 2048], replicated, may hold values from -0.25 to 0.25
- single_down: bfloat16 [2048, 512], replicated, may hold values from -0.125 to 0.125
- opm_proj: bfloat16 [2, 512, 32], replicated, may hold values from -0.25 to 0.25
- opm_out: bfloat16 [32, 32, 128], replicated, may hold values from -0.1875 to 0.1875
- mult_proj: bfloat16 [2, 4, 128, 128], replicated, may hold values from -0.5 to 0.5
- mult_gate: bfloat16 [2, 128, 128], replicated, may hold values from -0.5 to 0.5
- mult_out: bfloat16 [2, 128, 128], replicated, may hold values from -0.5 to 0.5
- att_proj: bfloat16 [2, 4, 128, 128], replicated, may hold values from -0.5 to 0.5
- att_bias: bfloat16 [2, 128, 4], replicated, may hold values from -0.5 to 0.5
- att_out: bfloat16 [2, 128, 128], replicated, may hold values from -1 to 1
- pair_up: bfloat16 [128, 512], replicated, may hold values from -0.5 to 0.5
- pair_down: bfloat16 [512, 128], replicated, may hold values from -0.25 to 0.25
- single_cot: bfloat16 [4, 128, 512], P('grp', 'rows'), may hold values from -6 to 6
- pair_cot: bfloat16 [4, 128, 128, 128], P('grp', 'rows'), may hold values from -6 to 6
Outputs:
- single_out: bfloat16 [4, 128, 512], P('grp', 'rows')
- pair_out: bfloat16 [4, 128, 128, 128], P('grp', 'rows')
- single_grad: float32 [4, 128, 512], P('grp', 'rows')
- pair_grad: float32 [4, 128, 128, 128], P('grp', 'rows')
- single_gains_grad: float32 [3, 512], replicated
- pair_gains_grad: float32 [6, 128], replicated
- mult_gains_grad: float32 [2, 128], replicated
- single_proj_grad: float32 [5, 512, 512], replicated
- single_bias_grad: float32 [128, 8], replicated
- single_up_grad: float32 [512, 2048], replicated
- single_down_grad: float32 [2048, 512], replicated
- opm_proj_grad: float32 [2, 512, 32], replicated
- opm_out_grad: float32 [32, 32, 128], replicated
- mult_proj_grad: float32 [2, 4, 128, 128], replicated
- mult_gate_grad: float32 [2, 128, 128], replicated
- mult_out_grad: float32 [2, 128, 128], replicated
- att_proj_grad: float32 [2, 4, 128, 128], replicated
- att_bias_grad: float32 [2, 128, 4], replicated
- att_out_grad: float32 [2, 128, 128], replicated
- pair_up_grad: float32 [128, 512], replicated
- pair_down_grad: float32 [512, 128], replicated
Inputs may be any that keep to these rules, and one draw needn't show every extreme that they name: `residue_mask`: 1 marks a residue that is present, 0 one that is missing.
All inputs are finite; a program needn't handle non-finite values. No bound on the sum of `residue_mask` on one device may be relied on, other than what follows from the above.
Results may differ from a plain program's by a relative error of at most 0.017.
Values may be sent and summed in bfloat16 or wider, within the bound.
No kernel may reach another device: no remote copies, remote signals or barrier semaphores. Data moves between devices by JAX's collectives and lax.ppermute only.
A program may use at most 128 MiB of HBM per device.

v0:
```python
import math

import jax
import jax.numpy as jnp
from jax import lax
from jax.experimental import pallas as pl
from jax.experimental.pallas import tpu as pltpu
from jax.sharding import PartitionSpec as P

BF = jnp.bfloat16
F32 = jnp.float32
EPSILON = 1e-05
MASKED = 1000000000.0
AX = ("grp", "rows")
L = 128
C = 128
TH = 4
HD = 32
HPAD = 16


def dot(a, b):
    return lax.dot_general(a, b, (((1,), (0,)), ((), ())), preferred_element_type=F32)


def dot_nt(a, b):
    return lax.dot_general(a, b, (((1,), (1,)), ((), ())), preferred_element_type=F32)


def dot_tn(a, b):
    return lax.dot_general(a, b, (((0,), (0,)), ((), ())), preferred_element_type=F32)


def b16(x):
    return x.astype(BF)


def f32(x):
    return x.astype(F32)


def sig(x):
    return 0.5 * jnp.tanh(0.5 * x) + 0.5


GELU_A = 0.7978845608028654
GELU_B = 0.044715


def gelu_parts(x):
    t = jnp.tanh(GELU_A * (x + GELU_B * x * x * x))
    half = 0.5 * (1.0 + t)
    slope = half + 0.5 * x * (1.0 - t * t) * (GELU_A * (1.0 + 3.0 * GELU_B * x * x))
    return x * half, slope


def norm_cols(z):
    c = z - jnp.mean(z, 0, keepdims=True)
    scale = lax.rsqrt(jnp.mean(c * c, 0, keepdims=True) + EPSILON)
    return c * scale, scale


def norm_cols_back(dx, xh, scale):
    return scale * (
        dx - jnp.mean(dx, 0, keepdims=True) - xh * jnp.mean(dx * xh, 0, keepdims=True)
    )


def cols(r):
    return pl.ds(pl.multiple_of(r * L, L), L)


def each_row(count, body):
    def step(r, carry):
        body(r)
        return carry

    lax.fori_loop(0, count, step, 0, unroll=4 if count > 4 else 2)


def call(kernel, outs, scratch, args, deps=(), raw=(), late=(), far=(), us=5):
    count, more, given = len(args), len(deps), len(outs)
    fetched = [args[k] for k in raw]

    def body(*refs):
        mine = list(refs[:count])
        results = list(refs[count + more : count + more + given])
        rest = list(refs[count + more + given :])
        sems = rest.pop() if raw or far else None
        stores = [rest.pop() for _ in far][::-1]
        held = [rest.pop() for _ in raw][::-1]
        moves = {}
        for i, k in enumerate(raw):
            moves[k] = pltpu.make_async_copy(mine[k], held[i], sems.at[i])
            moves[k].start()
        for k in raw:
            if k not in late:
                moves[k].wait()
        for i, k in enumerate(raw):
            mine[k] = held[i]
        ends = []
        for i, k in enumerate(far):
            ends.append(pltpu.make_async_copy(stores[i], results[k], sems.at[len(raw) + i]))
            results[k] = stores[i]
        if late:
            kernel(lambda k: moves[k].wait(), *mine, *results, *rest)
        else:
            kernel(*mine, *results, *rest)
        for end in ends:
            end.start()
        for end in ends:
            end.wait()

    vm = pl.BlockSpec(memory_space=pltpu.VMEM)
    sm = pl.BlockSpec(memory_space=pltpu.SMEM)
    away = pl.BlockSpec(memory_space=pl.ANY)
    moved = sum(a.size * a.dtype.itemsize for a in args)
    buffers = [pltpu.VMEM(s, d) for s, d in scratch]
    buffers += [pltpu.VMEM(a.shape, a.dtype) for a in fetched]
    buffers += [pltpu.VMEM(*outs[k]) for k in far]
    placed = sum(math.prod(b.shape) * jnp.dtype(b.dtype).itemsize for b in buffers)
    if raw or far:
        buffers.append(pltpu.SemaphoreType.DMA((len(raw) + len(far),)))
    return pl.pallas_call(
        body,
        out_shape=[
            pltpu.HBM(s, d) if k in far else jax.ShapeDtypeStruct(s, d)
            for k, (s, d) in enumerate(outs)
        ],
        in_specs=[
            away if k in raw else sm if a.dtype == jnp.int32 else vm for k, a in enumerate(args)
        ]
        + [away] * more,
        out_specs=[away if k in far else vm for k in range(given)],
        scratch_shapes=buffers,
        compiler_params=pltpu.CompilerParams(vmem_limit_bytes=(12 << 20) + placed),
        cost_estimate=pl.CostEstimate(flops=us * 10**9, bytes_accessed=moved, transcendentals=0),
    )(
        *[
            pltpu.with_memory_space_constraint(a, pltpu.HBM) if k in raw else a
            for k, a in enumerate(args)
        ],
        *deps,
    )


def prep_weights(gp, gm, mp, mg, mo, ap, ab, ao, pu, pd, sb):
    def kernel(
        gp, gm, mp, mg, mo, ap, ab, ao, pu, pd, sb,
        m5t, m5, mot, mof, a4t, a4, aot, abt, upt, up, dnt, sbt,
    ):
        gpv = f32(gp[...])
        gmv = f32(gm[...])

        def turned(w):
            shape = (HPAD, w.shape[1])
            row = lax.broadcasted_iota(jnp.int32, shape, 0)
            lane = lax.broadcasted_iota(jnp.int32, shape, 1)
            return dot_nt(b16(jnp.where(row == lane, 1.0, 0.0)), w)

        for t in range(2):
            g = gpv[1 + t : 2 + t]
            for k in range(5):
                w = f32(mp[t, k] if k < 4 else mg[t]).T * g
                m5t[t, k * C : (k + 1) * C] = b16(w)
                m5[t, :, k * C : (k + 1) * C] = b16(w.T)
            w = f32(mo[t]).T * gmv[t : t + 1]
            mot[t] = b16(w)
            mof[t] = b16(w.T)
            g = gpv[3 + t : 4 + t]
            for k in range(4):
                w = f32(ap[t, k]).T * (g * HD**-0.5 if k == 0 else g)
                a4t[t, k * C : (k + 1) * C] = b16(w)
                a4[t, :, k * C : (k + 1) * C] = b16(w.T)
            aot[t] = b16(f32(ao[t]).T)
            abt[t] = b16(turned(ab[t]) * g)
        g = gpv[5:6]
        for k in range(4):
            s = slice(k * C, (k + 1) * C)
            w = f32(pu[:, s]).T * g
            upt[s] = b16(w)
            up[:, s] = b16(w.T)
            dnt[:, s] = b16(f32(pd[s]).T)
        sbt[...] = b16(turned(sb[...]) * gpv[0:1])

    outs = [
        ((2, 640, C), BF), ((2, C, 640), BF), ((2, C, C), BF), ((2, C, C), BF),
        ((2, 512, C), BF), ((2, C, 512), BF), ((2, C, C), BF), ((2, HPAD, C), BF),
        ((512, C), BF), ((C, 512), BF), ((C, 512), BF), ((HPAD, C), BF),
    ]
    return call(kernel, outs, [], (gp, gm, mp, mg, mo, ap, ab, ao, pu, pd, sb), raw=(0, 1, 2, 3, 4, 5, 6, 7, 8, 9, 10), far=(0, 1, 2, 3, 4, 5, 6, 7, 8, 9, 10, 11), us=3)


def pack(rows, single, cot, pair, mask, sbt, where):
    def kernel(single, cot, pair, mask, sbt, where, mine, mask_col, s, sm):
        sm[...] = jnp.broadcast_to(mask[...], (L, L)).T
        mask_col[...] = sm[pl.ds(pl.multiple_of(where[3] * rows, rows), rows), :]
        key_row = (mask[...] - 1.0) * MASKED

        def body(r):
            xh, _ = norm_cols(f32(pair[r]).T)
            rb = dot(sbt[...], b16(xh)) + key_row
            s[pl.ds(r, HPAD, stride=rows), :] = rb

        each_row(rows, body)
        mine[0:rows] = single[...]
        mine[rows : 2 * rows] = cot[...]
        for h in range(8):
            mine[rows * (2 + h // 4) : rows * (3 + h // 4), (h % 4) * L : (h % 4 + 1) * L] = b16(
                s[h * rows : (h + 1) * rows]
            )

    width = single.shape[1]
    return call(
        kernel,
        [((4 * rows, width), BF), ((rows, L), F32)],
        [((HPAD * rows, L), F32), ((L, L), F32)],
        (single, cot, pair, mask, sbt, where), raw=(0, 1, 2, 4), us=2)


def copies_of(x, count, deps):
    def kernel(x, out):
        for d in range(count):
            out[d] = x[...]

    return call(kernel, [((count,) + x.shape, x.dtype)], [], (x,), deps=deps)[0]


def norm_rows16(x):
    c = x - jnp.mean(x, -1, keepdims=True)
    scale = lax.rsqrt(jnp.mean(c * c, -1, keepdims=True) + EPSILON)
    return c * scale, scale


def norm_rows16_back(dx, xh, scale):
    return scale * (
        dx - jnp.mean(dx, -1, keepdims=True) - xh * jnp.mean(dx * xh, -1, keepdims=True)
    )


def halves():
    lane = lax.broadcasted_iota(jnp.int32, (1, L), 1)
    low = jnp.where(lane < L // 2, 1.0, 0.0)
    return b16(low), b16(1.0 - low)


def pair_weights(q, k, bias0, bias1):
    out = []
    for m, bias in zip(halves(), (bias0, bias1)):
        s = dot_nt(q * m, k) + bias
        e = jnp.exp(s - jnp.max(s, -1, keepdims=True))
        out.append(b16(e / jnp.sum(e, -1, keepdims=True)))
    return out


def on_halves(x, axis=0):
    return jnp.concatenate([x * m for m in halves()], axis)


def single_own(n, rows, copies, gathered, mine, mask_col, gains, proj, up, down, outer):
    width = up.shape[0]
    opm2 = 64

    def kernel(arrive, gathered, mine, mask_col, gains, proj, up, down, outer, out, lr):
        g = f32(gains[...])
        sn = b16(norm_rows16(f32(gathered[...].reshape(n * rows, width)))[0] * g[0:1])
        arrive(4)
        keys, vals = b16(dot(sn, proj[1])), b16(dot(sn, proj[2]))
        x = f32(mine[0:rows])
        sn = b16(norm_rows16(x)[0] * g[0:1])
        query = b16(dot(sn, proj[0]) * 0.125)
        gate = sig(dot(sn, proj[3]))
        mixed = []
        for t in range(4):
            s = slice(t * L, (t + 1) * L)
            bias = [
                f32(mine[rows * (2 + h // 4) : rows * (3 + h // 4), (h % 4) * L : (h % 4 + 1) * L])
                for h in (2 * t, 2 * t + 1)
            ]
            p = pair_weights(query[:, s], keys[:, s], *bias)
            mixed.append(dot(jnp.concatenate(p, 1), on_halves(vals[:, s])))
        mixed = jnp.concatenate(mixed, 1)
        first = x + dot(b16(mixed * gate), proj[4])
        x1 = b16(norm_rows16(first)[0] * g[1:2])
        arrive(5)
        hidden = b16(gelu_parts(dot(x1, up[...]))[0])
        arrive(6)
        second = first + dot(hidden, down[...])
        out[...] = b16(second)
        x2 = b16(norm_rows16(second)[0] * g[2:3])
        both = dot(x2, outer[...]) * mask_col[...]
        lane = lax.broadcasted_iota(jnp.int32, (rows, L), 1)
        both = b16(jnp.where(lane >= opm2, mask_col[...], both))
        for d in range(copies):
            lr[d] = both

    return call(
        kernel,
        [((rows, width), BF), ((copies, rows, L), BF)],
        [],
        (gathered, mine, mask_col, gains, proj, up, down, outer), raw=(3, 4, 5, 6, 7), late=(4, 5, 6), us=6)


def single_every(n, rows, where, ga, gb, gains, proj, up, down, deps=()):
    width, wide = up.shape
    tokens = 4 * L
    half = ga.shape[0]

    def kernel(
        arrive, where, ga, gb, gains, proj, up, down,
        x_all, cot_all, xs, qkv, gm, probs, slope, first_out, second_out, held,
    ):
        core = where[3] % 2
        for k in range(half):
            held[2 * k + core] = ga[k]
            held[2 * k + 1 - core] = gb[k]
        g = f32(gains[...])

        def body(crop):
            rs = pl.ds(pl.multiple_of(crop * L, L), L)
            ds = pl.ds(crop * n, n)
            x16 = held[ds, 0:rows, :].reshape(L, width)
            x_all[rs, :] = x16
            cot_all[rs, :] = held[ds, rows : 2 * rows, :].reshape(L, width)
            x = f32(x16)
            sn = b16(norm_rows16(x)[0] * g[0:1])
            xs[rs, 0:width] = sn

            @pl.when(crop == 0)
            def _():
                arrive(4)

            query = b16(dot(sn, proj[0]) * 0.125)
            keys, vals = b16(dot(sn, proj[1])), b16(dot(sn, proj[2]))
            qkv[rs, 0:width] = query
            qkv[rs, width : 2 * width] = keys
            qkv[rs, 2 * width : 3 * width] = vals
            gate = sig(dot(sn, proj[3]))
            mixed = []
            for t in range(4):
                s = slice(t * L, (t + 1) * L)
                bias = [
                    f32(
                        held[
                            ds,
                            rows * (2 + h // 4) : rows * (3 + h // 4),
                            (h % 4) * L : (h % 4 + 1) * L,
                        ].reshape(L, L)
                    )
                    for h in (2 * t, 2 * t + 1)
                ]
                p = pair_weights(query[:, s], keys[:, s], *bias)
                for k in range(2):
                    at = pl.multiple_of((crop * 8 + 2 * t + k) * L, L)
                    probs[pl.ds(at, L), :] = p[k]
                mixed.append(dot(jnp.concatenate(p, 1), on_halves(vals[:, s])))
            mixed = jnp.concatenate(mixed, 1)
            gm[rs, 0:width] = b16(gate)
            gm[rs, width : 2 * width] = b16(mixed)
            u = b16(mixed * gate)
            xs[rs, width : 2 * width] = u
            first = x + dot(u, proj[4])
            first_out[rs, :] = first
            x1 = b16(norm_rows16(first)[0] * g[1:2])
            xs[rs, 2 * width : 3 * width] = x1

            @pl.when(crop == 0)
            def _():
                arrive(5)
                arrive(6)

            hid, slp = gelu_parts(dot(x1, up[...]))
            h16 = b16(hid)
            xs[rs, 3 * width : 3 * width + wide] = h16
            slope[rs, :] = b16(slp)
            second_out[rs, :] = first + dot(h16, down[...])

        each_row(4, body)

    return call(
        kernel,
        [
            ((tokens, width), BF), ((tokens, width), BF), ((tokens, 3 * width + wide), BF),
            ((tokens, 3 * width), BF), ((tokens, 2 * width), BF), ((4 * 8 * L, L), BF),
            ((tokens, wide), BF), ((tokens, width), F32), ((tokens, width), F32),
        ],
        [((2 * half, 4 * rows, width), BF)],
        (where, ga, gb, gains, proj, up, down),
        deps=deps, raw=(1, 2, 3, 4, 5, 6), late=(4, 5, 6), far=(0, 1, 2, 3, 4, 5, 6, 7, 8), us=19)


def single_back(members, rows, where, ea, eb, kept, gains, proj, up, down, outer, deps=()):
    width, wide = up.shape
    tokens = 4 * L
    x_all, cot_all, _, qkv, gm, probs, slope, first_in, second_in = kept

    def kernel(
        arrive, where, ea, eb, x_all, cot_all, qkv, gm, probs, slope, first_in, second_in,
        gains, proj, up, down, outer,
        ys, gain_grad, d_own, drb, m_op,
        dlr, o_x2, sdrb, sds,
    ):
        g = f32(gains[...])
        gain_grad[...] = jnp.zeros_like(gain_grad)
        for crop in range(4):
            total = f32(ea[members[crop][0]]) + f32(eb[members[crop][0]])
            for k in members[crop][1:]:
                total = total + (f32(ea[k]) + f32(eb[k]))
            total = jnp.concatenate([total, jnp.zeros_like(total)], 0)
            dlr[crop * L : (crop + 1) * L] = b16(total.T)

        def body(crop):
            rs = pl.ds(pl.multiple_of(crop * L, L), L)
            x2, sc2 = norm_rows16(second_in[rs, :])
            o_x2[rs, :] = b16(x2 * g[2:3])
            dx = dot_nt(dlr[rs, :], outer[...])
            gain_grad[2:3] += jnp.sum(dx * x2, 0, keepdims=True)
            ds2 = f32(cot_all[rs, :]) + norm_rows16_back(dx * g[2:3], x2, sc2)
            ds2_16 = b16(ds2)
            ys[rs, 5 * width + wide :] = ds2_16

            @pl.when(crop == 0)
            def _():
                for k in (14, 8, 13, 9):
                    arrive(k)

            dhp = b16(dot_nt(ds2_16, down[...]) * f32(slope[rs, :]))
            ys[rs, 5 * width : 5 * width + wide] = dhp
            dx = dot_nt(dhp, up[...])
            x1, sc1 = norm_rows16(first_in[rs, :])
            gain_grad[1:2] += jnp.sum(dx * x1, 0, keepdims=True)
            df = ds2 + norm_rows16_back(dx * g[1:2], x1, sc1)
            df16 = b16(df)
            ys[rs, 4 * width : 5 * width] = df16

            @pl.when(crop == 0)
            def _():
                for k in (12, 6, 5, 7):
                    arrive(k)

            du = dot_nt(df16, proj[4])
            gate, mixed = f32(gm[rs, 0:width]), f32(gm[rs, width : 2 * width])
            do = du * gate
            do16 = b16(do)
            row = do * mixed
            dgate = b16(du * mixed * gate * (1.0 - gate))
            ys[rs, 3 * width : 4 * width] = dgate
            lane = lax.broadcasted_iota(jnp.int32, (1, L), 1)
            low = jnp.where(lane < L // 2, 1.0, 0.0)
            for t in range(4):
                s = slice(t * L, (t + 1) * L)
                q = qkv[rs, t * L : (t + 1) * L]
                k = qkv[rs, width + t * L : width + (t + 1) * L]
                v = qkv[rs, 2 * width + t * L : 2 * width + (t + 1) * L]
                grads, weights = [], []
                for j, (m, mf) in enumerate(zip(halves(), (low, 1.0 - low))):
                    at = pl.multiple_of((crop * 8 + 2 * t + j) * L, L)
                    p16 = probs[pl.ds(at, L), :]
                    dp = dot_nt(do16[:, s] * m, v)
                    e = f32(p16) * (dp - jnp.sum(row[:, s] * mf, -1, keepdims=True))
                    sdrb[pl.ds(at, L), :] = e
                    grads.append(b16(e))
                    weights.append(p16)
                dq = dot(jnp.concatenate(grads, 1), on_halves(k)) * 0.125
                dk = dot_tn(jnp.concatenate(grads, 0), on_halves(q))
                dv = dot_tn(jnp.concatenate(weights, 0), on_halves(do16[:, s]))
                ys[rs, t * L : (t + 1) * L] = b16(dq)
                ys[rs, width + t * L : width + (t + 1) * L] = b16(dk)
                ys[rs, 2 * width + t * L : 2 * width + (t + 1) * L] = b16(dv)
            dx = dot_nt(ys[rs, 0:width], proj[0])
            for k in range(1, 4):
                dx = dx + dot_nt(ys[rs, k * width : (k + 1) * width], proj[k])
            x0, sc0 = norm_rows16(f32(x_all[rs, :]))
            gain_grad[0:1] += jnp.sum(dx * x0, 0, keepdims=True)
            sds[rs, :] = df + norm_rows16_back(dx * g[0:1], x0, sc0)

        each_row(4, body)
        grp, row = where[2], where[3]
        d_own[...] = sds[pl.ds(pl.multiple_of(grp * L + row * rows, rows), rows), :]
        for h in range(8):
            at = pl.multiple_of((grp * 8 + h) * L + row * rows, rows)
            drb[h * rows : (h + 1) * rows] = sdrb[pl.ds(at, rows), :]
        m_op[...] = dot_tn(o_x2[...], dlr[...])

    return call(
        kernel,
        [
            ((tokens, 6 * width + wide), BF), ((3, width), F32), ((rows, width), F32),
            ((8 * rows, L), F32), ((width, L), F32),
        ],
        [
            ((tokens, L), BF), ((tokens, width), BF), ((4 * 8 * L, L), F32), ((tokens, width), F32),
        ],
        (
            where, ea, eb, x_all, cot_all, qkv, gm, probs, slope, first_in, second_in,
            gains, proj, up, down, outer,
        ), deps=deps, raw=(3, 4, 5, 6, 7, 8, 9, 10, 11, 12, 13, 14, 15), late=(5, 6, 7, 8, 9, 12, 13, 14), far=(0, 1, 2, 3, 4), us=22)


def weight_grads(xs, ys, width, wide):
    tokens = xs.shape[0]
    blocks = wide // width

    def kernel(x, y, out):
        out[...] = dot_tn(x[...], y[...]).reshape(out.shape)

    def run(steps, x_at, y_at, shape, block, out_at):
        return pl.pallas_call(
            kernel,
            grid=(steps,),
            out_shape=jax.ShapeDtypeStruct(shape, F32),
            in_specs=[
                pl.BlockSpec((tokens, width), x_at),
                pl.BlockSpec((tokens, width), y_at),
            ],
            out_specs=pl.BlockSpec(block, out_at),
            compiler_params=pltpu.CompilerParams(vmem_limit_bytes=32 << 20),
            cost_estimate=pl.CostEstimate(
                flops=4 * 10**9,
                bytes_accessed=steps * width * width * 8,
                transcendentals=0,
            ),
        )(pltpu.with_memory_space_constraint(xs, pltpu.HBM), pltpu.with_memory_space_constraint(ys, pltpu.HBM))

    proj = run(
        5, lambda i: (0, i // 4), lambda i: (0, i), (5, width, width), (1, width, width),
        lambda i: (i, 0, 0),
    )
    up = run(
        blocks, lambda i: (0, 2), lambda i: (0, 5 + i), (width, wide), (width, width),
        lambda i: (0, i),
    )
    down = run(
        blocks, lambda i: (0, 3 + i), lambda i: (0, 5 + blocks), (wide, width), (width, width),
        lambda i: (i, 0),
    )
    return proj, up, down


def project_pair(z, r, rows, m5t, pmask, sa, sb):
    xh, _ = norm_cols(z)
    p = dot(m5t[0:512], b16(xh))
    mk = pmask[pl.ds(r, 1), :]
    sa[pl.ds(r, C, stride=rows), :] = sig(p[0:C]) * p[C : 2 * C] * mk
    sb[pl.ds(r, C, stride=rows), :] = sig(p[2 * C : 3 * C]) * p[3 * C : 4 * C] * mk


def put_pair(n, ab, sa, sb):
    part = sa.shape[0] // n
    for d in range(n):
        ab[d, 0:part] = b16(sa[d * part : (d + 1) * part])
        ab[d, part : 2 * part] = b16(sb[d * part : (d + 1) * part])


def gated_product(z, r, rows, gatet, mot, sp):
    xh, _ = norm_cols(z)
    gate = sig(dot(gatet[...], b16(xh)))
    ph, _ = norm_cols(sp[pl.ds(r, C, stride=rows), :])
    return z + dot(mot[...], b16(ph)) * gate


def front(n, rows, where, lr_all, pair, outer_w, m5ts, deps=()):
    opm = outer_w.shape[0]

    def kernel(
        where, lr_all, pair, outer_w, m5ts,
        z1, ab, pmask, key_row, inner, lrt, left_own, sa, sb, slr, spm,
    ):
        m5t = m5ts.at[0]
        crop, block = where[0], where[1]
        lr16 = lr_all[pl.ds(crop * n, n)].reshape(L, C)
        lr = f32(lr16)
        turned = lr.T
        lrt[...] = turned
        mrow = turned[2 * opm : 2 * opm + 1]
        key_row[...] = (mrow - 1.0) * MASKED
        first = pl.multiple_of(block * rows, rows)
        spm[...] = jnp.broadcast_to(mrow, (L, L)).T * mrow
        pmask[...] = spm[pl.ds(first, rows), :]
        slr[...] = lr
        left = b16(slr[pl.ds(first, rows), :])
        left_own[...] = left
        for b in range(opm):
            inner[b * rows : (b + 1) * rows] = dot(left[:, 0:opm], outer_w[b])
        edge = jnp.zeros((opm, C), BF)

        def body(r):
            mine = b16(inner[pl.ds(r, opm, stride=rows), :])
            mine = jnp.concatenate([edge, mine, edge, edge], 0)
            z = (f32(pair[r]) + dot(lr16, mine)).T
            z1[:, cols(r)] = z
            project_pair(z, r, rows, m5t, pmask, sa, sb)

        each_row(rows, body)
        put_pair(n, ab, sa, sb)

    part = C * rows // n
    return call(
        kernel,
        [
            ((C, rows * L), F32), ((n, 2 * part, L), BF), ((rows, L), F32), ((1, L), F32),
            ((opm * rows, C), F32), ((C, L), F32), ((rows, C), BF),
        ],
        [((C * rows, L), F32)] * 2 + [((L, C), F32), ((L, L), F32)],
        (where, lr_all, pair, outer_w, m5ts), deps=deps, raw=(2, 3, 4), far=(0, 2, 3, 4, 5, 6), us=5)


def middle(n, rows, z1, prod, mots, pmask, m5ts):
    def kernel(z1, prod, mots, pmask, m5ts, z2, ab, sa, sb, sp):
        gatet, mot, m5t = m5ts.at[0, 512:640], mots.at[0], m5ts.at[1]
        sp[...] = f32(prod[...])

        def body(r):
            z = gated_product(z1[:, cols(r)], r, rows, gatet, mot, sp)
            z2[:, cols(r)] = z
            project_pair(z, r, rows, m5t, pmask, sa, sb)

        each_row(rows, body)
        put_pair(n, ab, sa, sb)

    part = C * rows // n
    return call(
        kernel,
        [((C, rows * L), F32), ((n, 2 * part, L), BF)],
        [((C * rows, L), F32)] * 3,
        (z1, prod, mots, pmask, m5ts), raw=(0, 1, 2, 3, 4), far=(0,), us=4)


def start_front(n, rows, z2, prod, m5ts, mots, abts, deps=()):
    def kernel(z2, prod, m5ts, mots, abts, z3, tb, sp, st):
        gatet, mot, abt = m5ts.at[1, 512:640], mots.at[1], abts.at[0]
        sp[...] = f32(prod[...])

        def body(r):
            z = gated_product(z2[:, cols(r)], r, rows, gatet, mot, sp)
            z3[:, cols(r)] = z
            xh, _ = norm_cols(z)
            st[pl.ds(r, HPAD, stride=rows), :] = dot(abt[...], b16(xh))

        each_row(rows, body)
        for d in range(n):
            tb[d] = b16(st[0 : TH * rows])

    return call(
        kernel,
        [((C, rows * L), F32), ((n, TH * rows, L), BF)],
        [((C * rows, L), F32), ((HPAD * rows, L), F32)],
        (z2, prod, m5ts, mots, abts), deps=deps, raw=(0, 1, 2, 3, 4), far=(0,), us=4)


def channel_product(n, rows, outgoing, ab):
    def kernel(ab, out):
        part = C * rows // n
        for ch in range(C // n):
            a = ab[:, ch * rows : (ch + 1) * rows, :].reshape(L, L)
            b = ab[:, part + ch * rows : part + (ch + 1) * rows, :].reshape(L, L)
            prod = dot_nt(a, b) if outgoing else dot_tn(a, b)
            out[:, ch * rows : (ch + 1) * rows, :] = b16(prod).reshape(n, rows, L)

    return call(kernel, [((n, C * rows // n, L), BF)], [], (ab,), raw=(0,), us=1)[0]


def channel_product_back(n, rows, outgoing, ab, dprod, deps=()):
    def kernel(ab, dprod, out):
        part = C * rows // n
        for ch in range(C // n):
            low, high = ch * rows, (ch + 1) * rows
            a = ab[:, low:high, :].reshape(L, L)
            b = ab[:, part + low : part + high, :].reshape(L, L)
            g = dprod[:, low:high, :].reshape(L, L)
            if outgoing:
                da, db = dot(g, b), dot_tn(g, a)
            else:
                da, db = dot_nt(b, g), dot(a, g)
            out[:, low:high, :] = b16(da).reshape(n, rows, L)
            out[:, part + low : part + high, :] = b16(db).reshape(n, rows, L)

    return call(kernel, [((n, 2 * C * rows // n, L), BF)], [], (ab, dprod), deps=deps, raw=(0,), us=2)[0]


def head_masks():
    lane = lax.broadcasted_iota(jnp.int32, (1, C), 1)
    return [b16(jnp.where((lane >= h * HD) & (lane < (h + 1) * HD), 1.0, 0.0)) for h in range(TH)]


def by_head(x):
    pm = b16(x.T)
    return jnp.concatenate([pm * m for m in head_masks()], 0)


def attend(x16, a4t, bias):
    p4 = dot(a4t[...], x16)
    q, k, v = p4[0:C], p4[C : 2 * C], p4[2 * C : 3 * C]
    gate = sig(p4[3 * C : 4 * C])
    logits = dot(by_head(k), b16(q)) + bias[...]
    raised, outs = [], []
    v16 = b16(v)
    for h in range(TH):
        s = logits[h * L : (h + 1) * L]
        e = jnp.exp(s - jnp.max(s, 0, keepdims=True))
        inv = 1.0 / jnp.sum(e, 0, keepdims=True)
        raised.append((e, inv))
        outs.append(dot(v16[h * HD : (h + 1) * HD], b16(e)) * inv)
    mixed = jnp.concatenate(outs, 0)
    return (q, k, v, gate, raised, mixed)


def attend_back(state, dy16, ao, dbias):
    q, k, v, gate, raised, mixed = state
    du = dot(ao[...], dy16)
    do = du * gate
    dgate = du * mixed * gate * (1.0 - gate)
    do16, q16, k16 = b16(do), b16(q), b16(k)
    dp = dot(by_head(v), do16)
    row = do * mixed
    dq, dk, dv = [], [], []
    for h in range(TH):
        s = slice(h * HD, (h + 1) * HD)
        w = slice(h * L, (h + 1) * L)
        e, inv = raised[h]
        p = e * inv
        ds = p * (dp[w] - jnp.sum(row[s], 0, keepdims=True))
        dbias[w, :] += ds
        ds16, p16 = b16(ds), b16(p)
        dv.append(dot_nt(do16[s], p16))
        dq.append(dot(k16[s], ds16))
        dk.append(dot_nt(q16[s], ds16))
    return jnp.concatenate([b16(x) for x in dq + dk + dv] + [b16(dgate)], 0)


def start_attention(n, rows, z3, tb_all, key_row, a4ts, aots, abts, deps=()):
    def kernel(z3, tb_all, key_row, a4ts, aots, abts, z4, send, bias, st, se):
        a4t, aot, abt = a4ts.at[0], aots.at[0], abts.at[1]
        for h in range(TH):
            b = f32(tb_all[:, h * rows : (h + 1) * rows, :].reshape(L, L)) + key_row[...]
            bias[h * L : (h + 1) * L, :] = b.T

        def body(r):
            z = z3[:, cols(r)]
            xh, _ = norm_cols(z)
            q, k, v, gate, raised, mixed = attend(b16(xh), a4t, bias)
            z = z + dot(aot[...], b16(mixed * gate))
            z4[:, cols(r)] = z
            st[pl.ds(r, L, stride=rows), :] = z.T
            xe, _ = norm_cols(z)
            se[pl.ds(r, HPAD, stride=rows), :] = dot(abt[...], b16(xe))

        each_row(rows, body)
        part = L * rows // n
        for d in range(n):
            send[d, 0:part] = b16(st[d * part : (d + 1) * part])
            send[d, part : part + TH * rows] = b16(se[0 : TH * rows])

    part = L * rows // n
    return call(
        kernel,
        [((C, rows * L), F32), ((n, part + TH * rows, L), BF)],
        [((TH * L, L), F32), ((L * rows, C), F32), ((HPAD * rows, L), F32)],
        (z3, tb_all, key_row, a4ts, aots, abts), deps=deps, raw=(0, 1, 2, 3, 4, 5), far=(0,), us=12)


def end_both(n, rows, recv, cot, key_row, a4ts, a4s, aots, aos, upt, up, dnt, dn, deps=()):
    part = L * rows // n

    def kernel(
        recv, cot, key_row, a4ts, a4s, aots, aos, upt, up, dnt, dn,
        pout, send, m_up, m_dn, m_a4, m_ao,
        bias, dbias, sout, sdz, o_h, o_dh, o_x5, o_cot, o_x4, o_d4, o_u, o_dy,
    ):
        a4t, a4, aot, ao = a4ts.at[1], a4s.at[1], aots.at[1], aos.at[1]
        kb = jnp.broadcast_to(key_row[...], (L, L)).T
        for h in range(TH):
            b = recv[:, part + h * rows : part + (h + 1) * rows, :].reshape(L, L)
            bias[h * L : (h + 1) * L, :] = f32(b) + kb
        dbias[...] = jnp.zeros_like(dbias)

        def body(r):
            w = cols(r)
            z4 = f32(recv[:, pl.ds(pl.multiple_of(r * rows, rows), rows), :].reshape(L, C)).T
            x4, scale4 = norm_cols(z4)
            x16 = b16(x4)
            state = attend(x16, a4t, bias)
            gated = b16(state[5] * state[3])
            z5 = z4 + dot(aot[...], gated)
            x5, scale5 = norm_cols(z5)
            x516 = b16(x5)
            hid, slope = gelu_parts(dot(upt[...], x516))
            h16 = b16(hid)
            z6 = z5 + dot(dnt[...], h16)
            sout[pl.ds(r, L, stride=rows), :] = z6.T
            dz6 = f32(cot[r]).T
            c16 = b16(dz6)
            dh16 = b16(dot(dn[...], c16) * slope)
            dz5 = dz6 + norm_cols_back(dot(up[...], dh16), x5, scale5)
            dy16 = b16(dz5)
            d4 = attend_back(state, dy16, ao, dbias)
            dz4 = dz5 + norm_cols_back(dot(a4[...], d4), x4, scale4)
            sdz[pl.ds(r, L, stride=rows), :] = dz4.T
            o_h[:, w] = h16
            o_dh[:, w] = dh16
            o_x5[:, w] = x516
            o_cot[:, w] = c16
            o_x4[:, w] = x16
            o_d4[:, w] = d4
            o_u[:, w] = gated
            o_dy[:, w] = dy16

        each_row(rows, body)
        for d in range(n):
            pout[d] = b16(sout[d * part : (d + 1) * part])
            send[d, 0:part] = b16(sdz[d * part : (d + 1) * part])
            for h in range(TH):
                send[d, part + h * rows : part + (h + 1) * rows] = b16(
                    dbias[h * L + d * rows : h * L + (d + 1) * rows]
                )
        for k in range(4):
            s = slice(k * C, (k + 1) * C)
            m_up[s] = dot_nt(o_x5[...], o_dh[s])
            m_a4[s] = dot_nt(o_x4[...], o_d4[s])
        m_dn[...] = dot_nt(o_h[...], o_cot[...])
        m_ao[...] = dot_nt(o_u[...], o_dy[...])

    wide = rows * L
    return call(
        kernel,
        [
            ((n, part, C), BF), ((n, part + TH * rows, L), BF),
            ((512, C), F32), ((512, C), F32), ((512, C), F32), ((C, C), F32),
        ],
        [
            ((TH * L, L), F32), ((TH * L, L), F32), ((L * rows, C), F32), ((L * rows, C), F32),
            ((512, wide), BF), ((512, wide), BF), ((C, wide), BF), ((C, wide), BF),
            ((C, wide), BF), ((512, wide), BF), ((C, wide), BF), ((C, wide), BF),
        ],
        (recv, cot, key_row, a4ts, a4s, aots, aos, upt, up, dnt, dn),
        deps=deps, raw=(1, 2, 3, 4, 5, 6, 7, 8, 9, 10), far=(2, 3, 4, 5), us=36)


def start_back(n, rows, z3, z4, recv, tb_all, key_row, a4ts, a4s, aos, abts, deps=()):
    part = L * rows // n

    def kernel(
        z3, z4, recv, tb_all, key_row, a4ts, a4s, aos, abts,
        dz4_out, dxs, dtb, m_a4, m_ao, m_ab,
        bias, dbias, seb, o_x3, o_d4, o_u, o_dy, o_x4, o_eb,
    ):
        a4t, a4, ao, abt = a4ts.at[0], a4s.at[0], aos.at[0], abts.at[1]
        for h in range(TH):
            b = f32(tb_all[:, h * rows : (h + 1) * rows, :].reshape(L, L)) + key_row[...]
            bias[h * L : (h + 1) * L, :] = b.T
        dbias[...] = jnp.zeros_like(dbias)
        seb[...] = jnp.zeros_like(seb)
        total = f32(recv[0, part : part + TH * rows])
        for d in range(1, n):
            total = total + f32(recv[d, part : part + TH * rows])
        seb[0 : TH * rows, :] = total

        def body(r):
            w = cols(r)
            x4, scale4 = norm_cols(z4[:, w])
            eb16 = b16(seb[pl.ds(r, HPAD, stride=rows), :])
            dz4 = f32(recv[:, pl.ds(pl.multiple_of(r * rows, rows), rows), :].reshape(L, C)).T
            dz4 = dz4 + norm_cols_back(dot_tn(abt[...], eb16), x4, scale4)
            dz4_out[:, w] = dz4
            x3, _ = norm_cols(z3[:, w])
            x16 = b16(x3)
            state = attend(x16, a4t, bias)
            dy16 = b16(dz4)
            d4 = attend_back(state, dy16, ao, dbias)
            dxs[:, w] = dot(a4[...], d4)
            o_x3[:, w] = x16
            o_d4[:, w] = d4
            o_u[:, w] = b16(state[5] * state[3])
            o_dy[:, w] = dy16
            o_x4[:, w] = b16(x4)
            o_eb[:, w] = eb16

        each_row(rows, body)
        for h in range(TH):
            turned = b16(dbias[h * L : (h + 1) * L, :].T)
            for d in range(n):
                dtb[d, h * rows : (h + 1) * rows] = turned[d * rows : (d + 1) * rows]
        for k in range(4):
            s = slice(k * C, (k + 1) * C)
            m_a4[s] = dot_nt(o_x3[...], o_d4[s])
        m_ao[...] = dot_nt(o_u[...], o_dy[...])
        m_ab[...] = dot_nt(o_eb[...], o_x4[...])

    wide = rows * L
    return call(
        kernel,
        [
            ((C, wide), F32), ((C, wide), F32), ((n, TH * rows, L), BF),
            ((512, C), F32), ((C, C), F32), ((HPAD, C), F32),
        ],
        [
            ((TH * L, L), F32), ((TH * L, L), F32), ((HPAD * rows, L), F32),
            ((C, wide), BF), ((512, wide), BF), ((C, wide), BF), ((C, wide), BF),
            ((C, wide), BF), ((HPAD, wide), BF),
        ],
        (z3, z4, recv, tb_all, key_row, a4ts, a4s, aos, abts),
        deps=deps, raw=(0, 1, 3, 4, 5, 6, 7, 8), far=(0, 1, 3, 4, 5), us=20)


def product_back(z, dz, r, rows, sp, gatet, mot, mof, sdp, dgp_out, o_ph, o_do):
    w = cols(r)
    xh, _ = norm_cols(z)
    gate = sig(dot(gatet[...], b16(xh)))
    ph, scale = norm_cols(sp[pl.ds(r, C, stride=rows), :])
    ph16 = b16(ph)
    out = dot(mot[...], ph16)
    dgp_out[:, w] = b16(dz * out * gate * (1.0 - gate))
    do16 = b16(dz * gate)
    sdp[pl.ds(r, C, stride=rows), :] = norm_cols_back(dot(mof[...], do16), ph, scale)
    o_ph[:, w] = ph16
    o_do[:, w] = do16


def third_back(n, rows, z3, dz4, dxs, recv, abts, z2, prod, m5ts, mots, mofs, deps=()):
    def kernel(
        z3, dz4, dxs, recv, abts, z2, prod, m5ts, mots, mofs,
        dz3, dgp, dp, m_ab, m_mo,
        stb, sp, sdp, o_x3, o_tb, o_ph, o_do,
    ):
        abt, gatet, mot, mof = abts.at[0], m5ts.at[1, 512:640], mots.at[1], mofs.at[1]
        sp[...] = f32(prod[...])
        stb[...] = jnp.zeros_like(stb)
        total = f32(recv[0])
        for d in range(1, n):
            total = total + f32(recv[d])
        stb[0 : TH * rows, :] = total

        def body(r):
            w = cols(r)
            x3, scale3 = norm_cols(z3[:, w])
            tb16 = b16(stb[pl.ds(r, HPAD, stride=rows), :])
            dx = dxs[:, w] + dot_tn(abt[...], tb16)
            dz = dz4[:, w] + norm_cols_back(dx, x3, scale3)
            dz3[:, w] = dz
            o_x3[:, w] = b16(x3)
            o_tb[:, w] = tb16
            product_back(z2[:, w], dz, r, rows, sp, gatet, mot, mof, sdp, dgp, o_ph, o_do)

        each_row(rows, body)
        dp[...] = b16(sdp[...])
        m_ab[...] = dot_nt(o_tb[...], o_x3[...])
        m_mo[...] = dot_nt(o_ph[...], o_do[...])

    wide = rows * L
    return call(
        kernel,
        [
            ((C, wide), F32), ((C, wide), BF), ((C * rows, L), BF),
            ((HPAD, C), F32), ((C, C), F32),
        ],
        [
            ((HPAD * rows, L), F32), ((C * rows, L), F32), ((C * rows, L), F32),
            ((C, wide), BF), ((HPAD, wide), BF), ((C, wide), BF), ((C, wide), BF),
        ],
        (z3, dz4, dxs, recv, abts, z2, prod, m5ts, mots, mofs), deps=deps, raw=(0, 1, 2, 4, 5, 6, 7, 8, 9), far=(0, 1, 3, 4), us=7)


def projections_back(n, rows, z, dz, dgp, r, pmask, m5t, m5, sa, sb, o_x, o_d5):
    w = cols(r)
    xh, scale = norm_cols(z)
    x16 = b16(xh)
    p = dot(m5t[0:512], x16)
    mk = pmask[pl.ds(r, 1), :]
    da = sa[pl.ds(r, C, stride=rows), :] * mk
    db = sb[pl.ds(r, C, stride=rows), :] * mk
    ga, gb = sig(p[0:C]), sig(p[2 * C : 3 * C])
    va, vb = p[C : 2 * C], p[3 * C : 4 * C]
    d5 = jnp.concatenate(
        [
            b16(da * va * ga * (1.0 - ga)),
            b16(da * ga),
            b16(db * vb * gb * (1.0 - gb)),
            b16(db * gb),
            dgp[:, w],
        ],
        0,
    )
    o_x[:, w] = x16
    o_d5[:, w] = d5
    return dz + norm_cols_back(dot(m5[...], d5), xh, scale)


def take_pair(n, dab, sa, sb):
    part = sa.shape[0] // n
    for d in range(n):
        sa[d * part : (d + 1) * part, :] = f32(dab[d, 0:part])
        sb[d * part : (d + 1) * part, :] = f32(dab[d, part : 2 * part])


def second_back(n, rows, z2, dz3, dgp, dab, pmask, m5ts, m5s, z1, prod, mots, mofs, deps=()):
    def kernel(
        z2, dz3, dgp, dab, pmask, m5ts, m5s, z1, prod, mots, mofs,
        dz2, dgp_out, dp, m_m5, m_mo,
        sa, sb, sp, sdp, o_x, o_d5, o_ph, o_do,
    ):
        m5t, m5, gatet = m5ts.at[1], m5s.at[1], m5ts.at[0, 512:640]
        mot, mof = mots.at[0], mofs.at[0]
        sp[...] = f32(prod[...])
        take_pair(n, dab, sa, sb)

        def body(r):
            w = cols(r)
            dz = projections_back(
                n, rows, z2[:, w], dz3[:, w], dgp, r, pmask, m5t, m5, sa, sb, o_x, o_d5
            )
            dz2[:, w] = dz
            product_back(z1[:, w], dz, r, rows, sp, gatet, mot, mof, sdp, dgp_out, o_ph, o_do)

        each_row(rows, body)
        dp[...] = b16(sdp[...])
        for k in range(5):
            s = slice(k * C, (k + 1) * C)
            m_m5[s] = dot_nt(o_x[...], o_d5[s])
        m_mo[...] = dot_nt(o_ph[...], o_do[...])

    wide = rows * L
    return call(
        kernel,
        [
            ((C, wide), F32), ((C, wide), BF), ((C * rows, L), BF),
            ((640, C), F32), ((C, C), F32),
        ],
        [
            ((C * rows, L), F32), ((C * rows, L), F32), ((C * rows, L), F32), ((C * rows, L), F32),
            ((C, wide), BF), ((640, wide), BF), ((C, wide), BF), ((C, wide), BF),
        ],
        (z2, dz3, dgp, dab, pmask, m5ts, m5s, z1, prod, mots, mofs), deps=deps, raw=(0, 1, 2, 4, 5, 6, 7, 8, 9, 10), far=(0, 1, 3, 4), us=11)


def first_back(n, rows, copies, where, z1, dz2, dgp, dab, pmask, m5ts, m5s, inner, lrt, left_own, outer_w, deps=()):
    opm = outer_w.shape[0]

    def kernel(
        where, z1, dz2, dgp, dab, pmask, m5ts, m5s, inner, lrt, left_own, outer_w,
        dz1, ends, m_oo, m_m5,
        sa, sb, o_x, o_d5, sdi, sdr,
    ):
        m5t, m5 = m5ts.at[0], m5s.at[0]
        take_pair(n, dab, sa, sb)
        sdr[...] = jnp.zeros_like(sdr)
        right_t = b16(lrt[opm : 2 * opm])

        def body(r):
            w = cols(r)
            dz = projections_back(
                n, rows, z1[:, w], dz2[:, w], dgp, r, pmask, m5t, m5, sa, sb, o_x, o_d5
            ).T
            dz16 = b16(dz)
            dz1[r] = dz16
            sdi[pl.ds(r, opm, stride=rows), :] = dot(right_t, dz16)
            sdr[...] += dot_nt(b16(inner[pl.ds(r, opm, stride=rows), :]), dz16)

        each_row(rows, body)
        left = left_own[:, 0:opm]
        dleft = jnp.zeros((opm, rows), F32)
        for b in range(opm):
            d16 = b16(sdi[b * rows : (b + 1) * rows])
            m_oo[b * opm : (b + 1) * opm] = dot_tn(left, d16)
            dleft = dleft + dot_nt(outer_w[b], d16)
        lane = lax.broadcasted_iota(jnp.int32, (rows, L), 1)
        spot = lax.broadcasted_iota(jnp.int32, (rows, L), 0) + where[1] * rows
        dleft = dot(b16(dleft), b16(jnp.where(lane == spot, 1.0, 0.0)))
        both = jnp.concatenate([dleft, sdr[...]], 0) * lrt[2 * opm : 2 * opm + 1]
        for d in range(copies):
            ends[d] = b16(both)
        for k in range(5):
            s = slice(k * C, (k + 1) * C)
            m_m5[s] = dot_nt(o_x[...], o_d5[s])

    wide = rows * L
    return call(
        kernel,
        [
            ((rows, L, C), BF), ((copies, 2 * opm, L), BF), ((opm * opm, C), F32), ((640, C), F32),
        ],
        [
            ((C * rows, L), F32), ((C * rows, L), F32), ((C, wide), BF), ((640, wide), BF),
            ((opm * rows, C), F32), ((opm, L), F32),
        ],
        (where, z1, dz2, dgp, dab, pmask, m5ts, m5s, inner, lrt, left_own, outer_w), deps=deps, raw=(1, 2, 3, 5, 6, 7, 8, 9, 10, 11), far=(2, 3), us=11)


def last_back(rows, pair, drb, dz1, sbt, deps=()):
    def kernel(pair, drb, dz1, sbt, grad, m_sb, o_x, o_d):
        def body(r):
            w = cols(r)
            xh, scale = norm_cols(f32(pair[r]).T)
            d = drb[pl.ds(r, 8, stride=rows), :]
            d16 = b16(jnp.concatenate([d, jnp.zeros_like(d)], 0))
            back = norm_cols_back(dot_tn(sbt[...], d16), xh, scale)
            grad[r] = f32(dz1[r]) + back.T
            o_x[:, w] = b16(xh)
            o_d[:, w] = d16

        each_row(rows, body)
        m_sb[...] = dot_nt(o_d[...], o_x[...])

    wide = rows * L
    return call(
        kernel,
        [((rows, L, C), F32), ((HPAD, C), F32)],
        [((C, wide), BF), ((HPAD, wide), BF)],
        (pair, drb, dz1, sbt), deps=deps, raw=(0, 1, 2, 3), us=3)


def collect(where, parts, half, deps):
    def kernel(where, *refs):
        sources, (kept, given, rows) = refs[: len(parts)], refs[len(parts) :]
        core = where[3] % 2
        at = 0
        for ref in sources:
            rows[at : at + ref.shape[0]] = ref[...]
            at += ref.shape[0]
        if at < 2 * half:
            rows[at : 2 * half] = jnp.zeros((2 * half - at, C), F32)
        kept[...] = rows[pl.ds(pl.multiple_of(core * half, half), half), :]
        given[...] = b16(rows[pl.ds(pl.multiple_of((1 - core) * half, half), half), :])

    return call(
        kernel,
        [((half, C), F32), ((half, C), BF)],
        [((2 * half, C), F32)],
        (where, *parts),
        deps=deps,
        us=3,
    )


def sum_copies(x, count, deps):
    def kernel(x, out):
        total = b16(jnp.sum(f32(x[...]), 0))
        for d in range(count):
            out[d] = total

    return call(kernel, [((count,) + x.shape[1:], BF)], [], (x,), deps=deps, us=2)[0]


def finish(where, near, far, m_sb, gp, gm, mp, mg, mo, ap, ab, pu, sb, places, half, opm, n_all, deps):
    def kernel(
        where, near, far, m_sb, gp, gm, mp, mg, mo, ap, ab, pu, sb,
        g_pg, g_mg, g_sb, g_oo, g_mp, g_mgt, g_mo, g_ap, g_ab, g_ao, g_pu, g_pd,
        rows,
    ):
        core = where[3] % 2
        rows[pl.ds(pl.multiple_of(core * half, half), half), :] = f32(near[...])
        rows[pl.ds(pl.multiple_of((1 - core) * half, half), half), :] = f32(far[...])

        def take(name, count, skip=0):
            at = places[name] + skip
            return rows[at : at + count]

        gpv, gmv = f32(gp[...]), f32(gm[...])

        def column(row):
            return jnp.broadcast_to(row, (C, C)).T

        def over_lanes(x):
            return jnp.sum(x.T, 0, keepdims=True)

        def turned(w):
            shape = (HPAD, w.shape[1])
            row = lax.broadcasted_iota(jnp.int32, shape, 0)
            lane = lax.broadcasted_iota(jnp.int32, shape, 1)
            return dot_nt(b16(jnp.where(row == lane, 1.0, 0.0)), w)

        total = m_sb[0]
        for d in range(1, n_all):
            total = total + m_sb[d]
        g_pg[0:1] = jnp.sum(turned(sb[...]) * total, 0, keepdims=True)
        wide = jnp.concatenate([total * gpv[0:1], jnp.zeros((C - HPAD, C), F32)], 0)
        g_sb[...] = wide.T[:, 0:8]
        for t in range(2):
            g = column(gpv[1 + t : 2 + t])
            both = jnp.zeros((C, C), F32)
            for k in range(5):
                m = take("m5%d" % t, C, k * C)
                both = both + m * f32(mp[t, k] if k < 4 else mg[t])
                if k < 4:
                    g_mp[t, k] = m * g
                else:
                    g_mgt[t] = m * g
            g_pg[1 + t : 2 + t] = over_lanes(both)
            m = take("mo%d" % t, C)
            g_mo[t] = m * column(gmv[t : t + 1])
            g_mg[t : t + 1] = over_lanes(m * f32(mo[t]))
            g = column(gpv[3 + t : 4 + t])
            both = jnp.zeros((C, C), F32)
            for k in range(4):
                m = take("a4%d" % t, C, k * C)
                if k == 0:
                    m = m * HD**-0.5
                both = both + m * f32(ap[t, k])
                g_ap[t, k] = m * g
            m = take("ab%d" % t, HPAD)
            g_pg[3 + t : 4 + t] = over_lanes(both) + jnp.sum(turned(ab[t]) * m, 0, keepdims=True)
            wide = jnp.concatenate(
                [m * gpv[3 + t : 4 + t], jnp.zeros((C - HPAD, C), F32)], 0
            )
            g_ab[t] = wide.T[:, 0:TH]
            g_ao[t] = take("ao%d" % t, C)
        g = column(gpv[5:6])
        both = jnp.zeros((C, C), F32)
        for k in range(4):
            s = slice(k * C, (k + 1) * C)
            m = take("up", C, k * C)
            both = both + m * f32(pu[:, s])
            g_pu[:, s] = m * g
        g_pg[5:6] = over_lanes(both)
        g_pd[...] = take("dn", 512)
        for b in range(opm):
            g_oo[:, b, :] = take("oo", opm, b * opm)

    outs = [
        (6, C), (2, C), (C, 8), (opm, opm, C), (2, 4, C, C), (2, C, C), (2, C, C), (2, 4, C, C),
        (2, C, TH), (2, C, C), (C, 512), (512, C),
    ]
    return call(
        kernel,
        [(s, F32) for s in outs],
        [((2 * half, C), F32)],
        (where, near, far, m_sb, gp, gm, mp, mg, mo, ap, ab, pu, sb),

        raw=(4, 5, 6, 7, 8, 9, 10, 11, 12), deps=deps, us=4,
    )


PRECISE = lax.Precision.HIGHEST


def for_sending(shard):

    def short(part):
        return part.astype(jnp.bfloat16) if part.dtype == jnp.float32 else part

    return jax.tree.map(short, shard)


def widen(operand):
    return operand.astype(jnp.float32)


def narrow(operand):
    return operand.astype(jnp.bfloat16)


def rounded(operand):
    return lax.optimization_barrier(operand.astype(jnp.bfloat16)).astype(jnp.float32)


def contract(pattern, first_term, second_term):
    return jnp.einsum(pattern, first_term, second_term, precision=PRECISE)


def low_product(pattern, first_term, second_term):
    return jnp.einsum(pattern, first_term, second_term, preferred_element_type=jnp.float32)


def norm_rows(operand, gain_vec):
    centre = operand - jnp.mean(operand, -1, keepdims=True)
    spread = jnp.mean(centre * centre, -1, keepdims=True)
    return centre * lax.rsqrt(spread + EPSILON) * gain_vec


def soft_weights(logits):
    highest = jnp.max(logits, -1, keepdims=True)
    raised = jnp.exp(logits - highest)
    return raised / jnp.sum(raised, -1, keepdims=True)


def single_attend(queries, key_rows, values, gate_value, pair_bias, key_bias, weight_out):
    head_count = pair_bias.shape[0]
    feature_width = queries.shape[-1]
    head_size = feature_width // head_count
    query_heads = queries.reshape(queries.shape[0], head_count, head_size)
    key_heads = key_rows.reshape(key_rows.shape[0], head_count, head_size)
    value_heads = values.reshape(values.shape[0], head_count, head_size)
    logits = (
        contract("ihd,jhd->hij", query_heads, key_heads) * head_size ** (-0.5)
        + pair_bias
        + key_bias
    )
    mixed = contract("hij,jhd->ihd", soft_weights(logits), value_heads).reshape(
        queries.shape[0], feature_width
    )
    return contract("is,st->it", mixed * jax.nn.sigmoid(gate_value), weight_out)


def tri_attend(normed, pair_bias, weight_four, weight_out, key_bias):
    head_count = pair_bias.shape[0]
    feature_width = normed.shape[-1]
    head_size = feature_width // head_count

    def one_row(row_in):
        projected = contract("lc,ncd->nld", row_in, weight_four)
        shaped = projected[:3].reshape(3, row_in.shape[0], head_count, head_size)
        logits = (
            contract("jhd,khd->hjk", shaped[0], shaped[1]) * head_size ** (-0.5)
            + pair_bias
            + key_bias
        )
        mixed = contract("hjk,khd->jhd", soft_weights(logits), shaped[2]).reshape(
            row_in.shape[0], feature_width
        )
        return contract("lc,cd->ld", mixed * jax.nn.sigmoid(projected[3]), weight_out)

    return lax.map(jax.checkpoint(one_row), normed)


def mult_front(pair_in, gain_vec, weight_four, weight_gate, pair_mask):
    normed = norm_rows(pair_in, gain_vec)
    projected = contract("rlc,ncm->nmrl", normed, weight_four)
    left_side = jax.nn.sigmoid(projected[0]) * projected[1] * pair_mask
    right_side = jax.nn.sigmoid(projected[2]) * projected[3] * pair_mask
    gate_value = jax.nn.sigmoid(contract("rlc,cd->rld", normed, weight_gate))
    return (left_side, right_side, gate_value)


def mult_back(pair_in, product, gate_value, gain_vec, weight_out):
    centre = product - jnp.mean(product, 0, keepdims=True)
    spread = jnp.mean(centre * centre, 0, keepdims=True)
    scaled = centre * lax.rsqrt(spread + EPSILON) * gain_vec[:, None, None]
    return pair_in + contract("mrl,mc->rlc", scaled, weight_out) * gate_value


def outgoing_forward(left_chan, right_chan):
    return low_product("mik,mjk->mij", left_chan, right_chan)


def outgoing_backward(left_chan, right_chan, grad_out):
    return (
        low_product("mij,mjk->mik", grad_out, right_chan),
        low_product("mij,mik->mjk", grad_out, left_chan),
    )


def incoming_forward(left_chan, right_chan):
    return low_product("mki,mkj->mij", left_chan, right_chan)


def incoming_backward(left_chan, right_chan, grad_out):
    return (
        low_product("mij,mkj->mki", grad_out, right_chan),
        low_product("mij,mki->mkj", grad_out, left_chan),
    )


def to_channels(operand):
    return jax.tree.map(
        lambda part, own: part.astype(own.dtype),
        lax.all_to_all(for_sending(operand), "rows", split_axis=0, concat_axis=1, tiled=True),
        operand,
    )


def to_rows(operand):
    return jax.tree.map(
        lambda part, own: part.astype(own.dtype),
        lax.all_to_all(for_sending(operand), "rows", split_axis=1, concat_axis=0, tiled=True),
        operand,
    )


def turn_cols(operand):
    return jnp.swapaxes(
        lax.all_to_all(operand, "rows", split_axis=1, concat_axis=0, tiled=True), 0, 1
    )


def turn_rows(operand):
    return lax.all_to_all(
        jnp.swapaxes(operand, 0, 1), "rows", split_axis=0, concat_axis=1, tiled=True
    )


def gather_bias(operand):
    return lax.all_gather(operand, "rows", axis=1, tiled=True)


def scatter_bias(operand):
    return lax.psum_scatter(operand, "rows", scatter_dimension=1, tiled=True)


def general_local(
    single_rep,
    pair_rep,
    residue_mask,
    single_gains,
    pair_gains,
    mult_gains,
    single_proj,
    single_bias,
    single_up,
    single_down,
    opm_proj,
    opm_out,
    mult_proj,
    mult_gate,
    mult_out,
    att_proj,
    att_bias,
    att_out,
    pair_up,
    pair_down,
    single_cot,
    pair_cot,
):
    gains_s = widen(single_gains)
    gains_p = widen(pair_gains)
    gains_m = widen(mult_gains)
    proj_s = widen(single_proj)
    bias_sw = widen(single_bias)
    up_s = widen(single_up)
    down_s = widen(single_down)
    proj_o = widen(opm_proj)
    outer_w = widen(opm_out)
    proj_m = widen(mult_proj)
    gate_m = widen(mult_gate)
    out_m = widen(mult_out)
    proj_a = widen(att_proj)
    bias_a = widen(att_bias)
    out_a = widen(att_out)
    up_p = widen(pair_up)
    down_p = widen(pair_down)
    mask_all = widen(residue_mask[0])
    shard_rows = pair_rep.shape[1]
    first_row = lax.axis_index("rows") * shard_rows
    mask_own = lax.dynamic_slice_in_dim(mask_all, first_row, shard_rows, 0)
    key_bias = (mask_all - 1.0) * MASKED
    pair_mask = mask_own[:, None] * mask_all[None, :]
    single_own = widen(single_rep[0])
    pair_own = widen(pair_rep[0])

    def front_single(
        single_in, pair_in, gain_s, gain_z, proj_query, proj_key, proj_value, proj_gate, bias_w
    ):
        normed = norm_rows(single_in, gain_s)
        pair_normed = norm_rows(pair_in, gain_z)
        return (
            contract("rs,st->rt", normed, proj_query),
            contract("rs,st->rt", normed, proj_key),
            contract("rs,st->rt", normed, proj_value),
            contract("rs,st->rt", normed, proj_gate),
            contract("rlc,ch->hrl", pair_normed, bias_w),
        )

    def back_single(
        queries,
        key_rows,
        values,
        gate_value,
        row_bias,
        single_in,
        proj_out,
        gain_t,
        weight_up,
        weight_down,
        gain_o,
        left_w,
        right_w,
    ):
        first_sum = single_in + single_attend(
            queries, key_rows, values, gate_value, row_bias, key_bias, proj_out
        )
        hidden = jax.nn.gelu(contract("rs,st->rt", norm_rows(first_sum, gain_t), weight_up))
        second_sum = first_sum + contract("rt,ts->rs", hidden, weight_down)
        outer_in = norm_rows(second_sum, gain_o)
        left_side = contract("rs,sa->ra", outer_in, left_w) * mask_own[:, None]
        right_side = contract("rs,sa->ra", outer_in, right_w) * mask_own[:, None]
        return (second_sum, left_side, right_side)

    def outer_front(left_side, right_all, pair_in, weight_outer, gain_in, weight_four, weight_gate):
        inner = contract("ia,abc->ibc", left_side, weight_outer)
        updated = pair_in + contract("ibc,jb->ijc", inner, right_all)
        left_m, right_m, gate_value = mult_front(
            updated, gain_in, weight_four, weight_gate, pair_mask
        )
        return (updated, left_m, right_m, gate_value)

    def middle_mult(
        pair_in, product, gate_value, gain_out, weight_out, gain_in, weight_four, weight_gate
    ):
        updated = mult_back(pair_in, product, gate_value, gain_out, weight_out)
        left_m, right_m, gate_next = mult_front(
            updated, gain_in, weight_four, weight_gate, pair_mask
        )
        return (updated, left_m, right_m, gate_next)

    def start_front_general(pair_in, product, gate_value, gain_out, weight_out, gain_start, bias_w):
        updated = mult_back(pair_in, product, gate_value, gain_out, weight_out)
        normed = norm_rows(updated, gain_start)
        return (updated, normed, contract("rlc,ch->hrl", normed, bias_w))

    def start_core(pair_in, normed, bias_all, weight_four, weight_out, gain_end):
        updated = pair_in + tri_attend(normed, bias_all, weight_four, weight_out, key_bias)
        return (updated, norm_rows(updated, gain_end))

    def end_bias(turned, bias_w):
        return contract("rlc,ch->hrl", turned, bias_w)

    def end_core(turned, bias_all, weight_four, weight_out):
        return tri_attend(turned, bias_all, weight_four, weight_out, key_bias)

    def final_pair(pair_in, update, gain_vec, weight_up, weight_down):
        summed = pair_in + update
        hidden = jax.nn.gelu(contract("rlc,cd->rld", norm_rows(summed, gain_vec), weight_up))
        return summed + contract("rld,dc->rlc", hidden, weight_down)

    outs_one, back_one = jax.vjp(
        front_single,
        single_own,
        pair_own,
        gains_s[0],
        gains_p[0],
        proj_s[0],
        proj_s[1],
        proj_s[2],
        proj_s[3],
        bias_sw,
    )
    queries, keys_own, values_own, gate_single, row_bias = outs_one
    keys_all, values_all = (
        lax.all_gather(narrow(keys_own), "rows", axis=0, tiled=True),
        lax.all_gather(narrow(values_own), "rows", axis=0, tiled=True),
    )
    outs_two, back_two = jax.vjp(
        back_single,
        queries,
        widen(keys_all),
        widen(values_all),
        gate_single,
        row_bias,
        single_own,
        proj_s[4],
        gains_s[1],
        up_s,
        down_s,
        gains_s[2],
        proj_o[0],
        proj_o[1],
    )
    single_next, left_outer, right_outer = outs_two
    right_all = widen(lax.all_gather(narrow(right_outer), "rows", axis=0, tiled=True))
    outs_three, back_three = jax.vjp(
        outer_front,
        rounded(left_outer),
        right_all,
        pair_own,
        outer_w,
        gains_p[1],
        proj_m[0],
        gate_m[0],
    )
    pair_one, left_first, right_first, gate_first = outs_three
    chan_left, chan_right = to_channels((narrow(left_first), narrow(right_first)))
    product_one = outgoing_forward(chan_left, chan_right)
    rows_one = widen(to_rows(narrow(product_one)))
    outs_five, back_five = jax.vjp(
        middle_mult,
        pair_one,
        rows_one,
        gate_first,
        gains_m[0],
        out_m[0],
        gains_p[2],
        proj_m[1],
        gate_m[1],
    )
    pair_two, left_second, right_second, gate_second = outs_five
    chan_left_two, chan_right_two = to_channels((narrow(left_second), narrow(right_second)))
    product_two = incoming_forward(chan_left_two, chan_right_two)
    rows_two = widen(to_rows(narrow(product_two)))
    outs_seven, back_seven = jax.vjp(
        start_front_general, pair_two, rows_two, gate_second, gains_m[1], out_m[1], gains_p[3], bias_a[0]
    )
    pair_three, normed_start, bias_start = outs_seven
    bias_start_all = widen(gather_bias(narrow(bias_start)))
    outs_eight, back_eight = jax.vjp(
        start_core, pair_three, normed_start, bias_start_all, proj_a[0], out_a[0], gains_p[4]
    )
    pair_four, normed_end = outs_eight
    turned = widen(turn_cols(narrow(normed_end)))
    bias_end, back_nine = jax.vjp(end_bias, turned, bias_a[1])
    bias_end_all = widen(gather_bias(narrow(bias_end)))
    update_turned, back_ten = jax.vjp(end_core, turned, bias_end_all, proj_a[1], out_a[1])
    update = widen(turn_rows(narrow(update_turned)))
    pair_six, back_eleven = jax.vjp(final_pair, pair_four, update, gains_p[5], up_p, down_p)
    grad_four, grad_update, g_pg5, g_pu, g_pd = back_eleven(widen(pair_cot[0]))
    g_pg5, g_pu, g_pd = (g_pg5, g_pu, g_pd)
    grad_turned_update = widen(turn_cols(narrow(grad_update)))
    grad_turned_a, grad_bias_end_all, g_ap1, g_ao1 = back_ten(grad_turned_update)
    g_ap1, g_ao1 = (g_ap1, g_ao1)
    grad_bias_end = rounded(scatter_bias(grad_bias_end_all))
    grad_turned_b, g_ab1 = back_nine(grad_bias_end)
    grad_normed_end = widen(turn_rows(narrow(grad_turned_a + grad_turned_b)))
    grad_three, grad_normed_start, grad_bias_start_all, g_ap0, g_ao0, g_pg4 = back_eight(
        (grad_four, grad_normed_end)
    )
    g_ap0, g_ao0, g_pg4 = (g_ap0, g_ao0, g_pg4)
    grad_bias_start = rounded(scatter_bias(grad_bias_start_all))
    grad_two, grad_rows_two, grad_gate_second, g_mg1, g_mo1, g_pg3, g_ab0 = back_seven(
        (grad_three, grad_normed_start, grad_bias_start)
    )
    g_mg1, g_mo1, g_pg3, g_ab0 = (g_mg1, g_mo1, g_pg3, g_ab0)
    grad_chan_left_two, grad_chan_right_two = incoming_backward(
        chan_left_two, chan_right_two, to_channels(narrow(grad_rows_two))
    )
    grad_left_second, grad_right_second = to_rows(
        (narrow(grad_chan_left_two), narrow(grad_chan_right_two))
    )
    grad_one, grad_rows_one, grad_gate_first, g_mg0, g_mo0, g_pg2, g_mp1, g_mgt1 = back_five(
        (grad_two, widen(grad_left_second), widen(grad_right_second), grad_gate_second)
    )
    g_mg0, g_mo0, g_pg2, g_mp1, g_mgt1 = (g_mg0, g_mo0, g_pg2, g_mp1, g_mgt1)
    grad_chan_left, grad_chan_right = outgoing_backward(
        chan_left, chan_right, to_channels(narrow(grad_rows_one))
    )
    grad_left_first, grad_right_first = to_rows((narrow(grad_chan_left), narrow(grad_chan_right)))
    grad_left_outer, grad_right_all, grad_pair_a, g_oo, g_pg1, g_mp0, g_mgt0 = back_three(
        (grad_one, widen(grad_left_first), widen(grad_right_first), grad_gate_first)
    )
    g_oo, g_pg1, g_mp0, g_mgt0 = (g_oo, g_pg1, g_mp0, g_mgt0)
    grad_right_outer = rounded(
        lax.psum_scatter(grad_right_all, "rows", scatter_dimension=0, tiled=True)
    )
    two_grads = back_two((widen(single_cot[0]), rounded(grad_left_outer), grad_right_outer))
    grad_query, grad_keys_all, grad_values_all, grad_gate_single, grad_row_bias, grad_single_a = (
        two_grads[:6]
    )
    g_sp4, g_sg1, g_su, g_sd, g_sg2, g_op0, g_op1 = tuple(two_grads[6:])
    grad_keys, grad_values = (
        lax.psum_scatter(grad_keys_all, "rows", scatter_dimension=0, tiled=True),
        lax.psum_scatter(grad_values_all, "rows", scatter_dimension=0, tiled=True),
    )
    grad_single_b, grad_pair_b, g_sg0, g_pg0, g_sp0, g_sp1, g_sp2, g_sp3, g_sb = back_one(
        (grad_query, rounded(grad_keys), rounded(grad_values), grad_gate_single, grad_row_bias)
    )
    g_sg0, g_pg0, g_sp0, g_sp1, g_sp2, g_sp3, g_sb = (
        g_sg0,
        g_pg0,
        g_sp0,
        g_sp1,
        g_sp2,
        g_sp3,
        g_sb,
    )
    weight_totals = (
        jnp.stack([g_sg0, g_sg1, g_sg2]),
        jnp.stack([g_pg0, g_pg1, g_pg2, g_pg3, g_pg4, g_pg5]),
        jnp.stack([g_mg0, g_mg1]),
        jnp.stack([g_sp0, g_sp1, g_sp2, g_sp3, g_sp4]),
        g_sb,
        g_su,
        g_sd,
        jnp.stack([g_op0, g_op1]),
        g_oo,
        jnp.stack([g_mp0, g_mp1]),
        jnp.stack([g_mgt0, g_mgt1]),
        jnp.stack([g_mo0, g_mo1]),
        jnp.stack([g_ap0, g_ap1]),
        jnp.stack([g_ab0, g_ab1]),
        jnp.stack([g_ao0, g_ao1]),
        g_pu,
        g_pd,
    )
    weight_totals = lax.psum(
        (
            weight_totals[0],
            weight_totals[1],
            weight_totals[2],
            weight_totals[3],
            weight_totals[4],
            weight_totals[5],
            weight_totals[6],
            weight_totals[7],
            weight_totals[8],
            weight_totals[9],
            weight_totals[10],
            weight_totals[11],
            weight_totals[12],
            weight_totals[13],
            weight_totals[14],
            weight_totals[15],
            weight_totals[16],
        ),
        ("grp", "rows"),
    )
    return (
        narrow(single_next)[None],
        narrow(pair_six)[None],
        (grad_single_a + grad_single_b)[None],
        (grad_pair_a + grad_pair_b)[None],
    ) + tuple(weight_totals)


def pad_rows(x, count):
    return jnp.concatenate([x, jnp.zeros((count - x.shape[0],) + x.shape[1:], x.dtype)], 0)


def fast_local(square, row_count):
    n = row_count
    rows = L // n
    part = L * rows // n
    crops = 4
    total = crops * n

    def home(g, r):
        if square and (r // 2) // 2 != g % 2:
            g, r = g ^ 1, ((r // 2) ^ 2) * 2 + r % 2
        return g * n + r

    groups = [[home(g, r) for r in range(n)] for g in range(crops)]

    def swap(x):
        if not square:
            return x
        return lax.ppermute(x, AX, [(g * n + r, home(g, r)) for g in range(crops) for r in range(n)])

    def exchange(x):
        if square:
            return lax.all_to_all(x, AX, 0, 0, tiled=True, axis_index_groups=groups)
        return lax.all_to_all(x, "rows", 0, 0, tiled=True)

    def to_all(copies):
        return lax.all_to_all(copies, AX, 0, 0, tiled=True)

    chips = total // 2
    same_core = [[g * n + z * 2 + c for g in range(crops) for z in range(n // 2)] for c in range(2)]
    members = [sorted(set(d // 2 for d in group)) for group in groups]

    def other_core(x):
        return lax.ppermute(x, "rows", [(i, i ^ 1) for i in range(n)])

    def to_chips(copies):
        return lax.all_to_all(copies, AX, 0, 0, tiled=True, axis_index_groups=same_core)

    def local(
        single_rep, pair_rep, residue_mask, single_gains, pair_gains, mult_gains, single_proj,
        single_bias, single_up, single_down, opm_proj, opm_out, mult_proj, mult_gate, mult_out,
        att_proj, att_bias, att_out, pair_up, pair_down, single_cot, pair_cot,
    ):
        grp, row = lax.axis_index("grp"), lax.axis_index("rows")
        crop, block = grp, row
        if square:
            moved = (row // 4) != grp % 2
            crop = jnp.where(moved, grp ^ 1, grp)
            block = jnp.where(moved, row ^ 4, row)
        where = jnp.stack([crop, block, grp, row]).astype(jnp.int32)
        single, width = single_rep[0], single_rep.shape[2]
        gathered = lax.all_to_all(
            jnp.broadcast_to(single, (n,) + single.shape), "rows", 0, 0, tiled=True
        )
        pair = swap(pair_rep[0])
        cot = swap(pair_cot[0])
        m5t, m5, mot, mof, a4t, a4, aot, abt, upt, up, dnt, sbt = prep_weights(
            pair_gains, mult_gains, mult_proj, mult_gate, mult_out, att_proj, att_bias, att_out,
            pair_up, pair_down, single_bias,
        )
        opm = opm_proj.shape[2]
        outer = jnp.swapaxes(opm_proj, 0, 1).reshape(width, 2 * opm)
        outer = jnp.pad(outer, ((0, 0), (0, L - 2 * opm)))
        outer_w = jnp.swapaxes(opm_out, 0, 1)
        mask_row = f32(residue_mask)
        mine, mask_col = pack(rows, single, single_cot[0], pair_rep[0], mask_row, sbt, where)
        single_out, lr = single_own(
            n, rows, total, gathered, mine, mask_col, single_gains, single_proj, single_up,
            single_down, outer,
        )
        lr = to_all(lr)

        z1, ab1, pmask, key_row, inner, lrt, left_own = front(
            n, rows, where, lr, pair, outer_w, m5t, deps=(cot,)
        )
        ab1 = exchange(ab1)
        p1 = exchange(channel_product(n, rows, True, ab1)).reshape(C * rows, L)
        z2, ab2 = middle(n, rows, z1, p1, mot, pmask, m5t)
        ab2 = exchange(ab2)
        p2 = exchange(channel_product(n, rows, False, ab2)).reshape(C * rows, L)
        z3, tb = start_front(n, rows, z2, p2, m5t, mot, abt)
        tb_all = exchange(tb)
        cot = exchange(jnp.transpose(cot.reshape(rows, n, rows, C), (1, 2, 0, 3)))
        cot = jnp.swapaxes(cot, 0, 1).reshape(rows, L, C)
        z4, turn = start_attention(n, rows, z3, tb_all, key_row, a4t, aot, abt, deps=(cot,))
        turn = exchange(turn)
        copies = to_chips(copies_of(mine, chips, (turn,)))
        others = other_core(copies)

        pout, back, m_up, m_dn, m_a41, m_ao1 = end_both(
            n, rows, turn, cot, key_row, a4t, a4, aot, att_out, upt, up, dnt, pair_down
        )
        back = exchange(back)
        pout = exchange(pout).reshape(n, rows, rows, C)
        pair_six = swap(jnp.swapaxes(pout, 0, 1).reshape(rows, L, C))

        dz4, dxs, dtb, m_a40, m_ao0, m_ab1 = start_back(
            n, rows, z3, z4, back, tb_all, key_row, a4t, a4, att_out, abt, deps=(copies, others)
        )
        dtb = exchange(dtb)
        dz3, dgp2, dp2, m_ab0, m_mo1 = third_back(
            n, rows, z3, dz4, dxs, dtb, abt, z2, p2, m5t, mot, mof, deps=(pout,)
        )
        dp2 = exchange(dp2.reshape(n, part, L))
        dab2 = channel_product_back(n, rows, False, ab2, dp2)
        kept = single_every(
            n, rows, where, copies, others, single_gains, single_proj, single_up, single_down,
            deps=(dab2,),
        )
        dab2 = exchange(dab2)
        dz2, dgp1, dp1, m_m51, m_mo0 = second_back(
            n, rows, z2, dz3, dgp2, dab2, pmask, m5t, m5, z1, p1, mot, mof, deps=(pair_six, kept[0])
        )
        dp1 = exchange(dp1.reshape(n, part, L))
        dab1 = exchange(channel_product_back(n, rows, True, ab1, dp1))
        dz1, ends, m_oo, m_m50 = first_back(
            n, rows, chips, where, z1, dz2, dgp1, dab1, pmask, m5t, m5, inner, lrt, left_own,
            outer_w,
        )
        ends = to_chips(ends)
        others_ends = other_core(ends)
        dz1 = swap(copies_of(dz1, 1, (others_ends,))[0])
        names = "up dn a41 ao1 a40 ao0 m51 mo1 mo0 m50 oo ab1 ab0".split()
        sums = [
            m_up, m_dn, m_a41, m_ao1, m_a40, m_ao0, m_m51, m_mo1, m_mo0, m_m50, m_oo, m_ab1, m_ab0,
        ]
        places, at = {}, 0
        for name, m in zip(names, sums):
            places[name] = at
            at += m.shape[0]
        half = -(-at // (total * 16)) * total * 8
        near, far = collect(where, sums, half, (ends, others_ends))
        near = b16(near + f32(other_core(far)))
        near = to_chips(near.reshape(chips, half // chips, C))
        ys, g_sg, d_own, drb, m_op = single_back(
            members, rows, where, ends, others_ends, kept, single_gains, single_proj,
            single_up, single_down, outer,
        )
        pair_grad, m_sb = last_back(rows, pair_rep[0], drb, dz1, sbt)
        m_sb = to_all(copies_of(m_sb, total, ()))
        g_sp, g_su, g_sd = weight_grads(kept[2], ys, width, single_up.shape[1])
        g_op = jnp.swapaxes(m_op[:, : 2 * opm].reshape(width, 2, opm), 0, 1)

        near = to_chips(sum_copies(near, chips, (drb,))).reshape(half, C)
        grads = finish(
            where, near, other_core(near), m_sb, pair_gains, mult_gains, mult_proj, mult_gate,
            mult_out, att_proj, att_bias, pair_up, single_bias, places, half, opm, total,
            (g_sd, g_su, g_sp),
        )
        g_pg, g_mg, g_sb, g_oo, g_mp, g_mgt, g_mo, g_ap, g_ab, g_ao, g_pu, g_pd = grads
        return (
            single_out[None],
            pair_six[None],
            d_own[None],
            pair_grad[None],
            g_sg,
            g_pg,
            g_mg,
            g_sp,
            g_sb,
            g_su,
            g_sd,
            g_op,
            g_oo,
            g_mp,
            g_mgt,
            g_mo,
            g_ap,
            g_ab,
            g_ao,
            g_pu,
            g_pd,
        )

    return local


def solution(mesh):
    groups_of, n = mesh.shape["grp"], mesh.shape["rows"]
    whole = P()
    in_specs = (
        (P("grp", "rows", None), P("grp", "rows", None, None), P("grp", None))
        + (whole,) * 17
        + (P("grp", "rows", None), P("grp", "rows", None, None))
    )
    out_specs = (
        P("grp", "rows", None),
        P("grp", "rows", None, None),
        P("grp", "rows", None),
        P("grp", "rows", None, None),
    ) + (whole,) * 17
    if L % n == 0 and (L // n) % 16 == 0:
        body = fast_local((groups_of, n) == (4, 8), n)
    else:
        body = general_local
    return jax.shard_map(body, mesh=mesh, in_specs=in_specs, out_specs=out_specs, check_vma=False)
```

profile of v0, /device:TPU:0, one launch (start us, length us, event | category | flops | bytes accessed | tf_op | source)
XLA Modules:
  0.0 515.9 jit_solution(6331142643060741644)
XLA Ops:
  0.7 1.4 broadcast_in_dim.15
  2.0 6.3 %all-to-all-start = ((bf16[8,16,512]{2,1,0:T(8,128)(2,1)}), bf16[8,16,512]{2,1,0:T(8,128)(2,1)S(1)}, u32[]{:S(2)}, u32[]{:S(2)}) async-start(bf16[8,16,512]{2,1,0:T(8,128)(2,1)} %broadcast_in_dim.15), calls=%async_computation | async-start | bytes 262144 | tf_op jit(solution)/shard_map/all_to_all | solution.py:1754
  8.4 1.7 collective-permute-start
  10.1 1.7 collective-permute-start.1
  11.7 1.4 copy.66.refs_10_.refs_12_
  13.1 1.4 copy.65.refs_6_.refs_10_
  14.5 3.0 shard_map.373
  18.5 3.0 shard_map.374
  21.5 7.0 %shard_map.375 = (bf16[16,512]{1,0:T(8,128)(2,1)}, bf16[32,16,128]{2,1,0:T(8,128)(2,1)}) custom-call(bf16[8,16,512]{2,1,0:T(8,128)(2,1)S(1)} %all-to-all-done.refs_0_, bf16[64,512]{1,0:T(8,128)(2,1)S(1)} %get-tuple-element.107.refs_1_.refs_0_, f32[16,128]{1,0:T(8,128)S(1)} %get-tuple-element.108.refs_2_, bf16[3,512]{1,0:T(4,128)(2,1)} %refs_11_.2, ...), custom_call_target="tpu_custom_call" | custom-call | flops 6000000000 | bytes 7154688 | tf_op jit(solution)/shard_map/pallas_call | solution.py:124
  28.5 9.5 %all-to-all-start.1 = ((bf16[32,16,128]{2,1,0:T(8,128)(2,1)}), bf16[32,16,128]{2,1,0:T(8,128)(2,1)S(1)}, u32[]{:S(2)}, u32[]{:S(2)}) async-start(bf16[32,16,128]{2,1,0:T(8,128)(2,1)} %get-tuple-element.110), calls=%async_computation.1 | async-start | bytes 262144 | tf_op jit(solution)/shard_map/all_to_all | solution.py:1729
  38.8 24.9 %all-to-all-done.1.refs_1_ = bf16[32,16,128]{2,1,0:T(8,128)(2,1)S(1)} async-done(((bf16[32,16,128]{2,1,0:T(8,128)(2,1)}), bf16[32,16,128]{2,1,0:T(8,128)(2,1)S(1)}, u32[]{:S(2)}, u32[]{:S(2)}) %all-to-all-start.1) | async-done | bytes 131104 | tf_op jit(solution)/shard_map/all_to_all | solution.py:1729
  64.5 6.8 %shard_map.376 = (f32[128,2048]{1,0:T(8,128)}, bf16[8,512,128]{2,1,0:T(8,128)(2,1)S(1)}, f32[16,128]{1,0:T(8,128)}, f32[1,128]{1,0:T(1,128)}, f32[512,128]{1,0:T...) custom-call(s32[4]{0:T(128)S(1)} %pad_add_fusion.refs_5_.refs_0_, bf16[32,16,128]{2,1,0:T(8,128)(2,1)S(1)} %all-to-all-done.1.refs_1_, ...), custom_call_target="tpu_custom_call" | custom-call | flops 5000000000 | bytes 1245200 | tf_op jit(solution)/shard_map/pallas_call | solution.py:124
  71.3 18.5 %all_to_all.105.refs_0_ = bf16[8,512,128]{2,1,0:T(8,128)(2,1)} all-to-all(bf16[8,512,128]{2,1,0:T(8,128)(2,1)S(1)} %get-tuple-element.113), channel_id=1, replica_groups={{0,1,2,3,8,9,10,11},{4,5,6,7,12,13,14,15},{16,17,18,19,24,25,26,27},{20..., dimensions={0} | all-to-all | bytes 2097152 | tf_op jit(solution)/shard_map/all_to_all | solution.py:1725
  89.8 1.7 shard_map.377
  91.5 12.8 %all_to_all.106 = bf16[8,256,128]{2,1,0:T(8,128)(2,1)} all-to-all(bf16[8,256,128]{2,1,0:T(8,128)(2,1)S(1)} %shard_map.377), channel_id=1, replica_groups={{0,1,2,3,8,9,10,11},{4,5,6,7,12,13,14,15},{16,17,18,19,24,25,26,27},{20..., dimensions={0} | all-to-all | bytes 1048576 | tf_op jit(solution)/shard_map/all_to_all | solution.py:1725
  104.4 6.3 %shard_map.378 = (f32[128,2048]{1,0:T(8,128)}, bf16[8,512,128]{2,1,0:T(8,128)(2,1)S(1)}) custom-call(f32[128,2048]{1,0:T(8,128)} %get-tuple-element.112.refs_0_.refs_7_.refs_1_, bf16[2048,128]{1,0:T(8,128)(2,1)} %bitcast.51, bf16[2,128,128]{2,1,0:T(8,128)(2,1)} %get-tuple-element.114.refs_2_.refs_3_.refs_8_.refs_9_, ...), custom_call_target="tpu_custom_call" | custom-call | flops 4000000000 | bytes 1974272 | tf_op jit(solution)/shard_map/pallas_call | solution.py:124
  110.6 18.5 %all_to_all.107.refs_0_ = bf16[8,512,128]{2,1,0:T(8,128)(2,1)} all-to-all(bf16[8,512,128]{2,1,0:T(8,128)(2,1)S(1)} %get-tuple-element.117), channel_id=1, replica_groups={{0,1,2,3,8,9,10,11},{4,5,6,7,12,13,14,15},{16,17,18,19,24,25,26,27},{20..., dimensions={0} | all-to-all | bytes 2097152 | tf_op jit(solution)/shard_map/all_to_all | solution.py:1725
  129.1 2.4 shard_map.379
  131.5 3.5 all-to-all-start.5
  135.0 1.1 copy.79
  136.1 8.5 %all-to-all-done.5 = bf16[8,256,128]{2,1,0:T(8,128)(2,1)S(1)} async-done(((bf16[8,256,128]{2,1,0:T(8,128)(2,1)}), bf16[8,256,128]{2,1,0:T(8,128)(2,1)S(1)}, u32[]{:S(2)}, u32[]{:S(2)}) %all-to-all-start.5) | async-done | bytes 524320 | tf_op jit(solution)/shard_map/all_to_all | solution.py:1725
  144.7 3.5 all-to-all-start.7
  148.2 7.3 %shard_map.380 = (f32[128,2048]{1,0:T(8,128)}, bf16[8,64,128]{2,1,0:T(8,128)(2,1)}) custom-call(f32[128,2048]{1,0:T(8,128)} %get-tuple-element.116.refs_0_.refs_5_, bf16[2048,128]{1,0:T(8,128)(2,1)} %bitcast.53, bf16[2,640,128]{2,1,0:T(8,128)(2,1)} %get-tuple-element.111.refs_4_.refs_2_.refs_7_.refs_5_.refs_6_, ...), custom_call_target="tpu_custom_call" | custom-call | flops 4000000000 | bytes 1974272 | tf_op jit(solution)/shard_map/pallas_call | solution.py:124
  155.5 2.4 all-to-all-done.7
  157.9 3.4 all-to-all-start.6
  161.3 5.4 %all-to-all-done.6.refs_1_.refs_3_ = bf16[8,64,128]{2,1,0:T(8,128)(2,1)S(1)} async-done(((bf16[8,64,128]{2,1,0:T(8,128)(2,1)}), bf16[8,64,128]{2,1,0:T(8,128)(2,1)S(1)}, u32[]{:S(2)}, u32[]{:S(2)}) %all-to-all-start.6) | async-done | bytes 131104 | tf_op jit(solution)/shard_map/all_to_all | solution.py:1725
  167.4 13.1 %shard_map.381 = (f32[128,2048]{1,0:T(8,128)}, bf16[8,320,128]{2,1,0:T(8,128)(2,1)S(1)}) custom-call(f32[128,2048]{1,0:T(8,128)} %get-tuple-element.119.refs_0_, bf16[8,64,128]{2,1,0:T(8,128)(2,1)} %copy-done.24, f32[1,128]{1,0:T(1,128)} %get-tuple-element.121.refs_2_.refs_4_, bf16[2,512,128]{2,1,0:T(8,128)(2,1)} %get-tuple-element.122.refs_3_.refs_5_, ...), custom_call_target="tpu_custom_call" | custom-call | flops 12000000000 | bytes 1516032 | tf_op jit(solution)/shard_map/pallas_call | solution.py:124
  180.5 13.5 %all_to_all.108.refs_0_.refs_1_ = bf16[8,320,128]{2,1,0:T(8,128)(2,1)S(1)} all-to-all(bf16[8,320,128]{2,1,0:T(8,128)(2,1)S(1)} %get-tuple-element.124), channel_id=1, replica_groups={{0,1,2,3,8,9,10,11},{4,5,6,7,12,13,14,15},{16,17,18,19,24,25,26,27},{20..., dimensions={0} | all-to-all | bytes 1310720 | tf_op jit(solution)/shard_map/all_to_all | solution.py:1725
  194.0 1.1 shard_map.383
  195.1 4.3 all-to-all-start.11
  199.4 37.2 %shard_map.382 = (bf16[8,256,128]{2,1,0:T(8,128)(2,1)}, bf16[8,320,128]{2,1,0:T(8,128)(2,1)}, f32[512,128]{1,0:T(8,128)}, f32[512,128]{1,0:T(8,128)}, f32[512,128]{1,0:T(8,128)}, /*index=5*/f32[128,128]{1,0:T(8,128)}) custom-call(bf16[8,320,128]{2,1,0:T(8,128)(2,1)S(1)} %all_to_all.108.refs_0_.refs_1_, bf16[16,128,128]{2,1,0:T(8,128)(2,1)} %bitcast.46, ...), custom_call_target="tpu_custom_call" | custom-call | flops 35999997952 | bytes 2359808 | tf_op jit(solution)/shard_map/pallas_call | solution.py:124
  236.7 4.2 all-to-all-start.10
  241.4 10.6 %all-to-all-done.10.refs_2_ = bf16[8,320,128]{2,1,0:T(8,128)(2,1)S(1)} async-done(((bf16[8,320,128]{2,1,0:T(8,128)(2,1)}), bf16[8,320,128]{2,1,0:T(8,128)(2,1)S(1)}, u32[]{:S(2)}, u32[]{:S(2)}) %all-to-all-start.10) | async-done | bytes 655392 | tf_op jit(solution)/shard_map/all_to_all | solution.py:1725
  252.0 3.5 all-to-all-start.9
  255.6 21.5 %shard_map.384 = (f32[128,2048]{1,0:T(8,128)}, f32[128,2048]{1,0:T(8,128)}, bf16[8,64,128]{2,1,0:T(8,128)(2,1)S(1)}, f32[512,128]{1,0:T(8,128)}, f32[128,128]{1,0:T(8,128)}, /*index=5*/f32[16,128]{1,0:T(8,128)}) custom-call(f32[128,2048]{1,0:T(8,128)} %get-tuple-element.119.refs_0_, f32[128,2048]{1,0:T(8,128)} %get-tuple-element.130.refs_1_, ...), custom_call_target="tpu_custom_call" | custom-call | flops 20000000000 | bytes 3482112 | tf_op jit(solution)/shard_map/pallas_call | solution.py:124
  277.1 9.4 %all_to_all.109.refs_3_ = bf16[8,64,128]{2,1,0:T(8,128)(2,1)S(1)} all-to-all(bf16[8,64,128]{2,1,0:T(8,128)(2,1)S(1)} %get-tuple-element.134), channel_id=1, replica_groups={{0,1,2,3,8,9,10,11},{4,5,6,7,12,13,14,15},{16,17,18,19,24,25,26,27},{20..., dimensions={0} | all-to-all | bytes 262144 | tf_op jit(solution)/shard_map/all_to_all | solution.py:1725
  286.6 8.2 %shard_map.385 = (f32[128,2048]{1,0:T(8,128)}, bf16[128,2048]{1,0:T(8,128)(2,1)}, bf16[2048,128]{1,0:T(8,128)(2,1)S(1)}, f32[16,128]{1,0:T(8,128)}, f32[128,128]{1,0:T(8,128)}) custom-call(f32[128,2048]{1,0:T(8,128)} %get-tuple-element.119.refs_0_, f32[128,2048]{1,0:T(8,128)} %get-tuple-element.132.refs_1_, f32[128,2048]{1,0:T(8,128)} %get-tuple-element.133.refs_2_, ...), custom_call_target="tpu_custom_call" | custom-call | flops 7000000000 | bytes 5316608 | tf_op jit(solution)/shard_map/pallas_call | solution.py:124
  294.8 12.4 %all_to_all.110.refs_1_ = bf16[8,256,128]{2,1,0:T(8,128)(2,1)S(1)} all-to-all(bf16[8,256,128]{2,1,0:T(8,128)(2,1)S(1)} %bitcast.48), channel_id=1, replica_groups={{0,1,2,3,8,9,10,11},{4,5,6,7,12,13,14,15},{16,17,18,19,24,25,26,27},{20..., dimensions={0} | all-to-all | bytes 1048576 | tf_op jit(solution)/shard_map/all_to_all | solution.py:1725
  307.2 2.8 shard_map.386.refs_7_
  310.0 3.6 all-to-all-start.14
  314.3 20.5 %shard_map.387 = (bf16[512,512]{1,0:T(8,128)(2,1)}, bf16[512,512]{1,0:T(8,128)(2,1)}, bf16[512,3584]{1,0:T(8,128)(2,1)}, bf16[512,1536]{1,0:T(8,128)(2,1)}, bf16...) custom-call(s32[4]{0:T(128)S(1)} %pad_add_fusion.refs_5_.refs_0_, ...), custom_call_target="tpu_custom_call" | custom-call | flops 19000000512 | bytes 8915984 | tf_op jit(solution)/shard_map/pallas_call | solution.py:124
  334.9 1.0 copy-done.18
  335.9 11.8 %shard_map.388 = (f32[128,2048]{1,0:T(8,128)}, bf16[128,2048]{1,0:T(8,128)(2,1)}, bf16[2048,128]{1,0:T(8,128)(2,1)S(1)}, f32[640,128]{1,0:T(8,128)}, f32[128,128]{1,0:T(8,128)}) custom-call(f32[128,2048]{1,0:T(8,128)} %get-tuple-element.116.refs_0_.refs_5_, f32[128,2048]{1,0:T(8,128)} %get-tuple-element.136.refs_1_, ...), custom_call_target="tpu_custom_call" | custom-call | flops 11000000512 | bytes 6037504 | tf_op jit(solution)/shard_map/pallas_call | solution.py:124
  347.7 20.5 %all_to_all.111.refs_1_ = bf16[8,256,128]{2,1,0:T(8,128)(2,1)S(1)} all-to-all(bf16[8,256,128]{2,1,0:T(8,128)(2,1)S(1)} %bitcast.47), channel_id=1, replica_groups={{0,1,2,3,8,9,10,11},{4,5,6,7,12,13,14,15},{16,17,18,19,24,25,26,27},{20..., dimensions={0} | all-to-all | bytes 1048576 | tf_op jit(solution)/shard_map/all_to_all | solution.py:1725
  368.2 1.7 shard_map.389
  369.9 17.8 %all_to_all.112.refs_4_ = bf16[8,512,128]{2,1,0:T(8,128)(2,1)S(1)} all-to-all(bf16[8,512,128]{2,1,0:T(8,128)(2,1)S(1)} %shard_map.389), channel_id=1, replica_groups={{0,1,2,3,8,9,10,11},{4,5,6,7,12,13,14,15},{16,17,18,19,24,25,26,27},{20..., dimensions={0} | all-to-all | bytes 2097152 | tf_op jit(solution)/shard_map/all_to_all | solution.py:1725
  387.8 12.7 %shard_map.390 = (bf16[16,128,128]{2,1,0:T(8,128)(2,1)S(1)}, bf16[16,64,128]{2,1,0:T(8,128)(2,1)S(1)}, f32[1024,128]{1,0:T(8,128)}, f32[640,128]{1,0:T(8,128)}) custom-call(s32[4]{0:T(128)S(1)} %pad_add_fusion.refs_5_.refs_0_, f32[128,2048]{1,0:T(8,128)} %get-tuple-element.112.refs_0_.refs_7_.refs_1_, f32[128,2048]{1,0:T(8,128)} %get-tuple-element.141.refs_2_, ...), custom_call_target="tpu_custom_call" | custom-call | flops 11000000512 | bytes 4927504 | tf_op jit(solution)/shard_map/pallas_call | solution.py:124
  400.5 15.3 %all_to_all.113.refs_1_.refs_14_ = bf16[16,64,128]{2,1,0:T(8,128)(2,1)S(1)} all-to-all(bf16[16,64,128]{2,1,0:T(8,128)(2,1)S(1)} %get-tuple-element.147), channel_id=1, replica_groups={{0,2,4,6,8,10,12,14,16,18,20,22,24,26,28,30},{1,3,5,7,9,11,13,15,17,19,..., dimensions={0} | all-to-all | bytes 524288 | tf_op jit(solution)/shard_map/all_to_all | solution.py:1739
  415.7 1.5 collective-permute-done.4.refs_2_.refs_1_.refs_15_
  421.2 1.2 collective-permute-done.6
  423.4 4.3 all-to-all-start.18
  427.7 23.5 %shard_map.391 = (bf16[512,5120]{1,0:T(8,128)(2,1)}, f32[3,512]{1,0:T(4,128)}, f32[16,512]{1,0:T(8,128)}, f32[128,128]{1,0:T(8,128)}, f32[512,128]{1,0:T(8,128)}) custom-call(s32[4]{0:T(128)S(1)} %pad_add_fusion.refs_5_.refs_0_, bf16[16,64,128]{2,1,0:T(8,128)(2,1)S(1)} %all_to_all.113.refs_1_.refs_14_, ...), custom_call_target="tpu_custom_call" | custom-call | flops 22000001024 | bytes 16387088 | tf_op jit(solution)/shard_map/pallas_call | solution.py:124
  451.2 6.8 %all-to-all-done.18.refs_0_ = bf16[16,160,128]{2,1,0:T(8,128)(2,1)S(1)} async-done(((bf16[16,160,128]{2,1,0:T(8,128)(2,1)}), bf16[16,160,128]{2,1,0:T(8,128)(2,1)S(1)}, u32[]{:S(2)}, u32[]{:S(2)}) %all-to-all-start.18) | async-done | bytes 655392 | tf_op jit(solution)/shard_map/all_to_all | solution.py:1739
  459.8 7.6 %all-to-all-start.19 = ((bf16[16,160,128]{2,1,0:T(8,128)(2,1)}), bf16[16,160,128]{2,1,0:T(8,128)(2,1)S(1)}, u32[]{:S(2)}, u32[]{:S(2)}) async-start(bf16[16,160,128]{2,1,0:T(8,128)(2,1)} %shard_map.395), calls=%async_computation.19 | async-start | bytes 1310720 | tf_op jit(solution)/shard_map/all_to_all | solution.py:1739
  467.4 5.2 %shard_map.398.refs_14_ = f32[512,2048]{1,0:T(8,128)} custom-call(bf16[512,3584]{1,0:T(8,128)(2,1)} %get-tuple-element.176.x, bf16[512,5120]{1,0:T(8,128)(2,1)} %get-tuple-element.177.y), custom_call_target="tpu_custom_call" | custom-call | flops 4000000000 | bytes 8388608 | tf_op jit(solution)/shard_map/pallas_call | solution.py:508
  473.4 3.8 shard_map.393
  477.9 8.5 %all-to-all-done.19 = bf16[16,160,128]{2,1,0:T(8,128)(2,1)S(1)} async-done(((bf16[16,160,128]{2,1,0:T(8,128)(2,1)}), bf16[16,160,128]{2,1,0:T(8,128)(2,1)S(1)}, u32[]{:S(2)}, u32[]{:S(2)}) %all-to-all-start.19) | async-done | bytes 655392 | tf_op jit(solution)/shard_map/all_to_all | solution.py:1739
  486.4 2.6 all-to-all-start.20
  489.2 5.1 shard_map.397.refs_13_
  495.1 7.0 %shard_map.399.refs_15_ = f32[5,512,512]{2,1,0:T(8,128)} custom-call(bf16[512,3584]{1,0:T(8,128)(2,1)} %get-tuple-element.176.x, bf16[512,5120]{1,0:T(8,128)(2,1)} %get-tuple-element.177.y), custom_call_target="tpu_custom_call" | custom-call | flops 4000000000 | bytes 10485760 | tf_op jit(solution)/shard_map/pallas_call | solution.py:508
  502.2 2.5 copy-done
  504.7 2.2 copy-done.1
  506.9 2.2 copy-done.2
  509.0 4.3 shard_map.400
  (87 shorter events, 15.8 us)
Async XLA Ops:
  2.0 19.5 %all-to-all-start = ((bf16[8,16,512]{2,1,0:T(8,128)(2,1)}), bf16[8,16,512]{2,1,0:T(8,128)(2,1)S(1)}, u32[]{:S(2)}, u32[]{:S(2)}) async-start(bf16[8,16,512]{2,1,0:T(8,128)(2,1)} %broadcast_in_dim.15), calls=%async_computation | async-start | bytes 262144 | tf_op jit(solution)/shard_map/all_to_all | solution.py:1754
  8.4 55.4 %collective-permute-start = (bf16[16,128,128]{2,1,0:T(8,128)(2,1)}, bf16[16,128,128]{2,1,0:T(8,128)(2,1)S(1)}, u32[]{:S(2)}, u32[]{:S(2)}) collective-permute-start(bf16[16,128,128]{2,1,0:T(8,128)(2,1)} %bitcast.64), channel_id=1, source_target_pairs={{0,0},{1,1},{2,2},{3,3},{4,8},{5,9},{6,10},{7,11},{8,4},{9,5},{10,... | collective-permute-start | bytes 1572872 | tf_op jit(solution)/shard_map/ppermute | solution.py:1721
  10.1 53.7 %collective-permute-start.1 = (bf16[16,128,128]{2,1,0:T(8,128)(2,1)}, bf16[16,128,128]{2,1,0:T(8,128)(2,1)S(1)}, u32[]{:S(2)}, u32[]{:S(2)}) collective-permute-start(bf16[16,128,128]{2,1,0:T(8,128)(2,1)} %bitcast.63), channel_id=1, source_target_pairs={{0,0},{1,1},{2,2},{3,3},{4,8},{5,9},{6,10},{7,11},{8,4},{9,5},{10,... | collective-permute-start | bytes 1572872 | tf_op jit(solution)/shard_map/ppermute | solution.py:1721
  14.5 3.1 copy-start.28
  14.5 3.1 copy-start.25
  21.5 16.5 %copy-start.23 = (bf16[32,32,128]{2,1,0:T(8,128)(2,1)S(1)}, bf16[32,32,128]{2,1,0:T(8,128)(2,1)}, u32[]{:S(2)}) copy-start(bf16[32,32,128]{2,1,0:T(8,128)(2,1)} %param.33) | copy-start | bytes 786436
  28.5 35.2 %all-to-all-start.1 = ((bf16[32,16,128]{2,1,0:T(8,128)(2,1)}), bf16[32,16,128]{2,1,0:T(8,128)(2,1)S(1)}, u32[]{:S(2)}, u32[]{:S(2)}) async-start(bf16[32,16,128]{2,1,0:T(8,128)(2,1)} %get-tuple-element.110), calls=%async_computation.1 | async-start | bytes 262144 | tf_op jit(solution)/shard_map/all_to_all | solution.py:1729
  63.7 0.8 copy-start.26
  131.5 13.2 %all-to-all-start.5 = ((bf16[8,256,128]{2,1,0:T(8,128)(2,1)}), bf16[8,256,128]{2,1,0:T(8,128)(2,1)S(1)}, u32[]{:S(2)}, u32[]{:S(2)}) async-start(bf16[8,256,128]{2,1,0:T(8,128)(2,1)} %shard_map.379), calls=%async_computation.5 | async-start | bytes 1048576 | tf_op jit(solution)/shard_map/all_to_all | solution.py:1725
  144.7 3.5 copy-start.21
  144.7 13.2 %all-to-all-start.7 = ((bf16[8,16,16,128]{3,2,1,0:T(8,128)(2,1)}), bf16[8,16,16,128]{3,2,1,0:T(8,128)(2,1)S(1)}, u32[]{:S(2)}, u32[]{:S(2)}) async-start(bf16[8,16,16,128]{3,2,1,0:T(8,128)(2,1)} %bitcast.36), calls=%async_computation.7 | async-start | bytes 1048576 | tf_op jit(solution)/shard_map/all_to_all | solution.py:1725
  157.9 8.8 %all-to-all-start.6 = ((bf16[8,64,128]{2,1,0:T(8,128)(2,1)}), bf16[8,64,128]{2,1,0:T(8,128)(2,1)S(1)}, u32[]{:S(2)}, u32[]{:S(2)}) async-start(bf16[8,64,128]{2,1,0:T(8,128)(2,1)} %get-tuple-element.120), calls=%async_computation.6 | async-start | bytes 262144 | tf_op jit(solution)/shard_map/all_to_all | solution.py:1725
  161.3 19.2 %copy-start.4 = (bf16[16,8,16,128]{3,2,1,0:T(8,128)(2,1)}, bf16[16,8,16,128]{3,2,1,0:T(8,128)(2,1)S(1)}, u32[]{:S(2)}) copy-start(bf16[16,8,16,128]{3,2,1,0:T(8,128)(2,1)S(1)} %copy.70) | copy-start | bytes 1572868
  166.7 0.7 copy-start.24
  195.1 41.6 %all-to-all-start.11 = ((bf16[16,64,512]{2,1,0:T(8,128)(2,1)}), bf16[16,64,512]{2,1,0:T(8,128)(2,1)S(1)}, u32[]{:S(2)}, u32[]{:S(2)}) async-start(bf16[16,64,512]{2,1,0:T(8,128)(2,1)} %shard_map.383), calls=%async_computation.11 | async-start | bytes 2097152 | tf_op jit(solution)/shard_map/all_to_all | solution.py:1739
  236.7 40.4 %copy-start.3 = (bf16[16,64,512]{2,1,0:T(8,128)(2,1)}, bf16[16,64,512]{2,1,0:T(8,128)(2,1)S(1)}, u32[]{:S(2)}) copy-start(bf16[16,64,512]{2,1,0:T(8,128)(2,1)S(1)} %all-to-all-done.11.refs_9_.refs_1_) | copy-start | bytes 3145732
  236.7 15.4 %all-to-all-start.10 = ((bf16[8,320,128]{2,1,0:T(8,128)(2,1)}), bf16[8,320,128]{2,1,0:T(8,128)(2,1)S(1)}, u32[]{:S(2)}, u32[]{:S(2)}) async-start(bf16[8,320,128]{2,1,0:T(8,128)(2,1)} %get-tuple-element.131), calls=%async_computation.10 | async-start | bytes 1310720 | tf_op jit(solution)/shard_map/all_to_all | solution.py:1725
  240.9 14.7 %collective-permute-start.3 = (bf16[16,64,512]{2,1,0:T(8,128)(2,1)S(1)}, bf16[16,64,512]{2,1,0:T(8,128)(2,1)S(1)}, u32[]{:S(2)}, u32[]{:S(2)}) collective-permute-start(bf16[16,64,512]{2,1,0:T(8,128)(2,1)S(1)} %all-to-all-done.11.refs_9_.refs_1_), channel_id=1, source_target_pairs={{0,1},{1,0},{2,3},{3,2},{4,5},{5,4},{6,7},{7,6},{8,9},{9,8},{10,11... | collective-permute-start | bytes 3145736 | tf_op jit(solution)/shard_map/ppermute | solution.py:1736
  252.0 25.1 %all-to-all-start.9 = ((bf16[8,256,128]{2,1,0:T(8,128)(2,1)}), bf16[8,256,128]{2,1,0:T(8,128)(2,1)S(1)}, u32[]{:S(2)}, u32[]{:S(2)}) async-start(bf16[8,256,128]{2,1,0:T(8,128)(2,1)} %get-tuple-element.129), calls=%async_computation.9 | async-start | bytes 1048576 | tf_op jit(solution)/shard_map/all_to_all | solution.py:1725
  255.6 21.6 %copy-start.5 = (bf16[16,64,512]{2,1,0:T(8,128)(2,1)}, bf16[16,64,512]{2,1,0:T(8,128)(2,1)S(1)}, u32[]{:S(2)}) copy-start(bf16[16,64,512]{2,1,0:T(8,128)(2,1)S(1)} %collective-permute-done.3.refs_10_.refs_2_) | copy-start | bytes 3145732
  310.0 24.9 %all-to-all-start.14 = ((bf16[8,512,128]{2,1,0:T(8,128)(2,1)}), bf16[8,512,128]{2,1,0:T(8,128)(2,1)S(1)}, u32[]{:S(2)}, u32[]{:S(2)}) async-start(bf16[8,512,128]{2,1,0:T(8,128)(2,1)} %shard_map.386.refs_7_), calls=%async_computation.14 | async-start | bytes 2097152 | tf_op jit(solution)/shard_map/all_to_all | solution.py:1725
  313.6 21.2 %collective-permute-start.2 = (bf16[16,128,128]{2,1,0:T(8,128)(2,1)S(1)}, bf16[16,128,128]{2,1,0:T(8,128)(2,1)S(1)}, u32[]{:S(2)}, u32[]{:S(2)}) collective-permute-start(bf16[16,128,128]{2,1,0:T(8,128)(2,1)S(1)} %bitcast.55), channel_id=1, source_target_pairs={{0,0},{1,1},{2,2},{3,3},{4,8},{5,9},{6,10},{7,11},{8,4},{9,5},{10,... | collective-permute-start | bytes 1572872 | tf_op jit(solution)/shard_map/ppermute | solution.py:1721
  334.9 1.0 copy-start.18
  387.7 29.6 %copy-start.7 = (f32[640,128]{1,0:T(8,128)S(1)}, f32[640,128]{1,0:T(8,128)}, u32[]{:S(2)}) copy-start(f32[640,128]{1,0:T(8,128)} %get-tuple-element.166.refs_7_) | copy-start | bytes 983044
  387.7 29.6 %copy-start.9 = (f32[512,128]{1,0:T(8,128)S(1)}, f32[512,128]{1,0:T(8,128)}, u32[]{:S(2)}) copy-start(f32[512,128]{1,0:T(8,128)} %get-tuple-element.160.refs_1_) | copy-start | bytes 786436
  387.7 29.6 %copy-start.10 = (f32[512,128]{1,0:T(8,128)S(1)}, f32[512,128]{1,0:T(8,128)}, u32[]{:S(2)}) copy-start(f32[512,128]{1,0:T(8,128)} %get-tuple-element.161.refs_2_) | copy-start | bytes 786436
  387.7 29.6 %copy-start.11 = (f32[512,128]{1,0:T(8,128)S(1)}, f32[512,128]{1,0:T(8,128)}, u32[]{:S(2)}) copy-start(f32[512,128]{1,0:T(8,128)} %get-tuple-element.162.refs_3_) | copy-start | bytes 786436
  387.7 29.6 %copy-start.12 = (f32[512,128]{1,0:T(8,128)S(1)}, f32[512,128]{1,0:T(8,128)}, u32[]{:S(2)}) copy-start(f32[512,128]{1,0:T(8,128)} %get-tuple-element.164.refs_5_) | copy-start | bytes 786436
  387.7 29.6 %copy-start.14 = (f32[128,128]{1,0:T(8,128)S(1)}, f32[128,128]{1,0:T(8,128)}, u32[]{:S(2)}) copy-start(f32[128,128]{1,0:T(8,128)} %get-tuple-element.163.refs_4_) | copy-start | bytes 196612
  387.7 29.6 %copy-start.15 = (f32[128,128]{1,0:T(8,128)S(1)}, f32[128,128]{1,0:T(8,128)}, u32[]{:S(2)}) copy-start(f32[128,128]{1,0:T(8,128)} %get-tuple-element.165.refs_6_) | copy-start | bytes 196612
  387.7 29.6 %copy-start.16 = (f32[128,128]{1,0:T(8,128)S(1)}, f32[128,128]{1,0:T(8,128)}, u32[]{:S(2)}) copy-start(f32[128,128]{1,0:T(8,128)} %get-tuple-element.167.refs_8_) | copy-start | bytes 196612
  387.7 29.6 %copy-start.17 = (f32[128,128]{1,0:T(8,128)S(1)}, f32[128,128]{1,0:T(8,128)}, u32[]{:S(2)}) copy-start(f32[128,128]{1,0:T(8,128)} %get-tuple-element.168.refs_9_) | copy-start | bytes 196612
  387.7 29.6 %copy-start.19 = (f32[16,128]{1,0:T(8,128)S(1)}, f32[16,128]{1,0:T(8,128)}, u32[]{:S(2)}) copy-start(f32[16,128]{1,0:T(8,128)} %get-tuple-element.171.refs_12_) | copy-start | bytes 24580
  387.8 29.6 %copy-start.20 = (f32[16,128]{1,0:T(8,128)S(1)}, f32[16,128]{1,0:T(8,128)}, u32[]{:S(2)}) copy-start(f32[16,128]{1,0:T(8,128)} %get-tuple-element.172.refs_13_) | copy-start | bytes 24580
  415.7 1.5 collective-permute-start.4
  417.4 1.0 copy-start.6
  418.4 1.0 copy-start.8
  420.3 2.2 collective-permute-start.6
  420.5 52.1 %collective-permute-start.5 = (bf16[16,128,128]{2,1,0:T(8,128)(2,1)S(1)}, bf16[16,128,128]{2,1,0:T(8,128)(2,1)S(1)}, u32[]{:S(2)}, u32[]{:S(2)}) collective-permute-start(bf16[16,128,128]{2,1,0:T(8,128)(2,1)S(1)} %bitcast.49), channel_id=1, source_target_pairs={{0,0},{1,1},{2,2},{3,3},{4,8},{5,9},{6,10},{7,11},{8,4},{9,5},{10,... | collective-permute-start | bytes 1572872 | tf_op jit(solution)/shard_map/ppermute | solution.py:1721
  423.4 34.6 %all-to-all-start.18 = ((bf16[16,160,128]{2,1,0:T(8,128)(2,1)}), bf16[16,160,128]{2,1,0:T(8,128)(2,1)S(1)}, u32[]{:S(2)}, u32[]{:S(2)}) async-start(bf16[16,160,128]{2,1,0:T(8,128)(2,1)} %bitcast.27), calls=%async_computation.18 | async-start | bytes 1310720 | tf_op jit(solution)/shard_map/all_to_all | solution.py:1739
  458.0 0.8 copy-start.13
  459.8 26.7 %all-to-all-start.19 = ((bf16[16,160,128]{2,1,0:T(8,128)(2,1)}), bf16[16,160,128]{2,1,0:T(8,128)(2,1)S(1)}, u32[]{:S(2)}, u32[]{:S(2)}) async-start(bf16[16,160,128]{2,1,0:T(8,128)(2,1)} %shard_map.395), calls=%async_computation.19 | async-start | bytes 1310720 | tf_op jit(solution)/shard_map/all_to_all | solution.py:1739
  472.6 0.8 copy-start.27
  486.4 15.7 %all-to-all-start.20 = ((f32[32,16,128]{2,1,0:T(8,128)}), f32[32,16,128]{2,1,0:T(8,128)S(1)}, u32[]{:S(2)}, u32[]{:S(2)}) async-start(f32[32,16,128]{2,1,0:T(8,128)} %shard_map.396), calls=%async_computation.20 | async-start | bytes 524288 | tf_op jit(solution)/shard_map/all_to_all | solution.py:1729
  489.0 5.3 %copy-start.22 = (f32[512,128]{1,0:T(8,128)S(1)}, f32[512,128]{1,0:T(8,128)}, u32[]{:S(2)}) copy-start(f32[512,128]{1,0:T(8,128)} %get-tuple-element.181) | copy-start | bytes 786436
  489.0 13.1 %collective-permute-start.7 = (bf16[2560,128]{1,0:T(8,128)(2,1)S(1)}, bf16[2560,128]{1,0:T(8,128)(2,1)S(1)}, u32[]{:S(2)}, u32[]{:S(2)}) collective-permute-start(bf16[2560,128]{1,0:T(8,128)(2,1)S(1)} %bitcast.39), channel_id=1, source_target_pairs={{0,1},{1,0},{2,3},{3,2},{4,5},{5,4},{6,7},{7,6},{8,9},{9,8},{10,11... | collective-permute-start | bytes 1966088 | tf_op jit(solution)/shard_map/ppermute | solution.py:1736
  502.2 2.5 copy-start
  504.7 2.2 copy-start.1
  506.9 2.2 copy-start.2
where the time goes:
time: 525 us; the launch traced here: 516 us
  Pallas kernels  219 us (42%)
  blocking collectives  139 us (26%)
  waiting for transfers between devices  70.1 us (13%)
  starting transfers between devices  61.9 us (12%)
  local copies, waits for them, and re-layouts  23 us (4%)
    pallas_call x25, Pallas kernels, call(): pl.pallas_call(body, out_shape=[pltpu.HBM(s, d) if k in far else jax.Shap...  202 us
    all_to_all x8, blocking collectives, exchange(): return lax.all_to_all(x, AX, 0, 0, tiled=True, axis_index_groups=groups)  123 us
    all_to_all x6, waiting for transfers between devices, exchange(): return lax.all_to_all(x, AX, 0, 0, tiled=True, axis_index_groups=groups)  27.1 us
    all_to_all x2, waiting for transfers between devices, to_all(): return lax.all_to_all(copies, AX, 0, 0, tiled=True)  24.9 us
    all_to_all x6, starting transfers between devices, exchange(): return lax.all_to_all(x, AX, 0, 0, tiled=True, axis_index_groups=groups)  21.6 us
    unnamed x64, local copies, waits for them, and re-layouts  18.8 us
    pallas_call x3, Pallas kernels, run(): pl.pallas_call(kernel, grid=(steps,), out_shape=jax.ShapeDtypeStruct(shap...  17.3 us
    all_to_all x3, starting transfers between devices, to_chips(): lax.all_to_all(copies, AX, 0, 0, tiled=True, axis_index_groups=same_core)  16.3 us
  transfers between devices with their start and end apart: 20, of which 10 were waited for; matrix products, arithmetic and copies ran while one was open for 1% of the time, Pallas kernels for 28%

commit v1 on v0

--- a/solution.py
+++ b/solution.py
@@ -66,8 +66,42 @@
     )
 
 
+U = 2
+
+
 def cols(r):
-    return pl.ds(pl.multiple_of(r * L, L), L)
+    return pl.ds(pl.multiple_of(r * U * L, U * L), U * L)
+
+
+def side(parts):
+    return jnp.concatenate(parts, 1)
+
+
+def lanes(x, u):
+    return x[:, u * L : (u + 1) * L]
+
+
+def get_rows(ref, r, count, rows):
+    return side([ref[pl.ds(r * U + u, count, stride=rows), :] for u in range(U)])
+
+
+def put_rows(ref, r, count, rows, x):
+    for u in range(U):
+        ref[pl.ds(r * U + u, count, stride=rows), :] = lanes(x, u)
+
+
+def put_turned(ref, r, rows, x):
+    for u in range(U):
+        ref[pl.ds(r * U + u, L, stride=rows), :] = lanes(x, u).T
+
+
+def get_turned(ref, r, rows):
+    return side(
+        [
+            f32(ref[:, pl.ds(pl.multiple_of((r * U + u) * rows, rows), rows), :].reshape(L, C)).T
+            for u in range(U)
+        ]
+    )
 
 
 def each_row(count, body):
@@ -75,7 +109,7 @@
         body(r)
         return carry
 
-    lax.fori_loop(0, count, step, 0, unroll=4 if count > 4 else 2)
+    lax.fori_loop(0, count, step, 0, unroll=2)
 
 
 def call(kernel, outs, scratch, args, deps=(), raw=(), late=(), far=(), us=5):
@@ -140,7 +174,7 @@
             pltpu.with_memory_space_constraint(a, pltpu.HBM) if k in raw else a
             for k, a in enumerate(args)
         ],
-        *deps,
+        *[pltpu.with_memory_space_constraint(d, pltpu.HBM) for d in deps],
     )
 
 
@@ -152,11 +186,8 @@
         gpv = f32(gp[...])
         gmv = f32(gm[...])
 
-        def turned(w):
-            shape = (HPAD, w.shape[1])
-            row = lax.broadcasted_iota(jnp.int32, shape, 0)
-            lane = lax.broadcasted_iota(jnp.int32, shape, 1)
-            return dot_nt(b16(jnp.where(row == lane, 1.0, 0.0)), w)
+        def padded(w):
+            return jnp.concatenate([f32(w), jnp.zeros((HPAD - w.shape[0], C), F32)], 0)
 
         for t in range(2):
             g = gpv[1 + t : 2 + t]
@@ -173,7 +204,7 @@
                 a4t[t, k * C : (k + 1) * C] = b16(w)
                 a4[t, :, k * C : (k + 1) * C] = b16(w.T)
             aot[t] = b16(f32(ao[t]).T)
-            abt[t] = b16(turned(ab[t]) * g)
+            abt[t] = b16(padded(ab[t]) * g)
         g = gpv[5:6]
         for k in range(4):
             s = slice(k * C, (k + 1) * C)
@@ -181,7 +212,7 @@
             upt[s] = b16(w)
             up[:, s] = b16(w.T)
             dnt[:, s] = b16(f32(pd[s]).T)
-        sbt[...] = b16(turned(sb[...]) * gpv[0:1])
+        sbt[...] = b16(padded(sb[...]) * gpv[0:1])
 
     outs = [
         ((2, 640, C), BF), ((2, C, 640), BF), ((2, C, C), BF), ((2, C, C), BF),
@@ -198,11 +229,10 @@
         key_row = (mask[...] - 1.0) * MASKED
 
         def body(r):
-            xh, _ = norm_cols(f32(pair[r]).T)
-            rb = dot(sbt[...], b16(xh)) + key_row
-            s[pl.ds(r, HPAD, stride=rows), :] = rb
-
-        each_row(rows, body)
+            xh, _ = norm_cols(side([f32(pair[r * U + u]).T for u in range(U)]))
+            put_rows(s, r, HPAD, rows, dot(sbt[...], b16(xh)) + side([key_row] * U))
+
+        each_row(rows // U, body)
         mine[0:rows] = single[...]
         mine[rows : 2 * rows] = cot[...]
         for h in range(8):
@@ -224,6 +254,15 @@
             out[d] = x[...]
 
     return call(kernel, [((count,) + x.shape, x.dtype)], [], (x,), deps=deps)[0]
+
+
+def part_of(x, first, last, deps):
+    def kernel(x, out):
+        out[...] = x[first:last]
+
+    return call(
+        kernel, [((last - first,) + x.shape[1:], x.dtype)], [], (x,), deps=deps, raw=(0,), us=1
+    )[0]
 
 
 def norm_rows16(x):
@@ -316,18 +355,17 @@
             held[2 * k + 1 - core] = gb[k]
         g = f32(gains[...])
 
-        def body(crop):
-            rs = pl.ds(pl.multiple_of(crop * L, L), L)
-            ds = pl.ds(crop * n, n)
-            x16 = held[ds, 0:rows, :].reshape(L, width)
+        def body(step):
+            rs = pl.ds(pl.multiple_of(step * 2 * L, 2 * L), 2 * L)
+            ds = pl.ds(step * 2 * n, 2 * n)
+            x16 = held[ds, 0:rows, :].reshape(2 * L, width)
             x_all[rs, :] = x16
-            cot_all[rs, :] = held[ds, rows : 2 * rows, :].reshape(L, width)
+            cot_all[rs, :] = held[ds, rows : 2 * rows, :].reshape(2 * L, width)
             x = f32(x16)
             sn = b16(norm_rows16(x)[0] * g[0:1])
             xs[rs, 0:width] = sn
 
-            @pl.when(crop == 0)
-            def _():
+            if step == 0:
                 arrive(4)
 
             query = b16(dot(sn, proj[0]) * 0.125)
@@ -337,24 +375,30 @@
             qkv[rs, 2 * width : 3 * width] = vals
             gate = sig(dot(sn, proj[3]))
             mixed = []
-            for t in range(4):
-                s = slice(t * L, (t + 1) * L)
-                bias = [
-                    f32(
-                        held[
-                            ds,
-                            rows * (2 + h // 4) : rows * (3 + h // 4),
-                            (h % 4) * L : (h % 4 + 1) * L,
-                        ].reshape(L, L)
-                    )
-                    for h in (2 * t, 2 * t + 1)
-                ]
-                p = pair_weights(query[:, s], keys[:, s], *bias)
-                for k in range(2):
-                    at = pl.multiple_of((crop * 8 + 2 * t + k) * L, L)
-                    probs[pl.ds(at, L), :] = p[k]
-                mixed.append(dot(jnp.concatenate(p, 1), on_halves(vals[:, s])))
-            mixed = jnp.concatenate(mixed, 1)
+            for u in range(2):
+                crop = step * 2 + u
+                own = pl.ds(crop * n, n)
+                part = slice(u * L, (u + 1) * L)
+                outs = []
+                for t in range(4):
+                    s = slice(t * L, (t + 1) * L)
+                    bias = [
+                        f32(
+                            held[
+                                own,
+                                rows * (2 + h // 4) : rows * (3 + h // 4),
+                                (h % 4) * L : (h % 4 + 1) * L,
+                            ].reshape(L, L)
+                        )
+                        for h in (2 * t, 2 * t + 1)
+                    ]
+                    p = pair_weights(query[part, s], keys[part, s], *bias)
+                    for k in range(2):
+                        at = pl.multiple_of((crop * 8 + 2 * t + k) * L, L)
+                        probs[pl.ds(at, L), :] = p[k]
+                    outs.append(dot(jnp.concatenate(p, 1), on_halves(vals[part, s])))
+                mixed.append(jnp.concatenate(outs, 1))
+            mixed = jnp.concatenate(mixed, 0)
             gm[rs, 0:width] = b16(gate)
             gm[rs, width : 2 * width] = b16(mixed)
             u = b16(mixed * gate)
@@ -364,8 +408,7 @@
             x1 = b16(norm_rows16(first)[0] * g[1:2])
             xs[rs, 2 * width : 3 * width] = x1
 
-            @pl.when(crop == 0)
-            def _():
+            if step == 0:
                 arrive(5)
                 arrive(6)
 
@@ -375,7 +418,8 @@
             slope[rs, :] = b16(slp)
             second_out[rs, :] = first + dot(h16, down[...])
 
-        each_row(4, body)
+        for step in range(2):
+            body(step)
 
     return call(
         kernel,
@@ -409,8 +453,8 @@
             total = jnp.concatenate([total, jnp.zeros_like(total)], 0)
             dlr[crop * L : (crop + 1) * L] = b16(total.T)
 
-        def body(crop):
-            rs = pl.ds(pl.multiple_of(crop * L, L), L)
+        def body(step):
+            rs = pl.ds(pl.multiple_of(step * 2 * L, 2 * L), 2 * L)
             x2, sc2 = norm_rows16(second_in[rs, :])
             o_x2[rs, :] = b16(x2 * g[2:3])
             dx = dot_nt(dlr[rs, :], outer[...])
@@ -419,8 +463,7 @@
             ds2_16 = b16(ds2)
             ys[rs, 5 * width + wide :] = ds2_16
 
-            @pl.when(crop == 0)
-            def _():
+            if step == 0:
                 for k in (14, 8, 13, 9):
                     arrive(k)
 
@@ -433,8 +476,7 @@
             df16 = b16(df)
             ys[rs, 4 * width : 5 * width] = df16
 
-            @pl.when(crop == 0)
-            def _():
+            if step == 0:
                 for k in (12, 6, 5, 7):
                     arrive(k)
 
@@ -447,26 +489,30 @@
             ys[rs, 3 * width : 4 * width] = dgate
             lane = lax.broadcasted_iota(jnp.int32, (1, L), 1)
             low = jnp.where(lane < L // 2, 1.0, 0.0)
-            for t in range(4):
-                s = slice(t * L, (t + 1) * L)
-                q = qkv[rs, t * L : (t + 1) * L]
-                k = qkv[rs, width + t * L : width + (t + 1) * L]
-                v = qkv[rs, 2 * width + t * L : 2 * width + (t + 1) * L]
-                grads, weights = [], []
-                for j, (m, mf) in enumerate(zip(halves(), (low, 1.0 - low))):
-                    at = pl.multiple_of((crop * 8 + 2 * t + j) * L, L)
-                    p16 = probs[pl.ds(at, L), :]
-                    dp = dot_nt(do16[:, s] * m, v)
-                    e = f32(p16) * (dp - jnp.sum(row[:, s] * mf, -1, keepdims=True))
-                    sdrb[pl.ds(at, L), :] = e
-                    grads.append(b16(e))
-                    weights.append(p16)
-                dq = dot(jnp.concatenate(grads, 1), on_halves(k)) * 0.125
-                dk = dot_tn(jnp.concatenate(grads, 0), on_halves(q))
-                dv = dot_tn(jnp.concatenate(weights, 0), on_halves(do16[:, s]))
-                ys[rs, t * L : (t + 1) * L] = b16(dq)
-                ys[rs, width + t * L : width + (t + 1) * L] = b16(dk)
-                ys[rs, 2 * width + t * L : 2 * width + (t + 1) * L] = b16(dv)
+            for u in range(2):
+                crop = step * 2 + u
+                own = pl.ds(pl.multiple_of(crop * L, L), L)
+                part = slice(u * L, (u + 1) * L)
+                for t in range(4):
+                    s = slice(t * L, (t + 1) * L)
+                    q = qkv[own, t * L : (t + 1) * L]
+                    k = qkv[own, width + t * L : width + (t + 1) * L]
+                    v = qkv[own, 2 * width + t * L : 2 * width + (t + 1) * L]
+                    grads, weights = [], []
+                    for j, (m, mf) in enumerate(zip(halves(), (low, 1.0 - low))):
+                        at = pl.multiple_of((crop * 8 + 2 * t + j) * L, L)
+                        p16 = probs[pl.ds(at, L), :]
+                        dp = dot_nt(do16[part, s] * m, v)
+                        e = f32(p16) * (dp - jnp.sum(row[part, s] * mf, -1, keepdims=True))
+                        sdrb[pl.ds(at, L), :] = e
+                        grads.append(b16(e))
+                        weights.append(p16)
+                    dq = dot(jnp.concatenate(grads, 1), on_halves(k)) * 0.125
+                    dk = dot_tn(jnp.concatenate(grads, 0), on_halves(q))
+                    dv = dot_tn(jnp.concatenate(weights, 0), on_halves(do16[part, s]))
+                    ys[own, t * L : (t + 1) * L] = b16(dq)
+                    ys[own, width + t * L : width + (t + 1) * L] = b16(dk)
+                    ys[own, 2 * width + t * L : 2 * width + (t + 1) * L] = b16(dv)
             dx = dot_nt(ys[rs, 0:width], proj[0])
             for k in range(1, 4):
                 dx = dx + dot_nt(ys[rs, k * width : (k + 1) * width], proj[k])
@@ -474,7 +520,8 @@
             gain_grad[0:1] += jnp.sum(dx * x0, 0, keepdims=True)
             sds[rs, :] = df + norm_rows16_back(dx * g[0:1], x0, sc0)
 
-        each_row(4, body)
+        for step in range(2):
+            body(step)
         grp, row = where[2], where[3]
         d_own[...] = sds[pl.ds(pl.multiple_of(grp * L + row * rows, rows), rows), :]
         for h in range(8):
@@ -494,33 +541,38 @@
         (
             where, ea, eb, x_all, cot_all, qkv, gm, probs, slope, first_in, second_in,
             gains, proj, up, down, outer,
-        ), deps=deps, raw=(3, 4, 5, 6, 7, 8, 9, 10, 11, 12, 13, 14, 15), late=(5, 6, 7, 8, 9, 12, 13, 14), far=(0, 1, 2, 3, 4), us=22)
-
-
-def weight_grads(xs, ys, width, wide):
+        ), deps=deps, raw=(10, 15, 4, 11, 14, 8, 13, 9, 12, 6, 5, 7, 3), late=(5, 6, 7, 8, 9, 12, 13, 14), far=(0, 1, 2, 3, 4), us=22)
+
+
+def weight_grads(xs, ys, width, wide, after):
     tokens = xs.shape[0]
     blocks = wide // width
 
-    def kernel(x, y, out):
+    def kernel(x, y, after, out):
         out[...] = dot_tn(x[...], y[...]).reshape(out.shape)
 
     def run(steps, x_at, y_at, shape, block, out_at):
         return pl.pallas_call(
             kernel,
             grid=(steps,),
-            out_shape=jax.ShapeDtypeStruct(shape, F32),
+            out_shape=pltpu.HBM(shape, F32),
             in_specs=[
                 pl.BlockSpec((tokens, width), x_at),
                 pl.BlockSpec((tokens, width), y_at),
+                pl.BlockSpec(memory_space=pl.ANY),
             ],
             out_specs=pl.BlockSpec(block, out_at),
             compiler_params=pltpu.CompilerParams(vmem_limit_bytes=32 << 20),
             cost_estimate=pl.CostEstimate(
-                flops=4 * 10**9,
+                flops=2 * 10**9,
                 bytes_accessed=steps * width * width * 8,
                 transcendentals=0,
             ),
-        )(pltpu.with_memory_space_constraint(xs, pltpu.HBM), pltpu.with_memory_space_constraint(ys, pltpu.HBM))
+        )(
+            pltpu.with_memory_space_constraint(xs, pltpu.HBM),
+            pltpu.with_memory_space_constraint(ys, pltpu.HBM),
+            pltpu.with_memory_space_constraint(after, pltpu.HBM),
+        )
 
     proj = run(
         5, lambda i: (0, i // 4), lambda i: (0, i), (5, width, width), (1, width, width),
@@ -540,9 +592,9 @@
 def project_pair(z, r, rows, m5t, pmask, sa, sb):
     xh, _ = norm_cols(z)
     p = dot(m5t[0:512], b16(xh))
-    mk = pmask[pl.ds(r, 1), :]
-    sa[pl.ds(r, C, stride=rows), :] = sig(p[0:C]) * p[C : 2 * C] * mk
-    sb[pl.ds(r, C, stride=rows), :] = sig(p[2 * C : 3 * C]) * p[3 * C : 4 * C] * mk
+    mk = get_rows(pmask, r, 1, 1)
+    put_rows(sa, r, C, rows, sig(p[0:C]) * p[C : 2 * C] * mk)
+    put_rows(sb, r, C, rows, sig(p[2 * C : 3 * C]) * p[3 * C : 4 * C] * mk)
 
 
 def put_pair(n, ab, sa, sb):
@@ -555,7 +607,7 @@
 def gated_product(z, r, rows, gatet, mot, sp):
     xh, _ = norm_cols(z)
     gate = sig(dot(gatet[...], b16(xh)))
-    ph, _ = norm_cols(sp[pl.ds(r, C, stride=rows), :])
+    ph, _ = norm_cols(get_rows(sp, r, C, rows))
     return z + dot(mot[...], b16(ph)) * gate
 
 
@@ -585,13 +637,16 @@
         edge = jnp.zeros((opm, C), BF)
 
         def body(r):
-            mine = b16(inner[pl.ds(r, opm, stride=rows), :])
-            mine = jnp.concatenate([edge, mine, edge, edge], 0)
-            z = (f32(pair[r]) + dot(lr16, mine)).T
+            parts = []
+            for u in range(U):
+                mine = b16(inner[pl.ds(r * U + u, opm, stride=rows), :])
+                mine = jnp.concatenate([edge, mine, edge, edge], 0)
+                parts.append((f32(pair[r * U + u]) + dot(lr16, mine)).T)
+            z = side(parts)
             z1[:, cols(r)] = z
             project_pair(z, r, rows, m5t, pmask, sa, sb)
 
-        each_row(rows, body)
+        each_row(rows // U, body)
         put_pair(n, ab, sa, sb)
 
     part = C * rows // n
@@ -605,7 +660,7 @@
         (where, lr_all, pair, outer_w, m5ts), deps=deps, raw=(2, 3, 4), far=(0, 2, 3, 4, 5, 6), us=5)
 
 
-def middle(n, rows, z1, prod, mots, pmask, m5ts):
+def middle(n, rows, z1, prod, mots, pmask, m5ts, deps=()):
     def kernel(z1, prod, mots, pmask, m5ts, z2, ab, sa, sb, sp):
         gatet, mot, m5t = m5ts.at[0, 512:640], mots.at[0], m5ts.at[1]
         sp[...] = f32(prod[...])
@@ -615,7 +670,7 @@
             z2[:, cols(r)] = z
             project_pair(z, r, rows, m5t, pmask, sa, sb)
 
-        each_row(rows, body)
+        each_row(rows // U, body)
         put_pair(n, ab, sa, sb)
 
     part = C * rows // n
@@ -623,7 +678,7 @@
         kernel,
         [((C, rows * L), F32), ((n, 2 * part, L), BF)],
         [((C * rows, L), F32)] * 3,
-        (z1, prod, mots, pmask, m5ts), raw=(0, 1, 2, 3, 4), far=(0,), us=4)
+        (z1, prod, mots, pmask, m5ts), deps=deps, raw=(0, 1, 2, 3, 4), far=(0,), us=4)
 
 
 def start_front(n, rows, z2, prod, m5ts, mots, abts, deps=()):
@@ -635,9 +690,9 @@
             z = gated_product(z2[:, cols(r)], r, rows, gatet, mot, sp)
             z3[:, cols(r)] = z
             xh, _ = norm_cols(z)
-            st[pl.ds(r, HPAD, stride=rows), :] = dot(abt[...], b16(xh))
-
-        each_row(rows, body)
+            put_rows(st, r, HPAD, rows, dot(abt[...], b16(xh)))
+
+        each_row(rows // U, body)
         for d in range(n):
             tb[d] = b16(st[0 : TH * rows])
 
@@ -690,42 +745,50 @@
 
 def attend(x16, a4t, bias):
     p4 = dot(a4t[...], x16)
-    q, k, v = p4[0:C], p4[C : 2 * C], p4[2 * C : 3 * C]
     gate = sig(p4[3 * C : 4 * C])
-    logits = dot(by_head(k), b16(q)) + bias[...]
-    raised, outs = [], []
-    v16 = b16(v)
-    for h in range(TH):
-        s = logits[h * L : (h + 1) * L]
-        e = jnp.exp(s - jnp.max(s, 0, keepdims=True))
-        inv = 1.0 / jnp.sum(e, 0, keepdims=True)
-        raised.append((e, inv))
-        outs.append(dot(v16[h * HD : (h + 1) * HD], b16(e)) * inv)
-    mixed = jnp.concatenate(outs, 0)
-    return (q, k, v, gate, raised, mixed)
+    each, mixed = [], []
+    for u in range(U):
+        q, k, v = (lanes(p4[m * C : (m + 1) * C], u) for m in range(3))
+        logits = dot(by_head(k), b16(q)) + bias[...]
+        raised, outs = [], []
+        v16 = b16(v)
+        for h in range(TH):
+            s = logits[h * L : (h + 1) * L]
+            e = jnp.exp(s - jnp.max(s, 0, keepdims=True))
+            inv = 1.0 / jnp.sum(e, 0, keepdims=True)
+            raised.append((e, inv))
+            outs.append(dot(v16[h * HD : (h + 1) * HD], b16(e)) * inv)
+        each.append((q, k, v, raised))
+        mixed.append(jnp.concatenate(outs, 0))
+    return each, gate, side(mixed)
 
 
 def attend_back(state, dy16, ao, dbias):
-    q, k, v, gate, raised, mixed = state
+    each, gate, mixed = state
     du = dot(ao[...], dy16)
     do = du * gate
     dgate = du * mixed * gate * (1.0 - gate)
-    do16, q16, k16 = b16(do), b16(q), b16(k)
-    dp = dot(by_head(v), do16)
-    row = do * mixed
-    dq, dk, dv = [], [], []
-    for h in range(TH):
-        s = slice(h * HD, (h + 1) * HD)
-        w = slice(h * L, (h + 1) * L)
-        e, inv = raised[h]
-        p = e * inv
-        ds = p * (dp[w] - jnp.sum(row[s], 0, keepdims=True))
-        dbias[w, :] += ds
-        ds16, p16 = b16(ds), b16(p)
-        dv.append(dot_nt(do16[s], p16))
-        dq.append(dot(k16[s], ds16))
-        dk.append(dot_nt(q16[s], ds16))
-    return jnp.concatenate([b16(x) for x in dq + dk + dv] + [b16(dgate)], 0)
+    both = do * mixed
+    parts = []
+    for u in range(U):
+        q, k, v, raised = each[u]
+        do16, q16, k16 = b16(lanes(do, u)), b16(q), b16(k)
+        dp = dot(by_head(v), do16)
+        row = lanes(both, u)
+        dq, dk, dv = [], [], []
+        for h in range(TH):
+            s = slice(h * HD, (h + 1) * HD)
+            w = slice(h * L, (h + 1) * L)
+            e, inv = raised[h]
+            p = e * inv
+            ds = p * (dp[w] - jnp.sum(row[s], 0, keepdims=True))
+            dbias[w, :] += ds
+            ds16, p16 = b16(ds), b16(p)
+            dv.append(dot_nt(do16[s], p16))
+            dq.append(dot(k16[s], ds16))
+            dk.append(dot_nt(q16[s], ds16))
+        parts.append(jnp.concatenate([b16(x) for x in dq + dk + dv], 0))
+    return jnp.concatenate([side(parts), b16(dgate)], 0)
 
 
 def start_attention(n, rows, z3, tb_all, key_row, a4ts, aots, abts, deps=()):
@@ -738,14 +801,14 @@
         def body(r):
             z = z3[:, cols(r)]
             xh, _ = norm_cols(z)
-            q, k, v, gate, raised, mixed = attend(b16(xh), a4t, bias)
+            _, gate, mixed = attend(b16(xh), a4t, bias)
             z = z + dot(aot[...], b16(mixed * gate))
             z4[:, cols(r)] = z
-            st[pl.ds(r, L, stride=rows), :] = z.T
+            put_turned(st, r, rows, z)
             xe, _ = norm_cols(z)
-            se[pl.ds(r, HPAD, stride=rows), :] = dot(abt[...], b16(xe))
-
-        each_row(rows, body)
+            put_rows(se, r, HPAD, rows, dot(abt[...], b16(xe)))
+
+        each_row(rows // U, body)
         part = L * rows // n
         for d in range(n):
             send[d, 0:part] = b16(st[d * part : (d + 1) * part])
@@ -776,26 +839,26 @@
 
         def body(r):
             w = cols(r)
-            z4 = f32(recv[:, pl.ds(pl.multiple_of(r * rows, rows), rows), :].reshape(L, C)).T
+            z4 = get_turned(recv, r, rows)
             x4, scale4 = norm_cols(z4)
             x16 = b16(x4)
             state = attend(x16, a4t, bias)
-            gated = b16(state[5] * state[3])
+            gated = b16(state[2] * state[1])
             z5 = z4 + dot(aot[...], gated)
             x5, scale5 = norm_cols(z5)
             x516 = b16(x5)
             hid, slope = gelu_parts(dot(upt[...], x516))
             h16 = b16(hid)
             z6 = z5 + dot(dnt[...], h16)
-            sout[pl.ds(r, L, stride=rows), :] = z6.T
-            dz6 = f32(cot[r]).T
+            put_turned(sout, r, rows, z6)
+            dz6 = side([f32(cot[r * U + u]).T for u in range(U)])
             c16 = b16(dz6)
             dh16 = b16(dot(dn[...], c16) * slope)
             dz5 = dz6 + norm_cols_back(dot(up[...], dh16), x5, scale5)
             dy16 = b16(dz5)
             d4 = attend_back(state, dy16, ao, dbias)
             dz4 = dz5 + norm_cols_back(dot(a4[...], d4), x4, scale4)
-            sdz[pl.ds(r, L, stride=rows), :] = dz4.T
+            put_turned(sdz, r, rows, dz4)
             o_h[:, w] = h16
             o_dh[:, w] = dh16
             o_x5[:, w] = x516
@@ -805,7 +868,7 @@
             o_u[:, w] = gated
             o_dy[:, w] = dy16
 
-        each_row(rows, body)
+        each_row(rows // U, body)
         for d in range(n):
             pout[d] = b16(sout[d * part : (d + 1) * part])
             send[d, 0:part] = b16(sdz[d * part : (d + 1) * part])
@@ -858,8 +921,8 @@
         def body(r):
             w = cols(r)
             x4, scale4 = norm_cols(z4[:, w])
-            eb16 = b16(seb[pl.ds(r, HPAD, stride=rows), :])
-            dz4 = f32(recv[:, pl.ds(pl.multiple_of(r * rows, rows), rows), :].reshape(L, C)).T
+            eb16 = b16(get_rows(seb, r, HPAD, rows))
+            dz4 = get_turned(recv, r, rows)
             dz4 = dz4 + norm_cols_back(dot_tn(abt[...], eb16), x4, scale4)
             dz4_out[:, w] = dz4
             x3, _ = norm_cols(z3[:, w])
@@ -870,12 +933,12 @@
             dxs[:, w] = dot(a4[...], d4)
             o_x3[:, w] = x16
             o_d4[:, w] = d4
-            o_u[:, w] = b16(state[5] * state[3])
+            o_u[:, w] = b16(state[2] * state[1])
             o_dy[:, w] = dy16
             o_x4[:, w] = b16(x4)
             o_eb[:, w] = eb16
 
-        each_row(rows, body)
+        each_row(rows // U, body)
         for h in range(TH):
             turned = b16(dbias[h * L : (h + 1) * L, :].T)
             for d in range(n):
@@ -906,12 +969,12 @@
     w = cols(r)
     xh, _ = norm_cols(z)
     gate = sig(dot(gatet[...], b16(xh)))
-    ph, scale = norm_cols(sp[pl.ds(r, C, stride=rows), :])
+    ph, scale = norm_cols(get_rows(sp, r, C, rows))
     ph16 = b16(ph)
     out = dot(mot[...], ph16)
     dgp_out[:, w] = b16(dz * out * gate * (1.0 - gate))
     do16 = b16(dz * gate)
-    sdp[pl.ds(r, C, stride=rows), :] = norm_cols_back(dot(mof[...], do16), ph, scale)
+    put_rows(sdp, r, C, rows, norm_cols_back(dot(mof[...], do16), ph, scale))
     o_ph[:, w] = ph16
     o_do[:, w] = do16
 
@@ -933,7 +996,7 @@
         def body(r):
             w = cols(r)
             x3, scale3 = norm_cols(z3[:, w])
-            tb16 = b16(stb[pl.ds(r, HPAD, stride=rows), :])
+            tb16 = b16(get_rows(stb, r, HPAD, rows))
             dx = dxs[:, w] + dot_tn(abt[...], tb16)
             dz = dz4[:, w] + norm_cols_back(dx, x3, scale3)
             dz3[:, w] = dz
@@ -941,7 +1004,7 @@
             o_tb[:, w] = tb16
             product_back(z2[:, w], dz, r, rows, sp, gatet, mot, mof, sdp, dgp, o_ph, o_do)
 
-        each_row(rows, body)
+        each_row(rows // U, body)
         dp[...] = b16(sdp[...])
         m_ab[...] = dot_nt(o_tb[...], o_x3[...])
         m_mo[...] = dot_nt(o_ph[...], o_do[...])
@@ -965,9 +1028,9 @@
     xh, scale = norm_cols(z)
     x16 = b16(xh)
     p = dot(m5t[0:512], x16)
-    mk = pmask[pl.ds(r, 1), :]
-    da = sa[pl.ds(r, C, stride=rows), :] * mk
-    db = sb[pl.ds(r, C, stride=rows), :] * mk
+    mk = get_rows(pmask, r, 1, 1)
+    da = get_rows(sa, r, C, rows) * mk
+    db = get_rows(sb, r, C, rows) * mk
     ga, gb = sig(p[0:C]), sig(p[2 * C : 3 * C])
     va, vb = p[C : 2 * C], p[3 * C : 4 * C]
     d5 = jnp.concatenate(
@@ -1011,7 +1074,7 @@
             dz2[:, w] = dz
             product_back(z1[:, w], dz, r, rows, sp, gatet, mot, mof, sdp, dgp_out, o_ph, o_do)
 
-        each_row(rows, body)
+        each_row(rows // U, body)
         dp[...] = b16(sdp[...])
         for k in range(5):
             s = slice(k * C, (k + 1) * C)
@@ -1049,13 +1112,15 @@
             w = cols(r)
             dz = projections_back(
                 n, rows, z1[:, w], dz2[:, w], dgp, r, pmask, m5t, m5, sa, sb, o_x, o_d5
-            ).T
-            dz16 = b16(dz)
-            dz1[r] = dz16
-            sdi[pl.ds(r, opm, stride=rows), :] = dot(right_t, dz16)
-            sdr[...] += dot_nt(b16(inner[pl.ds(r, opm, stride=rows), :]), dz16)
-
-        each_row(rows, body)
+            )
+            for u in range(U):
+                dz16 = b16(lanes(dz, u).T)
+                dz1[r * U + u] = dz16
+                at = pl.ds(r * U + u, opm, stride=rows)
+                sdi[at, :] = dot(right_t, dz16)
+                sdr[...] += dot_nt(b16(inner[at, :]), dz16)
+
+        each_row(rows // U, body)
         left = left_own[:, 0:opm]
         dleft = jnp.zeros((opm, rows), F32)
         for b in range(opm):
@@ -1085,19 +1150,20 @@
         (where, z1, dz2, dgp, dab, pmask, m5ts, m5s, inner, lrt, left_own, outer_w), deps=deps, raw=(1, 2, 3, 5, 6, 7, 8, 9, 10, 11), far=(2, 3), us=11)
 
 
-def last_back(rows, pair, drb, dz1, sbt, deps=()):
-    def kernel(pair, drb, dz1, sbt, grad, m_sb, o_x, o_d):
+def last_back(rows, pair, drb, sbt, deps=()):
+    def kernel(pair, drb, sbt, grad, m_sb, o_x, o_d):
         def body(r):
             w = cols(r)
-            xh, scale = norm_cols(f32(pair[r]).T)
-            d = drb[pl.ds(r, 8, stride=rows), :]
+            xh, scale = norm_cols(side([f32(pair[r * U + u]).T for u in range(U)]))
+            d = get_rows(drb, r, 8, rows)
             d16 = b16(jnp.concatenate([d, jnp.zeros_like(d)], 0))
             back = norm_cols_back(dot_tn(sbt[...], d16), xh, scale)
-            grad[r] = f32(dz1[r]) + back.T
+            for u in range(U):
+                grad[r * U + u] = lanes(back, u).T
             o_x[:, w] = b16(xh)
             o_d[:, w] = d16
 
-        each_row(rows, body)
+        each_row(rows // U, body)
         m_sb[...] = dot_nt(o_d[...], o_x[...])
 
     wide = rows * L
@@ -1105,7 +1171,7 @@
         kernel,
         [((rows, L, C), F32), ((HPAD, C), F32)],
         [((C, wide), BF), ((HPAD, wide), BF)],
-        (pair, drb, dz1, sbt), deps=deps, raw=(0, 1, 2, 3), us=3)
+        (pair, drb, sbt), deps=deps, raw=(0, 1, 2), us=3)
 
 
 def collect(where, parts, half, deps):
@@ -1127,28 +1193,37 @@
         [((2 * half, C), F32)],
         (where, *parts),
         deps=deps,
+        raw=tuple(range(1, len(parts) + 1)),
         us=3,
     )
 
 
-def sum_copies(x, count, deps):
-    def kernel(x, out):
+def sum_copies(x, extra, count):
+    rows, more = x.shape[1], extra.shape[0]
+
+    def kernel(x, extra, out):
         total = b16(jnp.sum(f32(x[...]), 0))
         for d in range(count):
-            out[d] = total
-
-    return call(kernel, [((count,) + x.shape[1:], BF)], [], (x,), deps=deps, us=2)[0]
-
-
-def finish(where, near, far, m_sb, gp, gm, mp, mg, mo, ap, ab, pu, sb, places, half, opm, n_all, deps):
+            out[d, 0:rows] = total
+            out[d, rows : rows + more] = b16(extra[...])
+
+    return call(kernel, [((count, rows + more, C), BF)], [], (x, extra), us=2)[0]
+
+
+def finish(where, near, far, gp, gm, mp, mg, mo, ap, ab, pu, sb, places, half, opm, deps):
     def kernel(
-        where, near, far, m_sb, gp, gm, mp, mg, mo, ap, ab, pu, sb,
+        where, near, far, gp, gm, mp, mg, mo, ap, ab, pu, sb,
         g_pg, g_mg, g_sb, g_oo, g_mp, g_mgt, g_mo, g_ap, g_ab, g_ao, g_pu, g_pd,
         rows,
     ):
         core = where[3] % 2
-        rows[pl.ds(pl.multiple_of(core * half, half), half), :] = f32(near[...])
-        rows[pl.ds(pl.multiple_of((1 - core) * half, half), half), :] = f32(far[...])
+        chips = near.shape[0]
+        size = half // chips
+        for k in range(chips):
+            at = pl.multiple_of(core * half + k * size, 8)
+            rows[pl.ds(at, size), :] = f32(near[k, 0:size])
+            at = pl.multiple_of((1 - core) * half + k * size, 8)
+            rows[pl.ds(at, size), :] = f32(far[k, 0:size])
 
         def take(name, count, skip=0):
             at = places[name] + skip
@@ -1162,18 +1237,14 @@
         def over_lanes(x):
             return jnp.sum(x.T, 0, keepdims=True)
 
-        def turned(w):
-            shape = (HPAD, w.shape[1])
-            row = lax.broadcasted_iota(jnp.int32, shape, 0)
-            lane = lax.broadcasted_iota(jnp.int32, shape, 1)
-            return dot_nt(b16(jnp.where(row == lane, 1.0, 0.0)), w)
-
-        total = m_sb[0]
-        for d in range(1, n_all):
-            total = total + m_sb[d]
-        g_pg[0:1] = jnp.sum(turned(sb[...]) * total, 0, keepdims=True)
-        wide = jnp.concatenate([total * gpv[0:1], jnp.zeros((C - HPAD, C), F32)], 0)
-        g_sb[...] = wide.T[:, 0:8]
+        def padded(w):
+            return jnp.concatenate([f32(w), jnp.zeros((HPAD - w.shape[0], C), F32)], 0)
+
+        total = jnp.zeros((8, C), F32)
+        for k in range(chips):
+            total = total + (f32(near[k, size : size + 8]) + f32(far[k, size : size + 8]))
+        g_pg[0:1] = jnp.sum(f32(sb[...]) * total, 0, keepdims=True)
+        g_sb[...] = total * gpv[0:1]
         for t in range(2):
             g = column(gpv[1 + t : 2 + t])
             both = jnp.zeros((C, C), F32)
@@ -1197,11 +1268,8 @@
                 both = both + m * f32(ap[t, k])
                 g_ap[t, k] = m * g
             m = take("ab%d" % t, HPAD)
-            g_pg[3 + t : 4 + t] = over_lanes(both) + jnp.sum(turned(ab[t]) * m, 0, keepdims=True)
-            wide = jnp.concatenate(
-                [m * gpv[3 + t : 4 + t], jnp.zeros((C - HPAD, C), F32)], 0
-            )
-            g_ab[t] = wide.T[:, 0:TH]
+            g_pg[3 + t : 4 + t] = over_lanes(both) + jnp.sum(padded(ab[t]) * m, 0, keepdims=True)
+            g_ab[t] = (m * gpv[3 + t : 4 + t])[0:TH]
             g_ao[t] = take("ao%d" % t, C)
         g = column(gpv[5:6])
         both = jnp.zeros((C, C), F32)
@@ -1216,16 +1284,16 @@
             g_oo[:, b, :] = take("oo", opm, b * opm)
 
     outs = [
-        (6, C), (2, C), (C, 8), (opm, opm, C), (2, 4, C, C), (2, C, C), (2, C, C), (2, 4, C, C),
-        (2, C, TH), (2, C, C), (C, 512), (512, C),
+        (6, C), (2, C), (8, C), (opm, opm, C), (2, 4, C, C), (2, C, C), (2, C, C), (2, 4, C, C),
+        (2, TH, C), (2, C, C), (C, 512), (512, C),
     ]
     return call(
         kernel,
         [(s, F32) for s in outs],
         [((2 * half, C), F32)],
-        (where, near, far, m_sb, gp, gm, mp, mg, mo, ap, ab, pu, sb),
-
-        raw=(4, 5, 6, 7, 8, 9, 10, 11, 12), deps=deps, us=4,
+        (where, near, far, gp, gm, mp, mg, mo, ap, ab, pu, sb),
+
+        raw=(3, 4, 5, 6, 7, 8, 9, 10, 11), deps=deps, far=tuple(range(12)), us=4,
     )
 
 
@@ -1755,10 +1823,10 @@
             jnp.broadcast_to(single, (n,) + single.shape), "rows", 0, 0, tiled=True
         )
         pair = swap(pair_rep[0])
-        cot = swap(pair_cot[0])
+        att_b, single_b = jnp.swapaxes(att_bias, 1, 2), single_bias.T
         m5t, m5, mot, mof, a4t, a4, aot, abt, upt, up, dnt, sbt = prep_weights(
-            pair_gains, mult_gains, mult_proj, mult_gate, mult_out, att_proj, att_bias, att_out,
-            pair_up, pair_down, single_bias,
+            pair_gains, mult_gains, mult_proj, mult_gate, mult_out, att_proj, att_b, att_out,
+            pair_up, pair_down, single_b,
         )
         opm = opm_proj.shape[2]
         outer = jnp.swapaxes(opm_proj, 0, 1).reshape(width, 2 * opm)
@@ -1773,7 +1841,7 @@
         lr = to_all(lr)
 
         z1, ab1, pmask, key_row, inner, lrt, left_own = front(
-            n, rows, where, lr, pair, outer_w, m5t, deps=(cot,)
+            n, rows, where, lr, pair, outer_w, m5t
         )
         ab1 = exchange(ab1)
         p1 = exchange(channel_product(n, rows, True, ab1)).reshape(C * rows, L)
@@ -1781,10 +1849,15 @@
         ab2 = exchange(ab2)
         p2 = exchange(channel_product(n, rows, False, ab2)).reshape(C * rows, L)
         z3, tb = start_front(n, rows, z2, p2, m5t, mot, abt)
+        cot = swap(copies_of(pair_cot[0], 1, (p2,))[0])
+        tb, cot = lax.optimization_barrier((tb, cot))
         tb_all = exchange(tb)
-        cot = exchange(jnp.transpose(cot.reshape(rows, n, rows, C), (1, 2, 0, 3)))
+        cot = jnp.transpose(cot.reshape(rows, n, rows, C), (1, 2, 0, 3))
+        tb_all, cot = lax.optimization_barrier((tb_all, cot))
+        cot = exchange(cot)
+        z4, turn = start_attention(n, rows, z3, tb_all, key_row, a4t, aot, abt)
+        turn, cot = lax.optimization_barrier((turn, cot))
         cot = jnp.swapaxes(cot, 0, 1).reshape(rows, L, C)
-        z4, turn = start_attention(n, rows, z3, tb_all, key_row, a4t, aot, abt, deps=(cot,))
         turn = exchange(turn)
         copies = to_chips(copies_of(mine, chips, (turn,)))
         others = other_core(copies)
@@ -1822,7 +1895,9 @@
         ends = to_chips(ends)
         others_ends = other_core(ends)
         dz1 = swap(copies_of(dz1, 1, (others_ends,))[0])
-        names = "up dn a41 ao1 a40 ao0 m51 mo1 mo0 m50 oo ab1 ab0".split()
+        names = [
+            "up", "dn", "a41", "ao1", "a40", "ao0", "m51", "mo1", "mo0", "m50", "oo", "ab1", "ab0",
+        ]
         sums = [
             m_up, m_dn, m_a41, m_ao1, m_a40, m_ao0, m_m51, m_mo1, m_mo0, m_m50, m_oo, m_ab1, m_ab0,
         ]
@@ -1838,16 +1913,16 @@
             members, rows, where, ends, others_ends, kept, single_gains, single_proj,
             single_up, single_down, outer,
         )
-        pair_grad, m_sb = last_back(rows, pair_rep[0], drb, dz1, sbt)
-        m_sb = to_all(copies_of(m_sb, total, ()))
-        g_sp, g_su, g_sd = weight_grads(kept[2], ys, width, single_up.shape[1])
+        pair_grad, m_sb = last_back(rows, pair_rep[0], drb, sbt, deps=(dz1,))
+        near_sums = sum_copies(near, m_sb, chips)
+        g_sp, g_su, g_sd = weight_grads(kept[2], ys, width, single_up.shape[1], near_sums)
+        pair_grad = pair_grad + f32(dz1)
         g_op = jnp.swapaxes(m_op[:, : 2 * opm].reshape(width, 2, opm), 0, 1)
 
-        near = to_chips(sum_copies(near, chips, (drb,))).reshape(half, C)
+        near = copies_of(to_chips(near_sums), 1, (g_sp, g_su, g_sd))[0]
         grads = finish(
-            where, near, other_core(near), m_sb, pair_gains, mult_gains, mult_proj, mult_gate,
-            mult_out, att_proj, att_bias, pair_up, single_bias, places, half, opm, total,
-            (g_sd, g_su, g_sp),
+            where, near, other_core(near), pair_gains, mult_gains, mult_proj, mult_gate,
+            mult_out, att_proj, att_b, pair_up, single_b, places, half, opm, (),
         )
         g_pg, g_mg, g_sb, g_oo, g_mp, g_mgt, g_mo, g_ap, g_ab, g_ao, g_pu, g_pd = grads
         return (
@@ -1859,7 +1934,7 @@
             g_pg,
             g_mg,
             g_sp,
-            g_sb,
+            g_sb.T,
             g_su,
             g_sd,
             g_op,
@@ -1868,7 +1943,7 @@
             g_mgt,
             g_mo,
             g_ap,
-            g_ab,
+            jnp.swapaxes(g_ab, 1, 2),
             g_ao,
             g_pu,
             g_pd,

time: 525 us -> 477 us (0.909)
  Pallas kernels: 219 us -> 186 us
  waiting for transfers between devices: 70.1 us -> 52.3 us
  starting transfers between devices: 61.9 us -> 77.5 us
  local copies, waits for them, and re-layouts: 23 us -> 9.8 us
    pallas_call x25 -> x26, Pallas kernels: 202 us -> 168 us  [call(): pl.pallas_call(body, out_shape=[pltpu.HBM(s, d) if k in far else jax.Shap...]
    all_to_all x6, starting transfers between devices: 21.6 us -> 42 us  [exchange(): return lax.all_to_all(x, AX, 0, 0, tiled=True, axis_index_groups=groups)]
    all_to_all x2 -> x1, waiting for transfers between devices: 24.9 us -> 9.53 us  [to_all(): return lax.all_to_all(copies, AX, 0, 0, tiled=True)]
    unnamed x64 -> x42, local copies, waits for them, and re-layouts: 18.8 us -> 4.8 us
    all_to_all x2 -> x1, starting transfers between devices: 12 us -> 6.93 us  [to_all(): return lax.all_to_all(copies, AX, 0, 0, tiled=True)]
  transfers between devices with their start and end apart: 20 -> 19, of which waited for: 10 -> 10; matrix products, arithmetic and copies ran while one was open for 1% -> 1% of each run, Pallas kernels for 28% -> 28%
where the time goes in v1:
time: 477 us; the launch traced here: 467 us
  Pallas kernels  186 us (39%)
  blocking collectives  139 us (29%)
  starting transfers between devices  77.5 us (16%)
  waiting for transfers between devices  52.3 us (11%)
  local copies, waits for them, and re-layouts  9.8 us (2%)
    pallas_call x26, Pallas kernels, call(): pl.pallas_call(body, out_shape=[pltpu.HBM(s, d) if k in far else jax.Shap...  168 us
    all_to_all x8, blocking collectives, exchange(): return lax.all_to_all(x, AX, 0, 0, tiled=True, axis_index_groups=groups)  124 us
    all_to_all x6, starting transfers between devices, exchange(): return lax.all_to_all(x, AX, 0, 0, tiled=True, axis_index_groups=groups)  42 us
    all_to_all x6, waiting for transfers between devices, exchange(): return lax.all_to_all(x, AX, 0, 0, tiled=True, axis_index_groups=groups)  27.2 us
    pallas_call x3, Pallas kernels, run(): pl.pallas_call(kernel, grid=(steps,), out_shape=pltpu.HBM(shape, F32), in...  17.4 us
    all_to_all x3, starting transfers between devices, to_chips(): lax.all_to_all(copies, AX, 0, 0, tiled=True, axis_index_groups=same_core)  17.3 us
    all_to_all x1, blocking collectives, to_chips(): lax.all_to_all(copies, AX, 0, 0, tiled=True, axis_index_groups=same_core)  15 us
    all_to_all x3, waiting for transfers between devices, to_chips(): lax.all_to_all(copies, AX, 0, 0, tiled=True, axis_index_groups=same_core)  12.7 us
  transfers between devices with their start and end apart: 19, of which 10 were waited for; matrix products, arithmetic and copies ran while one was open for 1% of the time, Pallas kernels for 28%

profile of v1, /device:TPU:0, one launch (start us, length us, event | category | flops | bytes accessed | tf_op | source)
XLA Modules:
  0.0 467.5 jit_solution(8881456994371982828)
XLA Ops:
  0.7 1.4 broadcast_in_dim.15
  2.0 6.3 %all-to-all-start = ((bf16[8,16,512]{2,1,0:T(8,128)(2,1)}), bf16[8,16,512]{2,1,0:T(8,128)(2,1)S(1)}, u32[]{:S(2)}, u32[]{:S(2)}) async-start(bf16[8,16,512]{2,1,0:T(8,128)(2,1)} %broadcast_in_dim.15), calls=%async_computation | async-start | bytes 262144 | tf_op jit(solution)/shard_map/all_to_all | solution.py:1822
  8.4 1.7 collective-permute-start
  10.1 3.0 shard_map.373
  14.0 3.0 shard_map.374
  17.0 7.0 %shard_map.375 = (bf16[16,512]{1,0:T(8,128)(2,1)}, bf16[32,16,128]{2,1,0:T(8,128)(2,1)}) custom-call(bf16[8,16,512]{2,1,0:T(8,128)(2,1)S(1)} %all-to-all-done.refs_0_, bf16[64,512]{1,0:T(8,128)(2,1)S(1)} %get-tuple-element.113.refs_1_.refs_0_, f32[16,128]{1,0:T(8,128)S(1)} %get-tuple-element.114.refs_2_, bf16[3,512]{1,0:T(4,128)(2,1)} %refs_11_.1, ...), custom_call_target="tpu_custom_call" | custom-call | flops 6000000000 | bytes 7154688 | tf_op jit(solution)/shard_map/pallas_call | solution.py:158
  24.0 6.9 %all-to-all-start.1 = ((bf16[32,16,128]{2,1,0:T(8,128)(2,1)}), bf16[32,16,128]{2,1,0:T(8,128)(2,1)S(1)}, u32[]{:S(2)}, u32[]{:S(2)}) async-start(bf16[32,16,128]{2,1,0:T(8,128)(2,1)} %get-tuple-element.116), calls=%async_computation.1 | async-start | bytes 262144 | tf_op jit(solution)/shard_map/all_to_all | solution.py:1797
  31.7 9.5 %all-to-all-done.1.refs_1_ = bf16[32,16,128]{2,1,0:T(8,128)(2,1)S(1)} async-done(((bf16[32,16,128]{2,1,0:T(8,128)(2,1)}), bf16[32,16,128]{2,1,0:T(8,128)(2,1)S(1)}, u32[]{:S(2)}, u32[]{:S(2)}) %all-to-all-start.1) | async-done | bytes 131104 | tf_op jit(solution)/shard_map/all_to_all | solution.py:1797
  42.1 5.6 %shard_map.376 = (f32[128,2048]{1,0:T(8,128)}, bf16[8,512,128]{2,1,0:T(8,128)(2,1)S(1)}, f32[16,128]{1,0:T(8,128)}, f32[1,128]{1,0:T(1,128)}, f32[512,128]{1,0:T...) custom-call(s32[4]{0:T(128)S(1)} %pad_add_fusion.refs_5_.refs_0_, bf16[32,16,128]{2,1,0:T(8,128)(2,1)S(1)} %all-to-all-done.1.refs_1_, ...), custom_call_target="tpu_custom_call" | custom-call | flops 5000000000 | bytes 1245200 | tf_op jit(solution)/shard_map/pallas_call | solution.py:158
  47.6 18.5 %all_to_all.100.refs_0_ = bf16[8,512,128]{2,1,0:T(8,128)(2,1)} all-to-all(bf16[8,512,128]{2,1,0:T(8,128)(2,1)S(1)} %get-tuple-element.119), channel_id=1, replica_groups={{0,1,2,3,8,9,10,11},{4,5,6,7,12,13,14,15},{16,17,18,19,24,25,26,27},{20..., dimensions={0} | all-to-all | bytes 2097152 | tf_op jit(solution)/shard_map/all_to_all | solution.py:1793
  66.1 1.7 shard_map.377
  67.8 12.8 %all_to_all.101 = bf16[8,256,128]{2,1,0:T(8,128)(2,1)} all-to-all(bf16[8,256,128]{2,1,0:T(8,128)(2,1)S(1)} %shard_map.377), channel_id=1, replica_groups={{0,1,2,3,8,9,10,11},{4,5,6,7,12,13,14,15},{16,17,18,19,24,25,26,27},{20..., dimensions={0} | all-to-all | bytes 1048576 | tf_op jit(solution)/shard_map/all_to_all | solution.py:1793
  80.7 5.4 %shard_map.378 = (f32[128,2048]{1,0:T(8,128)}, bf16[8,512,128]{2,1,0:T(8,128)(2,1)S(1)}) custom-call(f32[128,2048]{1,0:T(8,128)} %get-tuple-element.118.refs_0_.refs_7_.refs_1_, bf16[2048,128]{1,0:T(8,128)(2,1)} %bitcast.56, bf16[2,128,128]{2,1,0:T(8,128)(2,1)} %get-tuple-element.120.refs_2_.refs_3_.refs_8_.refs_9_, ...), custom_call_target="tpu_custom_call" | custom-call | flops 4000000000 | bytes 1974272 | tf_op jit(solution)/shard_map/pallas_call | solution.py:158
  86.0 18.5 %all_to_all.102.refs_0_ = bf16[8,512,128]{2,1,0:T(8,128)(2,1)} all-to-all(bf16[8,512,128]{2,1,0:T(8,128)(2,1)S(1)} %get-tuple-element.123), channel_id=1, replica_groups={{0,1,2,3,8,9,10,11},{4,5,6,7,12,13,14,15},{16,17,18,19,24,25,26,27},{20..., dimensions={0} | all-to-all | bytes 2097152 | tf_op jit(solution)/shard_map/all_to_all | solution.py:1793
  104.5 1.6 shard_map.379
  106.2 12.8 %all_to_all.103 = bf16[8,256,128]{2,1,0:T(8,128)(2,1)} all-to-all(bf16[8,256,128]{2,1,0:T(8,128)(2,1)S(1)} %shard_map.379), channel_id=1, replica_groups={{0,1,2,3,8,9,10,11},{4,5,6,7,12,13,14,15},{16,17,18,19,24,25,26,27},{20..., dimensions={0} | all-to-all | bytes 1048576 | tf_op jit(solution)/shard_map/all_to_all | solution.py:1793
  119.8 6.0 %shard_map.380 = (f32[128,2048]{1,0:T(8,128)}, bf16[8,64,128]{2,1,0:T(8,128)(2,1)}) custom-call(f32[128,2048]{1,0:T(8,128)} %get-tuple-element.122.refs_0_.refs_5_, bf16[2048,128]{1,0:T(8,128)(2,1)} %bitcast.59, bf16[2,640,128]{2,1,0:T(8,128)(2,1)} %get-tuple-element.117.refs_4_.refs_2_.refs_7_.refs_5_.refs_6_, ...), custom_call_target="tpu_custom_call" | custom-call | flops 4000000000 | bytes 1974272 | tf_op jit(solution)/shard_map/pallas_call | solution.py:158
  125.8 23.0 %all-to-all-start.6 = ((bf16[8,64,128]{2,1,0:T(8,128)(2,1)}), bf16[8,64,128]{2,1,0:T(8,128)(2,1)S(1)}, u32[]{:S(2)}, u32[]{:S(2)}) async-start(bf16[8,64,128]{2,1,0:T(8,128)(2,1)} %get-tuple-element.127), calls=%async_computation.6 | async-start | bytes 262144 | tf_op jit(solution)/shard_map/all_to_all | solution.py:1793
  148.8 1.1 copy.61
  150.0 4.4 all-to-all-done.6.refs_1_.refs_3_
  154.4 3.5 all-to-all-start.7
  157.9 11.3 %shard_map.382 = (f32[128,2048]{1,0:T(8,128)}, bf16[8,320,128]{2,1,0:T(8,128)(2,1)}) custom-call(f32[128,2048]{1,0:T(8,128)} %get-tuple-element.125.refs_0_, bf16[8,64,128]{2,1,0:T(8,128)(2,1)} %copy-done.16, f32[1,128]{1,0:T(1,128)} %get-tuple-element.130.refs_2_.refs_4_, bf16[2,512,128]{2,1,0:T(8,128)(2,1)} %get-tuple-element.131.refs_3_.refs_5_, ...), custom_call_target="tpu_custom_call" | custom-call | flops 12000000000 | bytes 1516032 | tf_op jit(solution)/shard_map/pallas_call | solution.py:158
  169.2 4.1 all-to-all-start.8
  173.4 0.8 copy.56
  174.2 10.3 %all-to-all-done.8.refs_0_.refs_1_ = bf16[8,320,128]{2,1,0:T(8,128)(2,1)S(1)} async-done(((bf16[8,320,128]{2,1,0:T(8,128)(2,1)}), bf16[8,320,128]{2,1,0:T(8,128)(2,1)S(1)}, u32[]{:S(2)}, u32[]{:S(2)}) %all-to-all-start.8) | async-done | bytes 655392 | tf_op jit(solution)/shard_map/all_to_all | solution.py:1793
  184.5 0.8 copy-done
  185.3 1.0 shard_map.384
  186.4 5.2 %all-to-all-start.11 = ((bf16[16,64,512]{2,1,0:T(8,128)(2,1)}), bf16[16,64,512]{2,1,0:T(8,128)(2,1)S(1)}, u32[]{:S(2)}, u32[]{:S(2)}) async-start(bf16[16,64,512]{2,1,0:T(8,128)(2,1)} %shard_map.384), calls=%async_computation.11 | async-start | bytes 2097152 | tf_op jit(solution)/shard_map/all_to_all | solution.py:1807
  191.6 27.9 %shard_map.383 = (bf16[8,256,128]{2,1,0:T(8,128)(2,1)}, bf16[8,320,128]{2,1,0:T(8,128)(2,1)}, f32[512,128]{1,0:T(8,128)}, f32[512,128]{1,0:T(8,128)}, f32[512,128]{1,0:T(8,128)}, /*index=5*/f32[128,128]{1,0:T(8,128)}) custom-call(bf16[8,320,128]{2,1,0:T(8,128)(2,1)S(1)} %copy-done.1, bf16[16,128,128]{2,1,0:T(8,128)(2,1)} %bitcast.61, ...), custom_call_target="tpu_custom_call" | custom-call | flops 35999997952 | bytes 2359808 | tf_op jit(solution)/shard_map/pallas_call | solution.py:158
  219.5 4.2 all-to-all-start.10
  224.2 10.6 %all-to-all-done.10.refs_2_ = bf16[8,320,128]{2,1,0:T(8,128)(2,1)S(1)} async-done(((bf16[8,320,128]{2,1,0:T(8,128)(2,1)}), bf16[8,320,128]{2,1,0:T(8,128)(2,1)S(1)}, u32[]{:S(2)}, u32[]{:S(2)}) %all-to-all-start.10) | async-done | bytes 655392 | tf_op jit(solution)/shard_map/all_to_all | solution.py:1793
  234.9 3.5 all-to-all-start.9
  238.4 15.5 %shard_map.385 = (f32[128,2048]{1,0:T(8,128)}, f32[128,2048]{1,0:T(8,128)}, bf16[8,64,128]{2,1,0:T(8,128)(2,1)S(1)}, f32[512,128]{1,0:T(8,128)}, f32[128,128]{1,0:T(8,128)}, /*index=5*/f32[16,128]{1,0:T(8,128)}) custom-call(f32[128,2048]{1,0:T(8,128)} %get-tuple-element.125.refs_0_, f32[128,2048]{1,0:T(8,128)} %get-tuple-element.142.refs_1_, ...), custom_call_target="tpu_custom_call" | custom-call | flops 20000000000 | bytes 3482112 | tf_op jit(solution)/shard_map/pallas_call | solution.py:158
  253.9 9.4 %all_to_all.104.refs_3_ = bf16[8,64,128]{2,1,0:T(8,128)(2,1)S(1)} all-to-all(bf16[8,64,128]{2,1,0:T(8,128)(2,1)S(1)} %get-tuple-element.146), channel_id=1, replica_groups={{0,1,2,3,8,9,10,11},{4,5,6,7,12,13,14,15},{16,17,18,19,24,25,26,27},{20..., dimensions={0} | all-to-all | bytes 262144 | tf_op jit(solution)/shard_map/all_to_all | solution.py:1793
  263.4 7.4 %shard_map.386 = (f32[128,2048]{1,0:T(8,128)}, bf16[128,2048]{1,0:T(8,128)(2,1)}, bf16[2048,128]{1,0:T(8,128)(2,1)S(1)}, f32[16,128]{1,0:T(8,128)}, f32[128,128]{1,0:T(8,128)}) custom-call(f32[128,2048]{1,0:T(8,128)} %get-tuple-element.125.refs_0_, f32[128,2048]{1,0:T(8,128)} %get-tuple-element.144.refs_1_, f32[128,2048]{1,0:T(8,128)} %get-tuple-element.145.refs_2_, ...), custom_call_target="tpu_custom_call" | custom-call | flops 7000000000 | bytes 5316608 | tf_op jit(solution)/shard_map/pallas_call | solution.py:158
  270.8 12.2 %all_to_all.105.refs_1_ = bf16[8,256,128]{2,1,0:T(8,128)(2,1)S(1)} all-to-all(bf16[8,256,128]{2,1,0:T(8,128)(2,1)S(1)} %bitcast.46), channel_id=1, replica_groups={{0,1,2,3,8,9,10,11},{4,5,6,7,12,13,14,15},{16,17,18,19,24,25,26,27},{20..., dimensions={0} | all-to-all | bytes 1048576 | tf_op jit(solution)/shard_map/all_to_all | solution.py:1793
  283.0 2.8 shard_map.387.refs_7_
  285.8 3.7 all-to-all-start.14
  289.6 0.9 collective-permute-start.2
  290.5 18.5 %shard_map.388 = (bf16[512,512]{1,0:T(8,128)(2,1)}, bf16[512,512]{1,0:T(8,128)(2,1)}, bf16[512,3584]{1,0:T(8,128)(2,1)}, bf16[512,1536]{1,0:T(8,128)(2,1)}, bf16...) custom-call(s32[4]{0:T(128)S(1)} %pad_add_fusion.refs_5_.refs_0_, ...), custom_call_target="tpu_custom_call" | custom-call | flops 19000000512 | bytes 8915984 | tf_op jit(solution)/shard_map/pallas_call | solution.py:158
  309.0 1.9 all-to-all-done.14.refs_3_
  310.8 10.2 %shard_map.389 = (f32[128,2048]{1,0:T(8,128)}, bf16[128,2048]{1,0:T(8,128)(2,1)}, bf16[2048,128]{1,0:T(8,128)(2,1)S(1)}, f32[640,128]{1,0:T(8,128)}, f32[128,128]{1,0:T(8,128)}) custom-call(f32[128,2048]{1,0:T(8,128)} %get-tuple-element.122.refs_0_.refs_5_, f32[128,2048]{1,0:T(8,128)} %get-tuple-element.148.refs_1_, ...), custom_call_target="tpu_custom_call" | custom-call | flops 11000000512 | bytes 6037504 | tf_op jit(solution)/shard_map/pallas_call | solution.py:158
  321.1 21.3 %all_to_all.106.refs_1_ = bf16[8,256,128]{2,1,0:T(8,128)(2,1)S(1)} all-to-all(bf16[8,256,128]{2,1,0:T(8,128)(2,1)S(1)} %bitcast.45), channel_id=1, replica_groups={{0,1,2,3,8,9,10,11},{4,5,6,7,12,13,14,15},{16,17,18,19,24,25,26,27},{20..., dimensions={0} | all-to-all | bytes 1048576 | tf_op jit(solution)/shard_map/all_to_all | solution.py:1793
  342.4 1.7 shard_map.390
  344.1 18.2 %all_to_all.107.refs_4_ = bf16[8,512,128]{2,1,0:T(8,128)(2,1)S(1)} all-to-all(bf16[8,512,128]{2,1,0:T(8,128)(2,1)S(1)} %shard_map.390), channel_id=1, replica_groups={{0,1,2,3,8,9,10,11},{4,5,6,7,12,13,14,15},{16,17,18,19,24,25,26,27},{20..., dimensions={0} | all-to-all | bytes 2097152 | tf_op jit(solution)/shard_map/all_to_all | solution.py:1793
  362.3 10.4 %shard_map.391 = (bf16[16,128,128]{2,1,0:T(8,128)(2,1)S(1)}, bf16[16,64,128]{2,1,0:T(8,128)(2,1)S(1)}, f32[1024,128]{1,0:T(8,128)}, f32[640,128]{1,0:T(8,128)}) custom-call(s32[4]{0:T(128)S(1)} %pad_add_fusion.refs_5_.refs_0_, f32[128,2048]{1,0:T(8,128)} %get-tuple-element.118.refs_0_.refs_7_.refs_1_, f32[128,2048]{1,0:T(8,128)} %get-tuple-element.153.refs_2_, ...), custom_call_target="tpu_custom_call" | custom-call | flops 11000000512 | bytes 4927504 | tf_op jit(solution)/shard_map/pallas_call | solution.py:158
  372.7 15.0 %all_to_all.108.refs_1_.refs_14_ = bf16[16,64,128]{2,1,0:T(8,128)(2,1)S(1)} all-to-all(bf16[16,64,128]{2,1,0:T(8,128)(2,1)S(1)} %get-tuple-element.159), channel_id=1, replica_groups={{0,2,4,6,8,10,12,14,16,18,20,22,24,26,28,30},{1,3,5,7,9,11,13,15,17,19,..., dimensions={0} | all-to-all | bytes 524288 | tf_op jit(solution)/shard_map/all_to_all | solution.py:1807
  387.8 1.5 collective-permute-done.4.refs_2_.refs_1_.refs_15_
  390.0 2.6 shard_map.395
  392.9 0.8 collective-permute-start.5
  393.7 1.1 collective-permute-done.6
  394.8 1.0 add_convert_fusion
  395.8 4.5 all-to-all-start.18
  400.3 17.0 %shard_map.392 = (bf16[512,5120]{1,0:T(8,128)(2,1)}, f32[3,512]{1,0:T(4,128)}, f32[16,512]{1,0:T(8,128)}, f32[128,128]{1,0:T(8,128)}, f32[512,128]{1,0:T(8,128)}) custom-call(s32[4]{0:T(128)S(1)} %pad_add_fusion.refs_5_.refs_0_, bf16[16,64,128]{2,1,0:T(8,128)(2,1)S(1)} %copy-done.3, bf16[16,64,128]{2,1,0:T(8,128)(2,1)S(1)} %copy-done.6, ...), custom_call_target="tpu_custom_call" | custom-call | flops 22000001024 | bytes 16387088 | tf_op jit(solution)/shard_map/pallas_call | solution.py:158
  418.2 2.8 shard_map.394
  421.0 9.6 %all-to-all-done.18.refs_0_ = bf16[16,160,128]{2,1,0:T(8,128)(2,1)S(1)} async-done(((bf16[16,160,128]{2,1,0:T(8,128)(2,1)}), bf16[16,160,128]{2,1,0:T(8,128)(2,1)S(1)}, u32[]{:S(2)}, u32[]{:S(2)}) %all-to-all-start.18) | async-done | bytes 655392 | tf_op jit(solution)/shard_map/all_to_all | solution.py:1807
  430.5 1.0 shard_map.396.after
  431.5 7.6 %all-to-all-start.19 = ((bf16[16,176,128]{2,1,0:T(8,128)(2,1)}), bf16[16,176,128]{2,1,0:T(8,128)(2,1)S(1)}, u32[]{:S(2)}, u32[]{:S(2)}) async-start(bf16[16,176,128]{2,1,0:T(8,128)(2,1)} %shard_map.396.after), calls=%async_computation.19 | async-start | bytes 1441792 | tf_op jit(solution)/shard_map/all_to_all | solution.py:1807
  439.1 5.2 %shard_map.399.refs_3_ = f32[2048,512]{1,0:T(8,128)} custom-call(bf16[512,3584]{1,0:T(8,128)(2,1)} %get-tuple-element.188.x, bf16[512,5120]{1,0:T(8,128)(2,1)} %get-tuple-element.189.y, bf16[16,176,128]{2,1,0:T(8,128)(2,1)} %shard_map.396.after), custom_call_target="tpu_custom_call" | custom-call | flops 2000000000 | bytes 8388608 | tf_op jit(solution)/shard_map/pallas_call | solution.py:555
  444.3 5.2 %shard_map.398.refs_2_ = f32[512,2048]{1,0:T(8,128)} custom-call(bf16[512,3584]{1,0:T(8,128)(2,1)} %get-tuple-element.188.x, bf16[512,5120]{1,0:T(8,128)(2,1)} %get-tuple-element.189.y, bf16[16,176,128]{2,1,0:T(8,128)(2,1)} %shard_map.396.after), custom_call_target="tpu_custom_call" | custom-call | flops 2000000000 | bytes 8388608 | tf_op jit(solution)/shard_map/pallas_call | solution.py:555
  449.4 7.0 %shard_map.397.refs_1_ = f32[5,512,512]{2,1,0:T(8,128)} custom-call(bf16[512,3584]{1,0:T(8,128)(2,1)} %get-tuple-element.188.x, bf16[512,5120]{1,0:T(8,128)(2,1)} %get-tuple-element.189.y, bf16[16,176,128]{2,1,0:T(8,128)(2,1)} %shard_map.396.after), custom_call_target="tpu_custom_call" | custom-call | flops 2000000000 | bytes 10485760 | tf_op jit(solution)/shard_map/pallas_call | solution.py:555
  456.4 3.1 all-to-all-done.19.refs_0_
  460.5 1.1 add_bitcast_fusion
  461.9 4.6 shard_map.401
  (65 shorter events, 7.6 us)
Async XLA Ops:
  2.0 14.9 %all-to-all-start = ((bf16[8,16,512]{2,1,0:T(8,128)(2,1)}), bf16[8,16,512]{2,1,0:T(8,128)(2,1)S(1)}, u32[]{:S(2)}, u32[]{:S(2)}) async-start(bf16[8,16,512]{2,1,0:T(8,128)(2,1)} %broadcast_in_dim.15), calls=%async_computation | async-start | bytes 262144 | tf_op jit(solution)/shard_map/all_to_all | solution.py:1822
  8.4 32.9 %collective-permute-start = (bf16[16,128,128]{2,1,0:T(8,128)(2,1)}, bf16[16,128,128]{2,1,0:T(8,128)(2,1)S(1)}, u32[]{:S(2)}, u32[]{:S(2)}) collective-permute-start(bf16[16,128,128]{2,1,0:T(8,128)(2,1)} %bitcast.71), channel_id=1, source_target_pairs={{0,0},{1,1},{2,2},{3,3},{4,8},{5,9},{6,10},{7,11},{8,4},{9,5},{10,... | collective-permute-start | bytes 1572872 | tf_op jit(solution)/shard_map/ppermute | solution.py:1789
  10.1 3.1 copy-start.19
  10.1 3.1 copy-start.17
  17.0 13.9 %copy-start.15 = (bf16[32,32,128]{2,1,0:T(8,128)(2,1)S(1)}, bf16[32,32,128]{2,1,0:T(8,128)(2,1)}, u32[]{:S(2)}) copy-start(bf16[32,32,128]{2,1,0:T(8,128)(2,1)} %param.33) | copy-start | bytes 786436
  24.0 17.3 %all-to-all-start.1 = ((bf16[32,16,128]{2,1,0:T(8,128)(2,1)}), bf16[32,16,128]{2,1,0:T(8,128)(2,1)S(1)}, u32[]{:S(2)}, u32[]{:S(2)}) async-start(bf16[32,16,128]{2,1,0:T(8,128)(2,1)} %get-tuple-element.116), calls=%async_computation.1 | async-start | bytes 262144 | tf_op jit(solution)/shard_map/all_to_all | solution.py:1797
  41.3 0.8 copy-start.18
  104.5 14.5 %copy-start.4 = (bf16[1,16,128,128]{3,2,1,0:T(8,128)(2,1)S(1)}, bf16[1,16,128,128]{3,2,1,0:T(8,128)(2,1)}, u32[]{:S(2)}) copy-start(bf16[1,16,128,128]{3,2,1,0:T(8,128)(2,1)} %param.43) | copy-start | bytes 1572868
  119.1 6.8 %collective-permute-start.1 = (bf16[16,128,128]{2,1,0:T(8,128)(2,1)S(1)}, bf16[16,128,128]{2,1,0:T(8,128)(2,1)S(1)}, u32[]{:S(2)}, u32[]{:S(2)}) collective-permute-start(bf16[16,128,128]{2,1,0:T(8,128)(2,1)S(1)} %bitcast.51), channel_id=1, source_target_pairs={{0,0},{1,1},{2,2},{3,3},{4,8},{5,9},{6,10},{7,11},{8,4},{9,5},{10,... | collective-permute-start | bytes 1572872 | tf_op jit(solution)/shard_map/ppermute | solution.py:1789
  125.8 28.5 %all-to-all-start.6 = ((bf16[8,64,128]{2,1,0:T(8,128)(2,1)}), bf16[8,64,128]{2,1,0:T(8,128)(2,1)S(1)}, u32[]{:S(2)}, u32[]{:S(2)}) async-start(bf16[8,64,128]{2,1,0:T(8,128)(2,1)} %get-tuple-element.127), calls=%async_computation.6 | async-start | bytes 262144 | tf_op jit(solution)/shard_map/all_to_all | solution.py:1793
  154.4 3.5 copy-start.16
  154.4 14.9 %all-to-all-start.7 = ((bf16[8,16,16,128]{3,2,1,0:T(8,128)(2,1)}), bf16[8,16,16,128]{3,2,1,0:T(8,128)(2,1)S(1)}, u32[]{:S(2)}, u32[]{:S(2)}) async-start(bf16[8,16,16,128]{3,2,1,0:T(8,128)(2,1)} %bitcast.42), calls=%async_computation.7 | async-start | bytes 1048576 | tf_op jit(solution)/shard_map/all_to_all | solution.py:1793
  169.2 15.3 %all-to-all-start.8 = ((bf16[8,320,128]{2,1,0:T(8,128)(2,1)}), bf16[8,320,128]{2,1,0:T(8,128)(2,1)S(1)}, u32[]{:S(2)}, u32[]{:S(2)}) async-start(bf16[8,320,128]{2,1,0:T(8,128)(2,1)} %get-tuple-element.135), calls=%async_computation.8 | async-start | bytes 1310720 | tf_op jit(solution)/shard_map/all_to_all | solution.py:1793
  184.5 0.8 copy-start
  186.4 5.2 %copy-start.1 = (bf16[8,320,128]{2,1,0:T(8,128)(2,1)S(1)}, bf16[8,320,128]{2,1,0:T(8,128)(2,1)}, u32[]{:S(2)}) copy-start(bf16[8,320,128]{2,1,0:T(8,128)(2,1)} %copy-done) | copy-start | bytes 1966084
  186.4 33.1 %all-to-all-start.11 = ((bf16[16,64,512]{2,1,0:T(8,128)(2,1)}), bf16[16,64,512]{2,1,0:T(8,128)(2,1)S(1)}, u32[]{:S(2)}, u32[]{:S(2)}) async-start(bf16[16,64,512]{2,1,0:T(8,128)(2,1)} %shard_map.384), calls=%async_computation.11 | async-start | bytes 2097152 | tf_op jit(solution)/shard_map/all_to_all | solution.py:1807
  219.5 18.9 %copy-start.9 = (bf16[16,64,512]{2,1,0:T(8,128)(2,1)}, bf16[16,64,512]{2,1,0:T(8,128)(2,1)S(1)}, u32[]{:S(2)}) copy-start(bf16[16,64,512]{2,1,0:T(8,128)(2,1)S(1)} %all-to-all-done.11.refs_9_.refs_1_) | copy-start | bytes 3145732
  219.5 15.4 %all-to-all-start.10 = ((bf16[8,320,128]{2,1,0:T(8,128)(2,1)}), bf16[8,320,128]{2,1,0:T(8,128)(2,1)S(1)}, u32[]{:S(2)}, u32[]{:S(2)}) async-start(bf16[8,320,128]{2,1,0:T(8,128)(2,1)} %get-tuple-element.143), calls=%async_computation.10 | async-start | bytes 1310720 | tf_op jit(solution)/shard_map/all_to_all | solution.py:1793
  223.7 14.7 %collective-permute-start.3 = (bf16[16,64,512]{2,1,0:T(8,128)(2,1)S(1)}, bf16[16,64,512]{2,1,0:T(8,128)(2,1)}, u32[]{:S(2)}, u32[]{:S(2)}) collective-permute-start(bf16[16,64,512]{2,1,0:T(8,128)(2,1)S(1)} %all-to-all-done.11.refs_9_.refs_1_), channel_id=1, source_target_pairs={{0,1},{1,0},{2,3},{3,2},{4,5},{5,4},{6,7},{7,6},{8,9},{9,8},{10,11... | collective-permute-start | bytes 3145736 | tf_op jit(solution)/shard_map/ppermute | solution.py:1804
  234.9 19.0 %all-to-all-start.9 = ((bf16[8,256,128]{2,1,0:T(8,128)(2,1)}), bf16[8,256,128]{2,1,0:T(8,128)(2,1)S(1)}, u32[]{:S(2)}, u32[]{:S(2)}) async-start(bf16[8,256,128]{2,1,0:T(8,128)(2,1)} %get-tuple-element.141), calls=%async_computation.9 | async-start | bytes 1048576 | tf_op jit(solution)/shard_map/all_to_all | solution.py:1793
  253.9 9.5 %copy-start.7 = (bf16[8,256,128]{2,1,0:T(8,128)(2,1)}, bf16[8,256,128]{2,1,0:T(8,128)(2,1)S(1)}, u32[]{:S(2)}) copy-start(bf16[8,256,128]{2,1,0:T(8,128)(2,1)S(1)} %all-to-all-done.9) | copy-start | bytes 1572868
  285.8 3.7 copy-start.8
  285.8 25.0 %all-to-all-start.14 = ((bf16[8,512,128]{2,1,0:T(8,128)(2,1)}), bf16[8,512,128]{2,1,0:T(8,128)(2,1)S(1)}, u32[]{:S(2)}, u32[]{:S(2)}) async-start(bf16[8,512,128]{2,1,0:T(8,128)(2,1)} %shard_map.387.refs_7_), calls=%async_computation.14 | async-start | bytes 2097152 | tf_op jit(solution)/shard_map/all_to_all | solution.py:1793
  289.6 19.4 %collective-permute-start.2 = (bf16[16,128,128]{2,1,0:T(8,128)(2,1)S(1)}, bf16[16,128,128]{2,1,0:T(8,128)(2,1)S(1)}, u32[]{:S(2)}, u32[]{:S(2)}) collective-permute-start(bf16[16,128,128]{2,1,0:T(8,128)(2,1)S(1)} %bitcast.62), channel_id=1, source_target_pairs={{0,0},{1,1},{2,2},{3,3},{4,8},{5,9},{6,10},{7,11},{8,4},{9,5},{10,... | collective-permute-start | bytes 1572872 | tf_op jit(solution)/shard_map/ppermute | solution.py:1789
  309.0 1.9 copy-start.12
  387.8 1.5 copy-start.2
  387.8 1.5 collective-permute-start.4
  389.3 0.7 copy-start.5
  392.6 2.2 collective-permute-start.6
  392.9 7.4 %copy-start.3 = (bf16[16,64,128]{2,1,0:T(8,128)(2,1)S(1)}, bf16[16,64,128]{2,1,0:T(8,128)(2,1)}, u32[]{:S(2)}) copy-start(bf16[16,64,128]{2,1,0:T(8,128)(2,1)} %copy-done.2) | copy-start | bytes 786436
  392.9 7.4 %copy-start.6 = (bf16[16,64,128]{2,1,0:T(8,128)(2,1)S(1)}, bf16[16,64,128]{2,1,0:T(8,128)(2,1)}, u32[]{:S(2)}) copy-start(bf16[16,64,128]{2,1,0:T(8,128)(2,1)} %copy-done.5) | copy-start | bytes 786436
  392.9 24.5 %collective-permute-start.5 = (bf16[16,128,128]{2,1,0:T(8,128)(2,1)S(1)}, bf16[16,128,128]{2,1,0:T(8,128)(2,1)S(1)}, u32[]{:S(2)}, u32[]{:S(2)}) collective-permute-start(bf16[16,128,128]{2,1,0:T(8,128)(2,1)S(1)} %bitcast.50), channel_id=1, source_target_pairs={{0,0},{1,1},{2,2},{3,3},{4,8},{5,9},{6,10},{7,11},{8,4},{9,5},{10,... | collective-permute-start | bytes 1572872 | tf_op jit(solution)/shard_map/ppermute | solution.py:1789
  395.8 34.7 %all-to-all-start.18 = ((bf16[16,160,128]{2,1,0:T(8,128)(2,1)}), bf16[16,160,128]{2,1,0:T(8,128)(2,1)S(1)}, u32[]{:S(2)}, u32[]{:S(2)}) async-start(bf16[16,160,128]{2,1,0:T(8,128)(2,1)} %bitcast.30), calls=%async_computation.18 | async-start | bytes 1310720 | tf_op jit(solution)/shard_map/all_to_all | solution.py:1807
  417.4 0.8 copy-start.10
  431.5 28.1 %all-to-all-start.19 = ((bf16[16,176,128]{2,1,0:T(8,128)(2,1)}), bf16[16,176,128]{2,1,0:T(8,128)(2,1)S(1)}, u32[]{:S(2)}, u32[]{:S(2)}) async-start(bf16[16,176,128]{2,1,0:T(8,128)(2,1)} %shard_map.396.after), calls=%async_computation.19 | async-start | bytes 1441792 | tf_op jit(solution)/shard_map/all_to_all | solution.py:1807
  456.4 3.2 copy-start.14
  456.4 4.0 copy-start.11
  459.6 2.3 collective-permute-start.7
  461.6 4.9 %copy-start.13 = (bf16[16,128,128]{2,1,0:T(8,128)(2,1)S(1)}, bf16[16,128,128]{2,1,0:T(8,128)(2,1)}, u32[]{:S(2)}) copy-start(bf16[16,128,128]{2,1,0:T(8,128)(2,1)} %copy-done.12) | copy-start | bytes 1572868
